TPU v7x, 32 devices: a whole 2x2x4 slice. The times are simulated.
32 devices in a mesh: seq: 8 (over z, x), exp: 4 (over y, core).
Axes of the slice: x: 2, y: 2, z: 4, core: 2. Of those that a mesh axis runs over, the one named last changes fastest.
Arguments:
- queries: bfloat16 [2048, 2048], P('seq', 'exp'), may hold values from -112 to 112
- key_rows: bfloat16 [2048, 2048], P('seq', 'exp'), may hold values from -4 to 4
- value_rows: bfloat16 [2048, 2048], P('seq', 'exp'), may hold values from -6 to 6
- out_grad: bfloat16 [2048, 2048], P('seq', 'exp'), may hold values from -6 to 6
- expert_ids: int32 [2048, 2], P('seq'), may hold values from 0 to 7, all different within a row
- gate_values: float32 [2048, 2], P('seq'), may hold values from 0.1 to 1
- alibi_slope: float32 [16], P('exp'), may hold values from 0.00012207031 to 0.1
- expert_in: bfloat16 [8, 2048, 4096], P('seq', None, 'exp'), may hold values from -0.125 to 0.125
- expert_out: bfloat16 [8, 4096, 2048], P('seq', 'exp'), may hold values from -0.09375 to 0.09375
Outputs:
- query_grad: bfloat16 [2048, 2048], P('seq', 'exp')
- key_grad: bfloat16 [2048, 2048], P('seq', 'exp')
- value_grad: bfloat16 [2048, 2048], P('seq', 'exp')
- expert_in_grad: bfloat16 [8, 2048, 4096], P('seq', None, 'exp')
- expert_out_grad: bfloat16 [8, 4096, 2048], P('seq', 'exp')
Inputs may be any that keep to these rules, and one draw needn't show every extreme that they name: `expert_ids`: each token names two different experts.
All inputs are finite; a program needn't handle non-finite values.
Results may differ from a plain program's by a relative error of at most 0.024.
Values may be sent and summed in bfloat16 or wider, within the bound.
No kernel may reach another device: no remote copies, remote signals or barrier semaphores. Data moves between devices by JAX's collectives and lax.ppermute only.
A program may use at most 128 MiB of HBM per device.

v0:
```python
import jax
import jax.numpy as jnp
from jax import lax
from jax.sharding import PartitionSpec as P

HD = 128
WCH = 16


def shifted(block, axis, distance):
    devices = range(lax.axis_size(axis))
    route = [(i - distance, i) for i in devices if i - distance in devices]
    return lax.ppermute(block, axis, route)


def window_scores(query_heads, key_stack, slopes, seq_index, window):
    score_scale = HD ** (-0.5)
    block_len = query_heads.shape[0]
    raw_scores = (
        jnp.einsum("ihd,jhd->hij", query_heads, key_stack, preferred_element_type=jnp.float32)
        * score_scale
    )
    row_pos = lax.broadcasted_iota(jnp.int32, (block_len, key_stack.shape[0]), 0)
    col_pos = lax.broadcasted_iota(jnp.int32, (block_len, key_stack.shape[0]), 1)
    back_block = col_pos // block_len
    distance = row_pos - col_pos % block_len + back_block * block_len
    in_window = (distance >= 0) & (distance < window) & (seq_index - back_block >= 0)
    biased = raw_scores - slopes[:, None, None] * distance.astype(jnp.float32)[None]
    return jnp.where(in_window[None], biased, -jnp.inf)


def slot_routing(expert_ids, experts, capacity):
    flat_ids = jnp.concatenate([expert_ids[:, 0], expert_ids[:, 1]])
    entry_count = flat_ids.shape[0]
    expert_cols = lax.broadcasted_iota(jnp.int32, (entry_count, experts), 1)
    one_hot = (flat_ids[:, None] == expert_cols).astype(jnp.int32)
    before = jnp.cumsum(one_hot, axis=0) - one_hot
    position = jnp.sum(before * one_hot, axis=1)
    is_kept = position < capacity
    slot_index = flat_ids * capacity + position
    slot_rows = lax.broadcasted_iota(jnp.int32, (experts * capacity, entry_count), 0)
    return ((slot_rows == slot_index[None, :]) & is_kept[None, :]).astype(jnp.bfloat16)


def per_device(
    queries,
    key_rows,
    value_rows,
    out_grad,
    expert_ids,
    gate_values,
    alibi_slope,
    expert_in,
    expert_out,
):
    score_scale = HD ** (-0.5)
    block_len = queries.shape[0]
    features = queries.shape[1]
    head_count = features // HD
    seq_index = lax.axis_index("seq")
    stretches = WCH + 1
    window = WCH * block_len

    def relay_keys(step, carry):
        stack_keys, stack_values, current_keys, current_values = carry
        current_keys, current_values = shifted((current_keys, current_values), "seq", 1)
        stack_keys = lax.dynamic_update_index_in_dim(stack_keys, current_keys, step, 0)
        stack_values = lax.dynamic_update_index_in_dim(stack_values, current_values, step, 0)
        return (stack_keys, stack_values, current_keys, current_values)

    empty_stack = jnp.zeros((stretches, block_len, features), jnp.bfloat16)
    start_keys = lax.dynamic_update_index_in_dim(empty_stack, key_rows, 0, 0)
    start_values = lax.dynamic_update_index_in_dim(empty_stack, value_rows, 0, 0)
    key_stack, value_stack, unused_keys, unused_values = lax.fori_loop(
        1, stretches, relay_keys, (start_keys, start_values, key_rows, value_rows)
    )
    key_block = key_stack.reshape(stretches * block_len, head_count, HD)
    value_block = value_stack.reshape(stretches * block_len, head_count, HD)
    query_heads = queries.reshape(block_len, head_count, HD)
    scores = window_scores(query_heads, key_block, alibi_slope, seq_index, window)
    log_norm = jax.nn.logsumexp(scores, axis=2)
    probs_full = jnp.exp(scores - log_norm[:, :, None])
    weights = probs_full.astype(jnp.bfloat16)
    attn_heads = jnp.einsum(
        "hij,jhd->ihd", weights, value_block, preferred_element_type=jnp.float32
    ).astype(jnp.bfloat16)
    attn_out = attn_heads.reshape(block_len, features)
    experts = lax.axis_size("seq")
    capacity = 5 * block_len // (2 * experts)
    routing = slot_routing(expert_ids, experts, capacity)
    both_tokens = jnp.concatenate([attn_out, attn_out])
    scaled_grad = jnp.concatenate(
        [gate_values[:, 0:1] * out_grad, gate_values[:, 1:2] * out_grad]
    ).astype(jnp.bfloat16)
    send_tokens = jnp.dot(routing, both_tokens, preferred_element_type=jnp.float32).astype(
        jnp.bfloat16
    )
    send_grads = jnp.dot(routing, scaled_grad, preferred_element_type=jnp.float32).astype(
        jnp.bfloat16
    )
    recv_tokens, recv_grads = (
        lax.all_to_all(send_tokens, "seq", split_axis=0, concat_axis=0, tiled=True),
        lax.all_to_all(send_grads, "seq", split_axis=0, concat_axis=0, tiled=True),
    )
    weight_in = expert_in[0]
    weight_out = expert_out[0]
    full_tokens = lax.all_gather(recv_tokens, "exp", axis=1, tiled=True)
    pre_act = jnp.dot(full_tokens, weight_in, preferred_element_type=jnp.float32)
    full_grads = lax.all_gather(recv_grads, "exp", axis=1, tiled=True)
    logistic = jax.nn.sigmoid(pre_act)
    hidden = (pre_act * logistic).astype(jnp.bfloat16)
    through_out = lax.dot_general(
        full_grads, weight_out, (((1,), (1,)), ((), ())), preferred_element_type=jnp.float32
    )
    hidden_grad = (through_out * logistic * (1.0 + pre_act * (1.0 - logistic))).astype(jnp.bfloat16)
    out_weight_grad = lax.dot_general(
        hidden, full_grads, (((0,), (0,)), ((), ())), preferred_element_type=jnp.float32
    ).astype(jnp.bfloat16)
    in_weight_grad = lax.dot_general(
        full_tokens, hidden_grad, (((0,), (0,)), ((), ())), preferred_element_type=jnp.float32
    ).astype(jnp.bfloat16)
    back_rows = lax.psum_scatter(
        lax.dot_general(
            weight_in, hidden_grad, (((1,), (1,)), ((), ())), preferred_element_type=jnp.float32
        ).astype(jnp.bfloat16),
        "exp",
        scatter_dimension=0,
        tiled=True,
    )
    returned = lax.all_to_all(back_rows, "seq", split_axis=1, concat_axis=1, tiled=True)
    combined = lax.dot_general(
        routing, returned, (((0,), (1,)), ((), ())), preferred_element_type=jnp.float32
    )
    attn_grad = (out_grad.astype(jnp.float32) + combined[:block_len] + combined[block_len:]).astype(
        jnp.bfloat16
    )
    grad_heads = attn_grad.reshape(block_len, head_count, HD)
    row_delta = jnp.einsum(
        "ihd,ihd->hi", grad_heads, attn_heads, preferred_element_type=jnp.float32
    )
    dprob = jnp.einsum("ihd,jhd->hij", grad_heads, value_block, preferred_element_type=jnp.float32)
    dscore = (probs_full * (dprob - row_delta[:, :, None])).astype(jnp.bfloat16)
    query_grad = (
        jnp.einsum("hij,jhd->ihd", dscore, key_block, preferred_element_type=jnp.float32)
        * score_scale
    ).astype(jnp.bfloat16)
    key_parts = (
        jnp.einsum("hij,ihd->jhd", dscore, query_heads, preferred_element_type=jnp.float32)
        * score_scale
    ).reshape(stretches, block_len, features)
    value_parts = jnp.einsum(
        "hij,ihd->jhd", weights, grad_heads, preferred_element_type=jnp.float32
    ).reshape(stretches, block_len, features)

    def relay_grads(step, carry):
        key_acc, value_acc = carry
        key_acc, value_acc = (
            shifted(key_acc.astype(jnp.bfloat16), "seq", -1).astype(key_acc.dtype),
            shifted(value_acc.astype(jnp.bfloat16), "seq", -1).astype(value_acc.dtype),
        )
        index = stretches - 1 - step
        key_acc = key_acc + lax.dynamic_index_in_dim(key_parts, index, 0, keepdims=False)
        value_acc = value_acc + lax.dynamic_index_in_dim(value_parts, index, 0, keepdims=False)
        return (key_acc, value_acc)

    key_total, value_total = lax.fori_loop(
        1, stretches, relay_grads, (key_parts[stretches - 1], value_parts[stretches - 1])
    )
    key_grad = key_total.astype(jnp.bfloat16)
    value_grad = value_total.astype(jnp.bfloat16)
    return (
        query_grad.reshape(block_len, features),
        key_grad,
        value_grad,
        in_weight_grad[None],
        out_weight_grad[None],
    )


def solution(mesh):
    return jax.shard_map(
        per_device,
        mesh=mesh,
        in_specs=(
            P("seq", "exp"),
            P("seq", "exp"),
            P("seq", "exp"),
            P("seq", "exp"),
            P("seq", None),
            P("seq", None),
            P("exp"),
            P("seq", None, "exp"),
            P("seq", "exp", None),
        ),
        out_specs=(
            P("seq", "exp"),
            P("seq", "exp"),
            P("seq", "exp"),
            P("seq", None, "exp"),
            P("seq", "exp", None),
        ),
        check_vma=False,
    )
```

profile of v0, /device:TPU:0, one launch (start us, length us, event | category | flops | bytes accessed | tf_op | source)
XLA Modules:
  0.0 811.2 jit_solution(16870204203931458242)
XLA Ops:
  16.5 254.3 %while.36 = (s32[]{:T(128)}, bf16[17,256,512]{2,1,0:T(8,128)(2,1)}, bf16[17,256,512]{2,1,0:T(8,128)(2,1)}, bf16[256,512]{1,0:T(8,128)(2,1)S(1)}, bf16[256,512]{1...) while((s32[]{:T(128)}, bf16[17,256,512]{2,1,0:T(8,128)(2,1)}, bf16[17,256,512]{2,1,0:T(8,128)(2,1)}, ...), condition=%wide.region_1.2_spmd, body=%wide.region_0.1_spmd.sunk | while | flops 5 | bytes 4194519 | solution.py:74
  270.8 8.7 %reshape.291 = bf16[4352,4,128]{2,1,0:T(4,128)(2,1)} reshape(bf16[17,256,512]{2,1,0:T(8,128)(2,1)} %get-tuple-element.233) | data formatting | bytes 8912896 | tf_op jit(solution)/shard_map/reshape | solution.py:77
  279.5 8.3 %copy.40 = bf16[4352,4,128]{0,2,1:T(8,128)(2,1)} copy(bf16[4352,4,128]{2,1,0:T(4,128)(2,1)} %reshape.291) | data formatting | bytes 8912896 | tf_op jit(solution)/shard_map/reshape | solution.py:77
  297.6 9.0 %fusion.72 = (f32[4,256]{1,0:T(4,128)S(1)}, f32[4,256,4352]{1,2,0:T(8,128)}) fusion(f32[256,4352]{0,1:T(8,128)S(1)} %fusion.4, f32[4]{0:T(128)S(1)} %copy-done.5, bf16[4352,4,128]{0,2,1:T(8,128)(2,1)S(1)} %copy-done, bf16[256,4,128]{0,2,1:T(8,128)(2,1)S(1)} %bitcast.101, pred[256,4352]{0,1:T(8,128)(4,1)S(1)} %fusion.8), kind=kOutput, calls=%fused_computation.95 | convolution fusion | flops 1163131904 | bytes 28119056 | tf_op jit(solution)/shard_map/ihd,jhd->hij/dot_general | solution.py:20
  306.6 8.4 %exponential_reduce_fusion = f32[4,256]{1,0:T(4,128)S(1)} fusion(f32[4,256,4352]{1,2,0:T(8,128)} %get-tuple-element.286, f32[4,256]{1,0:T(4,128)S(1)} %is-finite_select_fusion), kind=kLoop, calls=%fused_computation.8 | loop fusion | flops 8911872 | bytes 17833984 | tf_op jit(solution)/shard_map/reduce_sum | solution.py:81
  315.0 8.9 %reshape.294 = bf16[4352,4,128]{2,1,0:T(4,128)(2,1)} reshape(bf16[17,256,512]{2,1,0:T(8,128)(2,1)} %get-tuple-element.234) | data formatting | bytes 8912896 | tf_op jit(solution)/shard_map/reshape | solution.py:78
  323.9 10.4 %fusion.35 = bf16[4,128,256]{2,1,0:T(8,128)(2,1)S(1)} fusion(f32[4,256,4352]{1,2,0:T(8,128)} %get-tuple-element.286, f32[4,256]{1,0:T(4,128)S(1)} %log_add_fusion, bf16[4352,4,128]{2,1,0:T(4,128)(2,1)} %reshape.294), kind=kOutput, calls=%fused_computation.45 | convolution fusion | flops 1149894656 | bytes 22548480 | tf_op jit(solution)/shard_map/hij,jhd->ihd/dot_general | solution.py:84
  334.9 23.5 %all_to_all.36 = bf16[8,80,512]{2,1,0:T(8,128)(2,1)} all-to-all(bf16[8,80,512]{2,1,0:T(8,128)(2,1)S(1)} %bitcast.112), channel_id=1, replica_groups=mesh['seq'=8,'exp'=4] {'seq'}, dimensions={0} | all-to-all | bytes 1310720 | tf_op jit(solution)/shard_map/all_to_all | solution.py:102
  359.3 15.2 %all_to_all.37 = bf16[8,80,512]{2,1,0:T(8,128)(2,1)} all-to-all(bf16[8,80,512]{2,1,0:T(8,128)(2,1)S(1)} %bitcast.111), channel_id=1, replica_groups=mesh['seq'=8,'exp'=4] {'seq'}, dimensions={0} | all-to-all | bytes 1310720 | tf_op jit(solution)/shard_map/all_to_all | solution.py:103
  374.5 8.3 %all-gather.5.cloned.1.call-done = bf16[640,2048]{1,0:T(8,128)(2,1)} async-done(((bf16[640,512]{1,0:T(8,128)(2,1)}), bf16[640,2048]{1,0:T(8,128)(2,1)}) %all-gather.5.cloned.1.call-update) | async-done | bytes 2621456 | tf_op jit(solution)/shard_map/all_gather | solution.py:107
  382.8 7.3 fusion.11
  390.1 19.8 %all-gather.3.cloned.1.call-done = bf16[640,2048]{1,0:T(8,128)(2,1)} async-done(((bf16[640,512]{1,0:T(8,128)(2,1)}), bf16[640,2048]{1,0:T(8,128)(2,1)}) %all-gather.3.cloned.1.call-update) | async-done | bytes 2621456 | tf_op jit(solution)/shard_map/all_gather | solution.py:109
  409.9 7.2 multiply_convert_fusion.2
  421.4 34.8 %reduce-scatter.2.cloned.1.call-done = bf16[512,640]{0,1:T(8,128)(2,1)} async-done(((bf16[2048,640]{0,1:T(8,128)(2,1)}), bf16[512,640]{0,1:T(8,128)(2,1)}) %reduce-scatter.2.cloned.1.call-update) | async-done | bytes 655376 | tf_op jit(solution)/shard_map/reduce_scatter | solution.py:122
  462.0 6.9 convert_bitcast_fusion.1
  480.0 10.0 %multiply_convert_fusion = bf16[4,256,4352]{1,2,0:T(8,128)(2,1)S(1)} fusion(f32[4,256,4352]{1,2,0:T(8,128)} %get-tuple-element.286, bf16[256,4,128]{0,2,1:T(8,128)(2,1)S(1)} %bitcast.99, f32[4,256]{1,0:T(4,128)S(1)} %get-tuple-element.277, f32[4,256]{1,0:T(4,128)S(1)} %log_add_fusion, bf16[4352,4,128]{2,1,0:T(4,128)(2,1)} %reshape.294), kind=kOutput, calls=%fused_computation.6 | convolution fusion | flops 1158676480 | bytes 31465472 | tf_op jit(solution)/shard_map/ihd,jhd->hij/dot_general | solution.py:141
  500.1 12.7 %convolution_bitcast_fusion = f32[4352,4,128]{0,2,1:T(8,128)} fusion(bf16[256,4,128]{0,2,1:T(8,128)(2,1)S(1)} %bitcast.100, f32[4,256,4352]{1,2,0:T(8,128)} %get-tuple-element.286, f32[4,256]{1,0:T(4,128)S(1)} %log_add_fusion), kind=kOutput, calls=%fused_computation.11 | convolution fusion | flops 1149763584 | bytes 27004928 | tf_op jit(solution)/shard_map/hij,ihd->jhd/dot_general | solution.py:151
  514.0 11.1 %copy.45 = f32[4352,4,128]{2,1,0:T(4,128)} copy(f32[4352,4,128]{0,2,1:T(8,128)} %multiply_bitcast_fusion) | data formatting | bytes 17825792 | tf_op jit(solution)/shard_map/mul | solution.py:148
  526.2 11.1 %copy.46 = f32[4352,4,128]{2,1,0:T(4,128)} copy(f32[4352,4,128]{0,2,1:T(8,128)} %convolution_bitcast_fusion) | data formatting | bytes 17825792 | tf_op jit(solution)/shard_map/hij,ihd->jhd/transpose | solution.py:151
  538.4 11.4 %reshape.298 = f32[17,256,512]{2,1,0:T(8,128)} reshape(f32[4352,4,128]{2,1,0:T(4,128)} %copy.45) | data formatting | bytes 17825792 | tf_op jit(solution)/shard_map/reshape | solution.py:150
  549.8 11.4 %reshape.299 = f32[17,256,512]{2,1,0:T(8,128)} reshape(f32[4352,4,128]{2,1,0:T(4,128)} %copy.46) | data formatting | bytes 17825792 | tf_op jit(solution)/shard_map/reshape | solution.py:153
  561.2 242.2 %while.37 = (s32[]{:T(128)}, bf16[256,512]{1,0:T(8,128)(2,1)S(1)}, bf16[256,512]{1,0:T(8,128)(2,1)S(1)}, f32[17,256,512]{2,1,0:T(8,128)}, f32[17,256,512]{2,1,0:...) while((s32[]{:T(128)}, bf16[256,512]{1,0:T(8,128)(2,1)S(1)}, bf16[256,512]{1,0:T(8,128)(2,1)S(1)}, ...), condition=%wide.region_9.10_spmd, body=%wide.region_8.9_spmd.sunk | while | flops 786438 | bytes 4194531 | solution.py:166
  563.8 8.5 %collective-permute-done.2 = bf16[256,512]{1,0:T(8,128)(2,1)S(1)} collective-permute-done((bf16[256,512]{1,0:T(8,128)(2,1)S(1)}, bf16[256,512]{1,0:T(8,128)(2,1)S(1)}, u32[]{:S(2)}, u32[]{:S(2)}) %collective-permute-start.2) | collective-permute-done | bytes 262176 | tf_op jit(solution)/shard_map/while/body/eval_jaxpr/ppermute | solution.py:13
  579.4 9.1 %collective-permute-done.2 = bf16[256,512]{1,0:T(8,128)(2,1)S(1)} collective-permute-done((bf16[256,512]{1,0:T(8,128)(2,1)S(1)}, bf16[256,512]{1,0:T(8,128)(2,1)S(1)}, u32[]{:S(2)}, u32[]{:S(2)}) %collective-permute-start.2) | collective-permute-done | bytes 262176 | tf_op jit(solution)/shard_map/while/body/eval_jaxpr/ppermute | solution.py:13
  595.3 8.4 %collective-permute-done.2 = bf16[256,512]{1,0:T(8,128)(2,1)S(1)} collective-permute-done((bf16[256,512]{1,0:T(8,128)(2,1)S(1)}, bf16[256,512]{1,0:T(8,128)(2,1)S(1)}, u32[]{:S(2)}, u32[]{:S(2)}) %collective-permute-start.2) | collective-permute-done | bytes 262176 | tf_op jit(solution)/shard_map/while/body/eval_jaxpr/ppermute | solution.py:13
  610.2 7.5 collective-permute-done.2
  690.8 6.7 collective-permute-done.2
  705.8 6.9 collective-permute-done.2
  722.0 7.9 collective-permute-done.2
  739.3 9.2 %collective-permute-done.2 = bf16[256,512]{1,0:T(8,128)(2,1)S(1)} collective-permute-done((bf16[256,512]{1,0:T(8,128)(2,1)S(1)}, bf16[256,512]{1,0:T(8,128)(2,1)S(1)}, u32[]{:S(2)}, u32[]{:S(2)}) %collective-permute-start.2) | collective-permute-done | bytes 262176 | tf_op jit(solution)/shard_map/while/body/eval_jaxpr/ppermute | solution.py:13
  757.8 9.5 %collective-permute-done.2 = bf16[256,512]{1,0:T(8,128)(2,1)S(1)} collective-permute-done((bf16[256,512]{1,0:T(8,128)(2,1)S(1)}, bf16[256,512]{1,0:T(8,128)(2,1)S(1)}, u32[]{:S(2)}, u32[]{:S(2)}) %collective-permute-start.2) | collective-permute-done | bytes 262176 | tf_op jit(solution)/shard_map/while/body/eval_jaxpr/ppermute | solution.py:13
  776.2 9.1 %collective-permute-done.2 = bf16[256,512]{1,0:T(8,128)(2,1)S(1)} collective-permute-done((bf16[256,512]{1,0:T(8,128)(2,1)S(1)}, bf16[256,512]{1,0:T(8,128)(2,1)S(1)}, u32[]{:S(2)}, u32[]{:S(2)}) %collective-permute-start.2) | collective-permute-done | bytes 262176 | tf_op jit(solution)/shard_map/while/body/eval_jaxpr/ppermute | solution.py:13
  (281 shorter events, 468.1 us)
Async XLA Ops:
  7.2 375.6 %all-gather.5.cloned.1.call-start = ((), (), s32[]{:S(2)}) async-start(), calls=%async_computation.5 | async-start | bytes 3276800 | tf_op jit(solution)/shard_map/all_gather | solution.py:107
  16.5 11.5 %collective-permute-start = (bf16[256,512]{1,0:T(8,128)(2,1)S(1)}, bf16[256,512]{1,0:T(8,128)(2,1)S(1)}, u32[]{:S(2)}, u32[]{:S(2)}) collective-permute-start(bf16[256,512]{1,0:T(8,128)(2,1)S(1)} %get-tuple-element.366), channel_id=1, source_target_pairs={{0,4},{4,8},{8,12},{12,16},{16,20},{20,24},{24,28},{1,5},{5,9},{9,... | collective-permute-start | bytes 786440 | tf_op jit(solution)/shard_map/while/body/eval_jaxpr/ppermute | solution.py:13
  21.3 11.1 %collective-permute-start.1 = (bf16[256,512]{1,0:T(8,128)(2,1)S(1)}, bf16[256,512]{1,0:T(8,128)(2,1)S(1)}, u32[]{:S(2)}, u32[]{:S(2)}) collective-permute-start(bf16[256,512]{1,0:T(8,128)(2,1)S(1)} %get-tuple-element.367), channel_id=1, source_target_pairs={{0,4},{4,8},{8,12},{12,16},{16,20},{20,24},{24,28},{1,5},{5,9},{9,... | collective-permute-start | bytes 786440 | tf_op jit(solution)/shard_map/while/body/eval_jaxpr/ppermute | solution.py:13
  81.5 11.0 %collective-permute-start = (bf16[256,512]{1,0:T(8,128)(2,1)S(1)}, bf16[256,512]{1,0:T(8,128)(2,1)S(1)}, u32[]{:S(2)}, u32[]{:S(2)}) collective-permute-start(bf16[256,512]{1,0:T(8,128)(2,1)S(1)} %get-tuple-element.366), channel_id=1, source_target_pairs={{0,4},{4,8},{8,12},{12,16},{16,20},{20,24},{24,28},{1,5},{5,9},{9,... | collective-permute-start | bytes 786440 | tf_op jit(solution)/shard_map/while/body/eval_jaxpr/ppermute | solution.py:13
  188.6 11.7 %collective-permute-start.1 = (bf16[256,512]{1,0:T(8,128)(2,1)S(1)}, bf16[256,512]{1,0:T(8,128)(2,1)S(1)}, u32[]{:S(2)}, u32[]{:S(2)}) collective-permute-start(bf16[256,512]{1,0:T(8,128)(2,1)S(1)} %get-tuple-element.367), channel_id=1, source_target_pairs={{0,4},{4,8},{8,12},{12,16},{16,20},{20,24},{24,28},{1,5},{5,9},{9,... | collective-permute-start | bytes 786440 | tf_op jit(solution)/shard_map/while/body/eval_jaxpr/ppermute | solution.py:13
  201.8 10.8 %collective-permute-start = (bf16[256,512]{1,0:T(8,128)(2,1)S(1)}, bf16[256,512]{1,0:T(8,128)(2,1)S(1)}, u32[]{:S(2)}, u32[]{:S(2)}) collective-permute-start(bf16[256,512]{1,0:T(8,128)(2,1)S(1)} %get-tuple-element.366), channel_id=1, source_target_pairs={{0,4},{4,8},{8,12},{12,16},{16,20},{20,24},{24,28},{1,5},{5,9},{9,... | collective-permute-start | bytes 786440 | tf_op jit(solution)/shard_map/while/body/eval_jaxpr/ppermute | solution.py:13
  206.2 12.0 %collective-permute-start.1 = (bf16[256,512]{1,0:T(8,128)(2,1)S(1)}, bf16[256,512]{1,0:T(8,128)(2,1)S(1)}, u32[]{:S(2)}, u32[]{:S(2)}) collective-permute-start(bf16[256,512]{1,0:T(8,128)(2,1)S(1)} %get-tuple-element.367), channel_id=1, source_target_pairs={{0,4},{4,8},{8,12},{12,16},{16,20},{20,24},{24,28},{1,5},{5,9},{9,... | collective-permute-start | bytes 786440 | tf_op jit(solution)/shard_map/while/body/eval_jaxpr/ppermute | solution.py:13
  219.7 11.7 %collective-permute-start = (bf16[256,512]{1,0:T(8,128)(2,1)S(1)}, bf16[256,512]{1,0:T(8,128)(2,1)S(1)}, u32[]{:S(2)}, u32[]{:S(2)}) collective-permute-start(bf16[256,512]{1,0:T(8,128)(2,1)S(1)} %get-tuple-element.366), channel_id=1, source_target_pairs={{0,4},{4,8},{8,12},{12,16},{16,20},{20,24},{24,28},{1,5},{5,9},{9,... | collective-permute-start | bytes 786440 | tf_op jit(solution)/shard_map/while/body/eval_jaxpr/ppermute | solution.py:13
  224.7 11.7 %collective-permute-start.1 = (bf16[256,512]{1,0:T(8,128)(2,1)S(1)}, bf16[256,512]{1,0:T(8,128)(2,1)S(1)}, u32[]{:S(2)}, u32[]{:S(2)}) collective-permute-start(bf16[256,512]{1,0:T(8,128)(2,1)S(1)} %get-tuple-element.367), channel_id=1, source_target_pairs={{0,4},{4,8},{8,12},{12,16},{16,20},{20,24},{24,28},{1,5},{5,9},{9,... | collective-permute-start | bytes 786440 | tf_op jit(solution)/shard_map/while/body/eval_jaxpr/ppermute | solution.py:13
  358.4 51.5 %all-gather.3.cloned.1.call-start = ((), (), s32[]{:S(2)}) async-start(), calls=%async_computation.4 | async-start | bytes 3276800 | tf_op jit(solution)/shard_map/all_gather | solution.py:109
  374.5 81.8 %reduce-scatter.2.cloned.1.call-start = ((), (), s32[]{:S(2)}) async-start(), calls=%async_computation.6 | async-start | bytes 3276800 | tf_op jit(solution)/shard_map/reduce_scatter | solution.py:122
  456.3 23.0 %all-to-all-start.2 = ((bf16[512,8,80]{0,2,1:T(8,128)(2,1)}), bf16[512,8,80]{0,2,1:T(8,128)(2,1)S(1)}, u32[]{:S(2)}, u32[]{:S(2)}) async-start(bf16[512,8,80]{0,2,1:T(8,128)(2,1)} %bitcast.109), calls=%async_computation.3 | async-start | bytes 1310720 | tf_op jit(solution)/shard_map/all_to_all | solution.py:130
  561.2 11.1 %collective-permute-start.2 = (bf16[256,512]{1,0:T(8,128)(2,1)S(1)}, bf16[256,512]{1,0:T(8,128)(2,1)S(1)}, u32[]{:S(2)}, u32[]{:S(2)}) collective-permute-start(bf16[256,512]{1,0:T(8,128)(2,1)S(1)} %get-tuple-element.389), channel_id=1, source_target_pairs={{4,0},{8,4},{12,8},{16,12},{20,16},{24,20},{28,24},{5,1},{9,5},{13... | collective-permute-start | bytes 786440 | tf_op jit(solution)/shard_map/while/body/eval_jaxpr/ppermute | solution.py:13
  562.5 13.2 %collective-permute-start.3 = (bf16[256,512]{1,0:T(8,128)(2,1)S(1)}, bf16[256,512]{1,0:T(8,128)(2,1)S(1)}, u32[]{:S(2)}, u32[]{:S(2)}) collective-permute-start(bf16[256,512]{1,0:T(8,128)(2,1)S(1)} %get-tuple-element.390), channel_id=1, source_target_pairs={{4,0},{8,4},{12,8},{16,12},{20,16},{24,20},{28,24},{5,1},{9,5},{13... | collective-permute-start | bytes 786440 | tf_op jit(solution)/shard_map/while/body/eval_jaxpr/ppermute | solution.py:13
  576.8 11.8 %collective-permute-start.2 = (bf16[256,512]{1,0:T(8,128)(2,1)S(1)}, bf16[256,512]{1,0:T(8,128)(2,1)S(1)}, u32[]{:S(2)}, u32[]{:S(2)}) collective-permute-start(bf16[256,512]{1,0:T(8,128)(2,1)S(1)} %get-tuple-element.389), channel_id=1, source_target_pairs={{4,0},{8,4},{12,8},{16,12},{20,16},{24,20},{28,24},{5,1},{9,5},{13... | collective-permute-start | bytes 786440 | tf_op jit(solution)/shard_map/while/body/eval_jaxpr/ppermute | solution.py:13
  578.1 13.5 %collective-permute-start.3 = (bf16[256,512]{1,0:T(8,128)(2,1)S(1)}, bf16[256,512]{1,0:T(8,128)(2,1)S(1)}, u32[]{:S(2)}, u32[]{:S(2)}) collective-permute-start(bf16[256,512]{1,0:T(8,128)(2,1)S(1)} %get-tuple-element.390), channel_id=1, source_target_pairs={{4,0},{8,4},{12,8},{16,12},{20,16},{24,20},{28,24},{5,1},{9,5},{13... | collective-permute-start | bytes 786440 | tf_op jit(solution)/shard_map/while/body/eval_jaxpr/ppermute | solution.py:13
  592.7 11.0 %collective-permute-start.2 = (bf16[256,512]{1,0:T(8,128)(2,1)S(1)}, bf16[256,512]{1,0:T(8,128)(2,1)S(1)}, u32[]{:S(2)}, u32[]{:S(2)}) collective-permute-start(bf16[256,512]{1,0:T(8,128)(2,1)S(1)} %get-tuple-element.389), channel_id=1, source_target_pairs={{4,0},{8,4},{12,8},{16,12},{20,16},{24,20},{28,24},{5,1},{9,5},{13... | collective-permute-start | bytes 786440 | tf_op jit(solution)/shard_map/while/body/eval_jaxpr/ppermute | solution.py:13
  594.0 12.5 %collective-permute-start.3 = (bf16[256,512]{1,0:T(8,128)(2,1)S(1)}, bf16[256,512]{1,0:T(8,128)(2,1)S(1)}, u32[]{:S(2)}, u32[]{:S(2)}) collective-permute-start(bf16[256,512]{1,0:T(8,128)(2,1)S(1)} %get-tuple-element.390), channel_id=1, source_target_pairs={{4,0},{8,4},{12,8},{16,12},{20,16},{24,20},{28,24},{5,1},{9,5},{13... | collective-permute-start | bytes 786440 | tf_op jit(solution)/shard_map/while/body/eval_jaxpr/ppermute | solution.py:13
  608.9 11.6 %collective-permute-start.3 = (bf16[256,512]{1,0:T(8,128)(2,1)S(1)}, bf16[256,512]{1,0:T(8,128)(2,1)S(1)}, u32[]{:S(2)}, u32[]{:S(2)}) collective-permute-start(bf16[256,512]{1,0:T(8,128)(2,1)S(1)} %get-tuple-element.390), channel_id=1, source_target_pairs={{4,0},{8,4},{12,8},{16,12},{20,16},{24,20},{28,24},{5,1},{9,5},{13... | collective-permute-start | bytes 786440 | tf_op jit(solution)/shard_map/while/body/eval_jaxpr/ppermute | solution.py:13
  623.0 10.7 %collective-permute-start.3 = (bf16[256,512]{1,0:T(8,128)(2,1)S(1)}, bf16[256,512]{1,0:T(8,128)(2,1)S(1)}, u32[]{:S(2)}, u32[]{:S(2)}) collective-permute-start(bf16[256,512]{1,0:T(8,128)(2,1)S(1)} %get-tuple-element.390), channel_id=1, source_target_pairs={{4,0},{8,4},{12,8},{16,12},{20,16},{24,20},{28,24},{5,1},{9,5},{13... | collective-permute-start | bytes 786440 | tf_op jit(solution)/shard_map/while/body/eval_jaxpr/ppermute | solution.py:13
  636.1 10.7 %collective-permute-start.3 = (bf16[256,512]{1,0:T(8,128)(2,1)S(1)}, bf16[256,512]{1,0:T(8,128)(2,1)S(1)}, u32[]{:S(2)}, u32[]{:S(2)}) collective-permute-start(bf16[256,512]{1,0:T(8,128)(2,1)S(1)} %get-tuple-element.390), channel_id=1, source_target_pairs={{4,0},{8,4},{12,8},{16,12},{20,16},{24,20},{28,24},{5,1},{9,5},{13... | collective-permute-start | bytes 786440 | tf_op jit(solution)/shard_map/while/body/eval_jaxpr/ppermute | solution.py:13
  649.2 10.8 %collective-permute-start.3 = (bf16[256,512]{1,0:T(8,128)(2,1)S(1)}, bf16[256,512]{1,0:T(8,128)(2,1)S(1)}, u32[]{:S(2)}, u32[]{:S(2)}) collective-permute-start(bf16[256,512]{1,0:T(8,128)(2,1)S(1)} %get-tuple-element.390), channel_id=1, source_target_pairs={{4,0},{8,4},{12,8},{16,12},{20,16},{24,20},{28,24},{5,1},{9,5},{13... | collective-permute-start | bytes 786440 | tf_op jit(solution)/shard_map/while/body/eval_jaxpr/ppermute | solution.py:13
  662.5 11.5 %collective-permute-start.3 = (bf16[256,512]{1,0:T(8,128)(2,1)S(1)}, bf16[256,512]{1,0:T(8,128)(2,1)S(1)}, u32[]{:S(2)}, u32[]{:S(2)}) collective-permute-start(bf16[256,512]{1,0:T(8,128)(2,1)S(1)} %get-tuple-element.390), channel_id=1, source_target_pairs={{4,0},{8,4},{12,8},{16,12},{20,16},{24,20},{28,24},{5,1},{9,5},{13... | collective-permute-start | bytes 786440 | tf_op jit(solution)/shard_map/while/body/eval_jaxpr/ppermute | solution.py:13
  689.5 12.6 %collective-permute-start.3 = (bf16[256,512]{1,0:T(8,128)(2,1)S(1)}, bf16[256,512]{1,0:T(8,128)(2,1)S(1)}, u32[]{:S(2)}, u32[]{:S(2)}) collective-permute-start(bf16[256,512]{1,0:T(8,128)(2,1)S(1)} %get-tuple-element.390), channel_id=1, source_target_pairs={{4,0},{8,4},{12,8},{16,12},{20,16},{24,20},{28,24},{5,1},{9,5},{13... | collective-permute-start | bytes 786440 | tf_op jit(solution)/shard_map/while/body/eval_jaxpr/ppermute | solution.py:13
  704.5 13.8 %collective-permute-start.3 = (bf16[256,512]{1,0:T(8,128)(2,1)S(1)}, bf16[256,512]{1,0:T(8,128)(2,1)S(1)}, u32[]{:S(2)}, u32[]{:S(2)}) collective-permute-start(bf16[256,512]{1,0:T(8,128)(2,1)S(1)} %get-tuple-element.390), channel_id=1, source_target_pairs={{4,0},{8,4},{12,8},{16,12},{20,16},{24,20},{28,24},{5,1},{9,5},{13... | collective-permute-start | bytes 786440 | tf_op jit(solution)/shard_map/while/body/eval_jaxpr/ppermute | solution.py:13
  720.7 14.9 %collective-permute-start.3 = (bf16[256,512]{1,0:T(8,128)(2,1)S(1)}, bf16[256,512]{1,0:T(8,128)(2,1)S(1)}, u32[]{:S(2)}, u32[]{:S(2)}) collective-permute-start(bf16[256,512]{1,0:T(8,128)(2,1)S(1)} %get-tuple-element.390), channel_id=1, source_target_pairs={{4,0},{8,4},{12,8},{16,12},{20,16},{24,20},{28,24},{5,1},{9,5},{13... | collective-permute-start | bytes 786440 | tf_op jit(solution)/shard_map/while/body/eval_jaxpr/ppermute | solution.py:13
  736.7 11.8 %collective-permute-start.2 = (bf16[256,512]{1,0:T(8,128)(2,1)S(1)}, bf16[256,512]{1,0:T(8,128)(2,1)S(1)}, u32[]{:S(2)}, u32[]{:S(2)}) collective-permute-start(bf16[256,512]{1,0:T(8,128)(2,1)S(1)} %get-tuple-element.389), channel_id=1, source_target_pairs={{4,0},{8,4},{12,8},{16,12},{20,16},{24,20},{28,24},{5,1},{9,5},{13... | collective-permute-start | bytes 786440 | tf_op jit(solution)/shard_map/while/body/eval_jaxpr/ppermute | solution.py:13
  738.0 16.1 %collective-permute-start.3 = (bf16[256,512]{1,0:T(8,128)(2,1)S(1)}, bf16[256,512]{1,0:T(8,128)(2,1)S(1)}, u32[]{:S(2)}, u32[]{:S(2)}) collective-permute-start(bf16[256,512]{1,0:T(8,128)(2,1)S(1)} %get-tuple-element.390), channel_id=1, source_target_pairs={{4,0},{8,4},{12,8},{16,12},{20,16},{24,20},{28,24},{5,1},{9,5},{13... | collective-permute-start | bytes 786440 | tf_op jit(solution)/shard_map/while/body/eval_jaxpr/ppermute | solution.py:13
  755.2 12.1 %collective-permute-start.2 = (bf16[256,512]{1,0:T(8,128)(2,1)S(1)}, bf16[256,512]{1,0:T(8,128)(2,1)S(1)}, u32[]{:S(2)}, u32[]{:S(2)}) collective-permute-start(bf16[256,512]{1,0:T(8,128)(2,1)S(1)} %get-tuple-element.389), channel_id=1, source_target_pairs={{4,0},{8,4},{12,8},{16,12},{20,16},{24,20},{28,24},{5,1},{9,5},{13... | collective-permute-start | bytes 786440 | tf_op jit(solution)/shard_map/while/body/eval_jaxpr/ppermute | solution.py:13
  756.5 15.9 %collective-permute-start.3 = (bf16[256,512]{1,0:T(8,128)(2,1)S(1)}, bf16[256,512]{1,0:T(8,128)(2,1)S(1)}, u32[]{:S(2)}, u32[]{:S(2)}) collective-permute-start(bf16[256,512]{1,0:T(8,128)(2,1)S(1)} %get-tuple-element.390), channel_id=1, source_target_pairs={{4,0},{8,4},{12,8},{16,12},{20,16},{24,20},{28,24},{5,1},{9,5},{13... | collective-permute-start | bytes 786440 | tf_op jit(solution)/shard_map/while/body/eval_jaxpr/ppermute | solution.py:13
  773.6 11.7 %collective-permute-start.2 = (bf16[256,512]{1,0:T(8,128)(2,1)S(1)}, bf16[256,512]{1,0:T(8,128)(2,1)S(1)}, u32[]{:S(2)}, u32[]{:S(2)}) collective-permute-start(bf16[256,512]{1,0:T(8,128)(2,1)S(1)} %get-tuple-element.389), channel_id=1, source_target_pairs={{4,0},{8,4},{12,8},{16,12},{20,16},{24,20},{28,24},{5,1},{9,5},{13... | collective-permute-start | bytes 786440 | tf_op jit(solution)/shard_map/while/body/eval_jaxpr/ppermute | solution.py:13
  774.9 14.6 %collective-permute-start.3 = (bf16[256,512]{1,0:T(8,128)(2,1)S(1)}, bf16[256,512]{1,0:T(8,128)(2,1)S(1)}, u32[]{:S(2)}, u32[]{:S(2)}) collective-permute-start(bf16[256,512]{1,0:T(8,128)(2,1)S(1)} %get-tuple-element.390), channel_id=1, source_target_pairs={{4,0},{8,4},{12,8},{16,12},{20,16},{24,20},{28,24},{5,1},{9,5},{13... | collective-permute-start | bytes 786440 | tf_op jit(solution)/shard_map/while/body/eval_jaxpr/ppermute | solution.py:13
  (46 other events, 441.5 us)
Sparse Core Ops, SparseCore 0:
  358.5 24.2 all-gather.4
  384.3 25.5 all-gather.2
  421.5 34.6 reduce-scatter.1
where the time goes:
time: 824 us; the launch traced here: 811 us
  waiting for transfers between devices  316 us (38%)
  starting transfers between devices  194 us (24%)
  local copies, waits for them, and re-layouts  107 us (13%)
  matrix products  84.8 us (10%)
  other arithmetic  55.1 us (7%)
  blocking collectives  38.7 us (5%)
  between operations  14.5 us (2%)
    ppermute x64, waiting for transfers between devices, shifted(): return lax.ppermute(block, axis, route)  248 us
    ppermute x64, starting transfers between devices, shifted(): return lax.ppermute(block, axis, route)  188 us
    reduce_scatter x1, waiting for transfers between devices, per_device(): lax.psum_scatter(lax.dot_general(weight_in, hidden_grad, (((1,), (1,)), (...  34.8 us
    all_to_all x1, blocking collectives, per_device(): lax.all_to_all(send_tokens, 'seq', split_axis=0, concat_axis=0, tiled=True)  23.5 us
    all_gather x1, waiting for transfers between devices, per_device(): full_grads = lax.all_gather(recv_grads, 'exp', axis=1, tiled=True)  19.8 us
    add x16, other arithmetic, relay_grads(): value_acc + lax.dynamic_index_in_dim(value_parts, index, 0, keepdims=False)  17.8 us
    add x16, other arithmetic, relay_grads(): key_acc + lax.dynamic_index_in_dim(key_parts, index, 0, keepdims=False)  17.8 us
    reshape x2, local copies, waits for them, and re-layouts, per_device(): key_block = key_stack.reshape(stretches * block_len, head_count, HD)  17 us
  transfers between devices with their start and end apart: 68, of which 66 were waited for; matrix products, arithmetic and copies ran while one was open for 5% of the time, Pallas kernels for 0%

commit v1 on v0

v1 whole, which is shorter than its diff:
```python
import functools
import math

import jax
import jax.numpy as jnp
from jax import lax
from jax.experimental import pallas as pl
from jax.experimental.pallas import tpu as pltpu
from jax.sharding import PartitionSpec as P

HD = 128
WCH = 16
LOG2E = math.log2(math.e)
BF16 = jnp.bfloat16
F32 = jnp.float32
VMEM_LIMIT = 56 * 1024 * 1024


def on(pair, dims):
    return lax.dot_general(pair[0], pair[1], ((dims[0], dims[1]), ((), ())), preferred_element_type=F32)


def rows_by_rows(a, b):
    return on((a, b), ((1,), (1,)))


def cols_by_cols(a, b):
    return on((a, b), ((0,), (0,)))


def plain(a, b):
    return on((a, b), ((1,), (0,)))


def swap(block, axis, distance):
    if distance == 0:
        return block
    devices = range(lax.axis_size(axis))
    return lax.ppermute(block, axis, [(i, i ^ distance) for i in devices])


def local_call(body, out_shapes, scalars, arrays, scratch=(), flops=0, nbytes=0):
    smem = pl.BlockSpec(memory_space=pltpu.SMEM)
    vmem = pl.BlockSpec(memory_space=pltpu.VMEM)
    return pl.pallas_call(
        body,
        out_shape=[jax.ShapeDtypeStruct(shape, dtype) for shape, dtype in out_shapes],
        in_specs=[smem] * len(scalars) + [vmem] * len(arrays),
        out_specs=[vmem] * len(out_shapes),
        scratch_shapes=list(scratch),
        compiler_params=pltpu.CompilerParams(vmem_limit_bytes=VMEM_LIMIT),
        cost_estimate=pl.CostEstimate(flops=flops, bytes_accessed=nbytes, transcendentals=0),
    )(*scalars, *arrays)


def relative_slots(id_rows, place, experts, capacity, stride):
    flat = jnp.concatenate([id_rows[k : k + 1] for k in range(id_rows.shape[0])], axis=1)
    entries = flat.shape[1]
    flat = flat.astype(F32).astype(jnp.int32)
    lanes = max(experts, 8)
    one_hot = lax.broadcasted_iota(jnp.int32, (lanes, entries), 0) == flat
    one_hot = one_hot.astype(F32)
    earlier = lax.broadcasted_iota(jnp.int32, (entries, entries), 0) < lax.broadcasted_iota(
        jnp.int32, (entries, entries), 1
    )
    before = plain(one_hot.astype(BF16), earlier.astype(F32).astype(BF16))
    position = jnp.sum(before * one_hot, axis=0, keepdims=True).astype(jnp.int32)
    return jnp.where(position < capacity, (flat ^ place) * stride + position, -1)


def pack_body(sizes, idx, q, k, v, ids, *outs):
    G, R, BL = sizes
    g = idx[1]
    for d in range(G):
        cols = pl.ds(pl.multiple_of((g ^ d) * HD, HD), HD)
        outs[d][0:BL] = k[:, cols]
        outs[d][BL : 2 * BL] = v[:, cols]
        outs[d][2 * BL : 3 * BL] = q[:, cols]
        outs[d][3 * BL : 3 * BL + 16] = ids[...]


def grads_body(sizes, idx, og, gates, ids, *outs):
    G, R, BL, cap, stride = sizes
    n = G * R
    s, g = idx[0], idx[1]
    slots = relative_slots(ids[0 : 2 * BL // 128], s, n, cap, stride)
    routing = lax.broadcasted_iota(jnp.int32, (n * stride, 2 * BL), 0) == slots
    block = og[...].astype(F32)
    scaled = jnp.concatenate([(gates[:, j : j + 1] * block).astype(BF16) for j in range(2)], axis=0)
    routed = plain(routing.astype(F32).astype(BF16), scaled).astype(BF16)
    for d in range(n):
        outs[d][...] = routed[d * stride : (d + 1) * stride]
    for d in range(G):
        outs[n + d][...] = og[:, pl.ds(pl.multiple_of((g ^ d) * HD, HD), HD)]


def forward_body(sizes, idx, slopes, *refs):
    G, R, BL, cap, stride = sizes
    n = G * R
    total = n * BL
    s, g, r = idx[0], idx[1], idx[2]
    own, refs = refs[:G], refs[G:]
    others, refs = refs[: G * (R - 1)], refs[G * (R - 1) :]
    probs, refs = refs[:G], refs[G:]
    sent, refs = refs[:n], refs[n:]
    attn, routing, keys, values, queries, ids = refs
    for d in range(G):
        i = g ^ d
        queries[pl.ds(pl.multiple_of(i * BL, BL), BL)] = own[d][2 * BL : 3 * BL]
        ids[pl.ds(i, 1)] = own[d][3 * BL : 3 * BL + 16].astype(F32)[None]
        for dr in range(R):
            piece = own[d] if dr == 0 else others[(dr - 1) * G + d]
            rows = pl.ds(pl.multiple_of((i * R + (r ^ dr)) * BL, BL), BL)
            keys[rows] = piece[0:BL]
            values[rows] = piece[BL : 2 * BL]
    slope = slopes[g]
    span = R * BL
    for i in range(G):
        slots = relative_slots(ids[i][0 : 2 * BL // 128], s, n, cap, stride)
        slot_rows = lax.broadcasted_iota(jnp.int32, (n * stride, BL), 0)
        chosen = (slot_rows == slots[:, :BL]) | (slot_rows == slots[:, BL:])
        chosen = chosen.astype(F32).astype(BF16)
        routing[i] = chosen
        N = (i + 1) * span
        scores = rows_by_rows(queries[i * BL : (i + 1) * BL], keys[0:N])
        col = lax.broadcasted_iota(jnp.int32, (1, N), 1)
        bias = (col - N).astype(F32) * (slope * LOG2E)
        scores = scores * (HD**-0.5 * LOG2E) + bias
        if total > WCH * BL:
            distance = (
                lax.broadcasted_iota(jnp.int32, (BL, N), 0) + (i * R + r) * BL - lax.broadcasted_iota(jnp.int32, (BL, N), 1)
            )
            scores = jnp.where((distance >= 0) & (distance < WCH * BL), scores, -jnp.inf)
        else:
            ahead = lax.broadcasted_iota(jnp.int32, (BL, span), 1) - lax.broadcasted_iota(jnp.int32, (BL, span), 0)
            last = jnp.where(ahead <= r * BL, scores[:, N - span :], -jnp.inf)
            scores = last if i == 0 else jnp.concatenate([scores[:, : N - span], last], axis=1)
        top = jnp.max(scores, axis=1, keepdims=True)
        grown = jnp.exp2(scores - top)
        norm = jnp.sum(grown, axis=1, keepdims=True)
        weights = (grown * (1.0 / norm)).astype(BF16)
        probs[i][...] = weights
        out = plain(weights, values[0:N]).astype(BF16)
        attn[i * BL : (i + 1) * BL] = out
        routed = plain(chosen, out).astype(BF16)
        for d in range(n):
            sent[d][i * stride : (i + 1) * stride] = routed[d * stride : (d + 1) * stride]


def backward_body(sizes, idx, *refs):
    G, R, BL, cap, stride = sizes
    n = G * R
    g, r = idx[1], idx[2]
    back, refs = refs[:n], refs[n:]
    upper, refs = refs[:G], refs[G:]
    probs, refs = refs[:G], refs[G:]
    attn, routing, keys, values, queries = refs[:5]
    refs = refs[5:]
    query_out, refs = refs[:G], refs[G:]
    pair_out, refs = refs[: G * R], refs[G * R :]
    upper_rows, query_rows, key_sum, value_sum = refs
    scale = HD**-0.5
    for d in range(G):
        upper_rows[pl.ds(pl.multiple_of((g ^ d) * BL, BL), BL)] = upper[d][...]
    for i in reversed(range(G)):
        N = (i + 1) * R * BL
        mine = slice(i * BL, (i + 1) * BL)
        rows = jnp.concatenate([back[d][i * stride : (i + 1) * stride] for d in range(n)], axis=0)
        picked = cols_by_cols(routing[i], rows)
        grad = (upper_rows[mine].astype(F32) + picked).astype(BF16)
        delta = jnp.sum(grad.astype(F32) * attn[mine].astype(F32), axis=1, keepdims=True)
        weights = probs[i][...]
        dprob = rows_by_rows(grad, values[0:N])
        dscore = (weights.astype(F32) * (dprob - delta)).astype(BF16)
        query_rows[mine] = (plain(dscore, keys[0:N]) * scale).astype(BF16)
        key_part = cols_by_cols(dscore, queries[mine]) * scale
        value_part = cols_by_cols(weights, grad)
        if i == G - 1:
            key_sum[...] = key_part
            value_sum[...] = value_part
        else:
            key_sum[0:N] += key_part
            value_sum[0:N] += value_part
    for d in range(G):
        i = g ^ d
        query_out[d][...] = query_rows[pl.ds(pl.multiple_of(i * BL, BL), BL)]
        for dr in range(R):
            rows = pl.ds(pl.multiple_of((i * R + (r ^ dr)) * BL, BL), BL)
            pair_out[dr * G + d][0:BL] = key_sum[rows].astype(BF16)
            pair_out[dr * G + d][BL : 2 * BL] = value_sum[rows].astype(BF16)


def unpack_body(sizes, idx, *refs):
    G, R, BL = sizes
    g = idx[1]
    query_in, pair_in, outs = refs[:G], refs[G : 2 * G], refs[2 * G :]
    for d in range(G):
        cols = pl.ds(pl.multiple_of((g ^ d) * HD, HD), HD)
        outs[0][:, cols] = query_in[d][...]
        outs[1][:, cols] = pair_in[d][0:BL]
        outs[2][:, cols] = pair_in[d][BL : 2 * BL]


def gather_tokens_body(sizes, idx, *refs):
    G, R, rows = sizes
    g = idx[1]
    out = refs[-1]
    for dg in range(G):
        cols = pl.ds(pl.multiple_of((g ^ dg) * HD, HD), HD)
        for dr in range(R):
            out[dr * rows : (dr + 1) * rows, cols] = refs[dg * R + dr][...]


def gather_grads_body(sizes, idx, *refs):
    G, R, stride = sizes
    g = idx[1]
    out = refs[-1]
    for dg in range(G):
        for dr in range(R):
            at = pl.multiple_of((dr * G + (g ^ dg)) * stride, 16)
            out[pl.ds(at, stride)] = refs[dg * R + dr][...]


def through_body(idx, *refs):
    shards, weight, out = refs[:-2], refs[-2], refs[-1]
    width = shards[0].shape[1]
    total = None
    for k, shard in enumerate(shards):
        cols = pl.ds(pl.multiple_of((idx[3] ^ k) * width, 128), width)
        part = rows_by_rows(shard[...], weight[:, cols])
        total = part if total is None else total + part
    out[...] = total


def pre_body(first, start, idx, *refs):
    if start is None:
        shards, weight, out = refs[:-2], refs[-2], refs[-1]
        total = None
    else:
        shards, weight, begun, through, hidden, hidden_grad = refs[:-5], refs[-5], refs[-4], refs[-3], refs[-2], refs[-1]
        total = begun[...]
    width = shards[0].shape[1]
    for k, shard in enumerate(shards):
        rows = pl.ds(pl.multiple_of((idx[3] ^ (first + k)) * width, 128), width)
        part = plain(shard[...], weight[rows, :])
        total = part if total is None else total + part
    if start is None:
        out[...] = total
    else:
        logistic = 1.0 / (1.0 + jnp.exp(-total))
        hidden[...] = (total * logistic).astype(BF16)
        hidden_grad[...] = (through[...] * logistic * (1.0 + total * (1.0 - logistic))).astype(BF16)


def back_body(shards, idx, grad, weight, out):
    width = out.shape[2]
    for at, k in enumerate(shards):
        rows = pl.ds(pl.multiple_of((idx[3] ^ k) * width, 128), width)
        out[at] = rows_by_rows(grad[...], weight[rows, :]).astype(BF16)


def out_weight_body(idx, hidden, *refs):
    out = refs[-1]
    width = refs[0].shape[1]
    for k, shard in enumerate(refs[:-1]):
        cols = pl.ds(pl.multiple_of((idx[3] ^ k) * width, 128), width)
        out[:, cols] = cols_by_cols(hidden[...], shard[...]).astype(BF16)


def in_weight_body(idx, grad, *refs):
    out = refs[-1]
    width = refs[0].shape[1]
    for k, shard in enumerate(refs[:-1]):
        rows = pl.ds(pl.multiple_of((idx[3] ^ k) * width, 128), width)
        out[rows, :] = cols_by_cols(shard[...], grad[...]).astype(BF16)


def gather_exp(block, size):
    shards = [block]
    distance = size // 2
    by_place = {0: block}
    while distance:
        for place in list(by_place):
            by_place[place ^ distance] = swap(by_place[place], "exp", distance)
        distance //= 2
    shards = [by_place[k] for k in range(size)]
    return shards


def per_device(
    queries,
    key_rows,
    value_rows,
    out_grad,
    expert_ids,
    gate_values,
    alibi_slope,
    expert_in,
    expert_out,
):
    BL, features = queries.shape
    G = features // HD
    n = lax.axis_size("seq")
    E = lax.axis_size("exp")
    R = n // G
    cap = 5 * BL // (2 * n)
    stride = -(-cap // 16) * 16
    rows = n * stride
    FFL = expert_in.shape[2]
    L = n * BL
    seq_index = lax.axis_index("seq")
    idx = jnp.stack([seq_index, seq_index // R, seq_index % R, lax.axis_index("exp")]).astype(jnp.int32)
    weight_in = expert_in[0]
    weight_out = expert_out[0]

    id_rows = expert_ids.T.reshape(2 * BL // 128, 128).astype(BF16)
    id_rows = jnp.pad(id_rows, ((0, 16 - 2 * BL // 128), (0, 0)))
    payload = local_call(
        functools.partial(pack_body, (G, R, BL)),
        [((3 * BL + 16, HD), BF16)] * G,
        [idx],
        [queries, key_rows, value_rows, id_rows],
        nbytes=6 * BL * features * 2,
    )
    own = [swap(payload[d], "seq", d * R) for d in range(G)]
    others = [swap(own[d][: 2 * BL], "seq", dr) for dr in range(1, R) for d in range(G)]

    sent = local_call(
        functools.partial(grads_body, (G, R, BL, cap, stride)),
        [((stride, features), BF16)] * n + [((BL, HD), BF16)] * G,
        [idx],
        [out_grad, gate_values, id_rows],
        flops=2 * rows * 2 * BL * features,
        nbytes=3 * BL * features * 2,
    )
    grad_pieces = [swap(sent[d], "seq", d) for d in range(n)]
    upper = [swap(sent[n + d], "seq", d * R) for d in range(G)]

    shapes = [((BL, (i + 1) * R * BL), BF16) for i in range(G)]
    shapes += [((G * stride, HD), BF16)] * n
    shapes += [((G * BL, HD), BF16), ((G, rows, BL), BF16), ((L, HD), BF16), ((L, HD), BF16), ((G * BL, HD), BF16)]
    made = local_call(
        functools.partial(forward_body, (G, R, BL, cap, stride)),
        shapes,
        [idx, alibi_slope],
        own + others,
        scratch=[pltpu.VMEM((G, 16, 128), F32)],
        flops=4 * G * BL * L * HD,
        nbytes=10 * 1024 * 1024,
    )
    probs, made = made[:G], made[G:]
    token_sent, made = made[:n], made[n:]
    attn, routing, keys, values, query_rows = made

    grads = local_call(
        functools.partial(gather_grads_body, (G, R, stride)),
        [((rows, features), BF16)],
        [idx],
        grad_pieces,
        nbytes=rows * features * 4,
    )[0]
    grad_shards = gather_exp(grads, E)
    through = local_call(
        through_body,
        [((rows, FFL), F32)],
        [idx],
        grad_shards + [weight_out],
        flops=2 * rows * FFL * features * E,
        nbytes=10 * 1024 * 1024,
    )[0]

    token_pieces = [swap(token_sent[d], "seq", d) for d in range(n)]
    tokens = local_call(
        functools.partial(gather_tokens_body, (G, R, G * stride)),
        [((rows, features), BF16)],
        [idx],
        token_pieces,
        nbytes=rows * features * 4,
    )[0]
    token_shards = gather_exp(tokens, E)
    half = E // 2
    begun = local_call(
        functools.partial(pre_body, 0, None),
        [((rows, FFL), F32)],
        [idx],
        token_shards[:half] + [weight_in],
        flops=2 * rows * FFL * features * half,
        nbytes=8 * 1024 * 1024,
    )[0]
    hidden, hidden_grad = local_call(
        functools.partial(pre_body, half, True),
        [((rows, FFL), BF16)] * 2,
        [idx],
        token_shards[half:] + [weight_in, begun, through],
        flops=2 * rows * FFL * features * half,
        nbytes=8 * 1024 * 1024,
    )

    def back_parts(shards):
        return local_call(
            functools.partial(back_body, shards),
            [((len(shards), rows, features), BF16)],
            [idx],
            [hidden_grad, weight_in],
            flops=2 * rows * FFL * features * len(shards),
            nbytes=8 * 1024 * 1024,
        )[0]

    odd = list(range(1, E, 2))
    even = list(range(0, E, 2))
    held = back_parts(odd)
    moved = swap(held, "exp", 1)
    kept = back_parts(even)
    held = [(kept[k].astype(F32) + moved[k].astype(F32)) for k in range(E // 2)]
    distance = E // 2
    while distance > 1:
        count = len(held) // 2
        moved = [swap(held[count + k].astype(BF16), "exp", distance) for k in range(count)]
        held = [held[k] + moved[k].astype(F32) for k in range(count)]
        distance //= 2
    back = held[0].astype(BF16)

    g = idx[1]
    back_view = back.reshape(R, G * stride, features)
    back_sent = [
        lax.dynamic_slice_in_dim(back_view[d % R], (g ^ (d // R)) * HD, HD, axis=1) for d in range(n)
    ]
    returned = [swap(back_sent[d], "seq", d) for d in range(n)]

    out_weight_grad = local_call(
        out_weight_body,
        [((FFL, features * E), BF16)],
        [idx],
        [hidden] + grad_shards,
        flops=2 * rows * FFL * features * E,
        nbytes=10 * 1024 * 1024,
    )[0]
    in_weight_grad = local_call(
        in_weight_body,
        [((features * E, FFL), BF16)],
        [idx],
        [hidden_grad] + token_shards,
        flops=2 * rows * FFL * features * E,
        nbytes=10 * 1024 * 1024,
    )[0]

    made = local_call(
        functools.partial(backward_body, (G, R, BL, cap, stride)),
        [((BL, HD), BF16)] * G + [((2 * BL, HD), BF16)] * (G * R),
        [idx],
        returned + upper + list(probs) + [attn, routing, keys, values, query_rows],
        scratch=[
            pltpu.VMEM((G * BL, HD), BF16),
            pltpu.VMEM((G * BL, HD), BF16),
            pltpu.VMEM((L, HD), F32),
            pltpu.VMEM((L, HD), F32),
        ],
        flops=8 * G * BL * L * HD,
        nbytes=10 * 1024 * 1024,
    )
    query_pieces, pair_pieces = made[:G], made[G:]
    query_home = [swap(query_pieces[d], "seq", d * R) for d in range(G)]
    pair_home = []
    for d in range(G):
        total = pair_pieces[d].astype(F32)
        for dr in range(1, R):
            total = total + swap(pair_pieces[dr * G + d], "seq", dr).astype(F32)
        pair_home.append(swap(total.astype(BF16), "seq", d * R))
    query_grad, key_grad, value_grad = local_call(
        functools.partial(unpack_body, (G, R, BL)),
        [((BL, features), BF16)] * 3,
        [idx],
        query_home + pair_home,
        nbytes=6 * BL * features * 2,
    )
    return query_grad, key_grad, value_grad, in_weight_grad[None], out_weight_grad[None]


def solution(mesh):
    return jax.shard_map(
        per_device,
        mesh=mesh,
        in_specs=(
            P("seq", "exp"),
            P("seq", "exp"),
            P("seq", "exp"),
            P("seq", "exp"),
            P("seq", None),
            P("seq", None),
            P("exp"),
            P("seq", None, "exp"),
            P("seq", "exp", None),
        ),
        out_specs=(
            P("seq", "exp"),
            P("seq", "exp"),
            P("seq", "exp"),
            P("seq", None, "exp"),
            P("seq", "exp", None),
        ),
        check_vma=False,
    )
```

time: 824 us -> 208 us (0.25); the launches traced: 811 us -> 208 us
  waiting for transfers between devices: 316 us -> 50.9 us
  starting transfers between devices: 194 us -> 67.4 us
  local copies, waits for them, and re-layouts: 107 us -> 9.73 us
  matrix products: 84.8 us -> 0 us
  Pallas kernels: 0 us -> 73.8 us
  other arithmetic: 55.1 us -> 4.62 us
  blocking collectives: 38.7 us -> 0 us
  between operations: 14.5 us -> 1.19 us
    ppermute x64 -> x49, waiting for transfers between devices: 248 us -> 50.9 us  [swap(): return lax.ppermute(block, axis, [(i, i ^ distance) for i in devices])]
    ppermute x64 -> x49, starting transfers between devices: 188 us -> 67.4 us  [swap(): return lax.ppermute(block, axis, [(i, i ^ distance) for i in devices])]
    dot_general x14 -> x0, matrix products: 84.8 us -> none  [the longest x1 12.7 us: per_device(): jnp.einsum('hij,ihd->jhd', weights, grad_heads, preferred_element_type=jn...]
    pallas_call x0 -> x14, Pallas kernels: none -> 73.8 us  [local_call(): pl.pallas_call(body, out_shape=[jax.ShapeDtypeStruct(shape, dtype) for sh...]
    reshape x6 -> x0, local copies, waits for them, and re-layouts: 48.8 us -> none  [the longest x2 17 us: per_device(): key_block = key_stack.reshape(stretches * block_len, head_count, HD)]
    all_to_all x2 -> x0, blocking collectives: 38.7 us -> none  [the longest x1 23.5 us: per_device(): lax.all_to_all(send_tokens, 'seq', split_axis=0, concat_axis=0, tiled=True)]
    add x35 -> x0, other arithmetic: 35.6 us -> none  [the longest x16 17.8 us: relay_grads(): value_acc + lax.dynamic_index_in_dim(value_parts, index, 0, keepdims=False)]
    reduce_scatter x1 -> x0, waiting for transfers between devices: 34.8 us -> none  [per_device(): lax.psum_scatter(lax.dot_general(weight_in, hidden_grad, (((1,), (1,)), (...]
  transfers between devices with their start and end apart: 68 -> 49, of which waited for: 66 -> 16; matrix products, arithmetic and copies ran while one was open for 5% -> 2% of each run, Pallas kernels for 0% -> 23%
where the time goes in v1:
time: 208 us
  Pallas kernels  73.8 us (35%)
  starting transfers between devices  67.4 us (32%)
  waiting for transfers between devices  50.9 us (24%)
  local copies, waits for them, and re-layouts  9.73 us (5%)
  other arithmetic  4.62 us (2%)
    pallas_call x14, Pallas kernels, local_call(): pl.pallas_call(body, out_shape=[jax.ShapeDtypeStruct(shape, dtype) for sh...  73.8 us
    ppermute x49, starting transfers between devices, swap(): return lax.ppermute(block, axis, [(i, i ^ distance) for i in devices])  67.4 us
    ppermute x49, waiting for transfers between devices, swap(): return lax.ppermute(block, axis, [(i, i ^ distance) for i in devices])  50.9 us
    unnamed x115, local copies, waits for them, and re-layouts  8.27 us
  transfers between devices with their start and end apart: 49, of which 16 were waited for; matrix products, arithmetic and copies ran while one was open for 2% of the time, Pallas kernels for 23%

profile of v1, /device:TPU:0, one launch (start us, length us, event | category | flops | bytes accessed | tf_op | source)
XLA Modules:
  0.0 207.6 jit_solution(4242722658128151314)
XLA Ops:
  2.6 2.1 %shard_map.128 = (bf16[784,128]{1,0:T(8,128)(2,1)}, bf16[784,128]{1,0:T(8,128)(2,1)}, bf16[784,128]{1,0:T(8,128)(2,1)}, bf16[784,128]{1,0:T(8,128)(2,1)}) custom-call(s32[4]{0:T(128)} %pad_add_fusion.idx, bf16[256,512]{1,0:T(8,128)(2,1)} %q.1, bf16[256,512]{1,0:T(8,128)(2,1)} %k.1, bf16[256,512]{1,0:T(8,128)(2,1)} %v.1, bf16[16,128]{1,0:T(8,128)(2,1)} %pad.4.ids), custom_call_target="tpu_custom_call" | custom-call | bytes 1572864 | tf_op jit(solution)/shard_map/pallas_call | solution.py:45
  4.7 3.0 %collective-permute-start = (bf16[784,128]{1,0:T(8,128)(2,1)}, bf16[784,128]{1,0:T(8,128)(2,1)S(1)}, u32[]{:S(2)}, u32[]{:S(2)}) collective-permute-start(bf16[784,128]{1,0:T(8,128)(2,1)} %get-tuple-element.56), channel_id=1, source_target_pairs={{0,8},{4,12},{8,0},{12,4},{16,24},{20,28},{24,16},{28,20},{1,9},{5... | collective-permute-start | bytes 602120 | tf_op jit(solution)/shard_map/ppermute | solution.py:39
  7.8 2.6 %collective-permute-start.1 = (bf16[784,128]{1,0:T(8,128)(2,1)}, bf16[784,128]{1,0:T(8,128)(2,1)S(1)}, u32[]{:S(2)}, u32[]{:S(2)}) collective-permute-start(bf16[784,128]{1,0:T(8,128)(2,1)} %get-tuple-element.57), channel_id=1, source_target_pairs={{0,16},{4,20},{8,24},{12,28},{16,0},{20,4},{24,8},{28,12},{1,17},{... | collective-permute-start | bytes 602120 | tf_op jit(solution)/shard_map/ppermute | solution.py:39
  11.8 2.5 %shard_map.132 = (bf16[80,512]{1,0:T(8,128)(2,1)}, bf16[80,512]{1,0:T(8,128)(2,1)}, bf16[80,512]{1,0:T(8,128)(2,1)}, bf16[80,512]{1,0:T(8,128)(2,1)}, bf16[80,51...) custom-call(s32[4]{0:T(128)} %pad_add_fusion.idx, ...), custom_call_target="tpu_custom_call" | custom-call | flops 335544320 | bytes 786432 | tf_op jit(solution)/shard_map/pallas_call | solution.py:45
  16.8 2.3 %collective-permute-done.17.refs_1_ = bf16[80,512]{1,0:T(8,128)(2,1)S(1)} collective-permute-done((bf16[80,512]{1,0:T(8,128)(2,1)}, bf16[80,512]{1,0:T(8,128)(2,1)S(1)}, u32[]{:S(2)}, u32[]{:S(2)}) %collective-permute-start.17) | collective-permute-done | bytes 81952 | tf_op jit(solution)/shard_map/ppermute | solution.py:39
  20.9 3.5 %collective-permute-start.20 = (bf16[80,512]{1,0:T(8,128)(2,1)}, bf16[80,512]{1,0:T(8,128)(2,1)S(1)}, u32[]{:S(2)}, u32[]{:S(2)}) collective-permute-start(bf16[80,512]{1,0:T(8,128)(2,1)} %get-tuple-element.71), channel_id=1, source_target_pairs={{0,16},{4,20},{8,24},{12,28},{16,0},{20,4},{24,8},{28,12},{1,17},{... | collective-permute-start | bytes 245768 | tf_op jit(solution)/shard_map/ppermute | solution.py:39
  25.9 2.5 %collective-permute-start.22 = (bf16[80,512]{1,0:T(8,128)(2,1)}, bf16[80,512]{1,0:T(8,128)(2,1)S(1)}, u32[]{:S(2)}, u32[]{:S(2)}) collective-permute-start(bf16[80,512]{1,0:T(8,128)(2,1)} %get-tuple-element.73), channel_id=1, source_target_pairs={{0,24},{4,28},{8,16},{12,20},{16,8},{20,12},{24,0},{28,4},{1,25},{... | collective-permute-start | bytes 245768 | tf_op jit(solution)/shard_map/ppermute | solution.py:39
  30.5 6.2 %collective-permute-done.20.refs_4_ = bf16[80,512]{1,0:T(8,128)(2,1)S(1)} collective-permute-done((bf16[80,512]{1,0:T(8,128)(2,1)}, bf16[80,512]{1,0:T(8,128)(2,1)S(1)}, u32[]{:S(2)}, u32[]{:S(2)}) %collective-permute-start.20) | collective-permute-done | bytes 81952 | tf_op jit(solution)/shard_map/ppermute | solution.py:39
  39.5 3.3 %collective-permute-start.23 = (bf16[80,512]{1,0:T(8,128)(2,1)}, bf16[80,512]{1,0:T(8,128)(2,1)S(1)}, u32[]{:S(2)}, u32[]{:S(2)}) collective-permute-start(bf16[80,512]{1,0:T(8,128)(2,1)} %get-tuple-element.74), channel_id=1, source_target_pairs={{0,28},{4,24},{8,20},{12,16},{16,12},{20,8},{24,4},{28,0},{1,29},{... | collective-permute-start | bytes 245768 | tf_op jit(solution)/shard_map/ppermute | solution.py:39
  42.8 4.2 %collective-permute-done.23.refs_7_ = bf16[80,512]{1,0:T(8,128)(2,1)S(1)} collective-permute-done((bf16[80,512]{1,0:T(8,128)(2,1)}, bf16[80,512]{1,0:T(8,128)(2,1)S(1)}, u32[]{:S(2)}, u32[]{:S(2)}) %collective-permute-start.23) | collective-permute-done | bytes 81952 | tf_op jit(solution)/shard_map/ppermute | solution.py:39
  47.6 2.1 %shard_map.133.refs_0_ = bf16[640,512]{1,0:T(8,128)(2,1)} custom-call(s32[4]{0:T(128)} %pad_add_fusion.idx, bf16[80,512]{1,0:T(8,128)(2,1)} %get-tuple-element.67.refs_0_, bf16[80,512]{1,0:T(8,128)(2,1)} %copy-done.16, bf16[80,512]{1,0:T(8,128)(2,1)} %copy-done.17, bf16[80,512]{1,0:T(8,128)(2,1)} %copy-done.18, bf16[80,512]{1,0:T(8,128)(2,1)} %copy-done.19, ...), custom_call_target="tpu_custom_call" | custom-call | bytes 1310720 | tf_op jit(solution)/shard_map/pallas_call | solution.py:45
  52.6 7.5 %shard_map.129 = (bf16[256,512]{1,0:T(8,128)(2,1)}, bf16[256,1024]{1,0:T(8,128)(2,1)}, bf16[256,1536]{1,0:T(8,128)(2,1)}, bf16[256,2048]{1,0:T(8,128)(2,1)}, bf1...) custom-call(s32[4]{0:T(128)} %pad_add_fusion.idx, ...), custom_call_target="tpu_custom_call" | custom-call | flops 1073741824 | bytes 10485760 | tf_op jit(solution)/shard_map/pallas_call | solution.py:45
  60.3 3.7 %collective-permute-start.11 = (bf16[320,128]{1,0:T(8,128)(2,1)}, bf16[320,128]{1,0:T(8,128)(2,1)S(1)}, u32[]{:S(2)}, u32[]{:S(2)}) collective-permute-start(bf16[320,128]{1,0:T(8,128)(2,1)} %get-tuple-element.64), channel_id=1, source_target_pairs={{0,20},{4,16},{8,28},{12,24},{16,4},{20,0},{24,12},{28,8},{1,21},{... | collective-permute-start | bytes 245768 | tf_op jit(solution)/shard_map/ppermute | solution.py:39
  64.0 2.3 %collective-permute-start.12 = (bf16[320,128]{1,0:T(8,128)(2,1)}, bf16[320,128]{1,0:T(8,128)(2,1)S(1)}, u32[]{:S(2)}, u32[]{:S(2)}) collective-permute-start(bf16[320,128]{1,0:T(8,128)(2,1)} %get-tuple-element.65), channel_id=1, source_target_pairs={{0,24},{4,28},{8,16},{12,20},{16,8},{20,12},{24,0},{28,4},{1,25},{... | collective-permute-start | bytes 245768 | tf_op jit(solution)/shard_map/ppermute | solution.py:39
  71.8 2.1 collective-permute-start.9
  78.1 2.2 %shard_map.130.refs_0_ = bf16[640,512]{1,0:T(8,128)(2,1)} custom-call(s32[4]{0:T(128)} %pad_add_fusion.idx, bf16[320,128]{1,0:T(8,128)(2,1)} %get-tuple-element.59.refs_0_, bf16[320,128]{1,0:T(8,128)(2,1)} %copy-done.26, bf16[320,128]{1,0:T(8,128)(2,1)} %copy-done.27, bf16[320,128]{1,0:T(8,128)(2,1)} %copy-done.28, bf16[320,128]{1,0:T(8,128)(2,1)} %copy-done.22, ...), custom_call_target="tpu_custom_call" | custom-call | bytes 1310720 | tf_op jit(solution)/shard_map/pallas_call | solution.py:45
  81.3 9.7 %collective-permute-done.14.refs_0_.refs_2_ = bf16[640,512]{1,0:T(8,128)(2,1)S(1)} collective-permute-done((bf16[640,512]{1,0:T(8,128)(2,1)}, bf16[640,512]{1,0:T(8,128)(2,1)S(1)}, u32[]{:S(2)}, u32[]{:S(2)}) %collective-permute-start.14) | collective-permute-done | bytes 655392 | tf_op jit(solution)/shard_map/ppermute | solution.py:39
  91.9 5.6 %shard_map.131.refs_3_ = f32[640,1024]{1,0:T(8,128)} custom-call(s32[4]{0:T(128)} %pad_add_fusion.idx, bf16[640,512]{1,0:T(8,128)(2,1)} %shard_map.130.refs_0_, bf16[640,512]{1,0:T(8,128)(2,1)} %copy-done.1, bf16[2048,1024]{1,0:T(8,128)(2,1)} %bitcast.16), custom_call_target="tpu_custom_call" | custom-call | flops 1342177280 | bytes 8388608 | tf_op jit(solution)/shard_map/pallas_call | solution.py:45
  98.7 7.4 %shard_map.134.refs_4_ = f32[640,1024]{1,0:T(8,128)} custom-call(s32[4]{0:T(128)} %pad_add_fusion.idx, bf16[640,512]{1,0:T(8,128)(2,1)} %shard_map.133.refs_0_, bf16[640,512]{1,0:T(8,128)(2,1)} %copy-done.34, bf16[640,512]{1,0:T(8,128)(2,1)} %copy-done.33, bf16[640,512]{1,0:T(8,128)(2,1)} %copy-done.35, bf16[1024,2048]{1,0:T(8,128)(2,1)} %bitcast.20), custom_call_target="tpu_custom_call" | custom-call | flops 2684354560 | bytes 10485760 | tf_op jit(solution)/shard_map/pallas_call | solution.py:45
  107.0 8.2 %shard_map.135 = (bf16[640,1024]{1,0:T(8,128)(2,1)}, bf16[640,1024]{1,0:T(8,128)(2,1)}) custom-call(s32[4]{0:T(128)} %pad_add_fusion.idx, bf16[640,512]{1,0:T(8,128)(2,1)} %copy-done.3, bf16[640,512]{1,0:T(8,128)(2,1)} %copy-done.4, bf16[2048,1024]{1,0:T(8,128)(2,1)} %bitcast.17, f32[640,1024]{1,0:T(8,128)} %shard_map.131.refs_3_, ...), custom_call_target="tpu_custom_call" | custom-call | flops 1342177280 | bytes 8388608 | tf_op jit(solution)/shard_map/pallas_call | solution.py:45
  115.2 5.2 %shard_map.137 = bf16[2,640,512]{2,1,0:T(8,128)(2,1)} custom-call(s32[4]{0:T(128)} %pad_add_fusion.idx, bf16[640,1024]{1,0:T(8,128)(2,1)} %get-tuple-element.75.grad, bf16[2048,1024]{1,0:T(8,128)(2,1)} %bitcast.18), custom_call_target="tpu_custom_call" | custom-call | flops 1342177280 | bytes 8388608 | tf_op jit(solution)/shard_map/pallas_call | solution.py:45
  120.8 5.2 %shard_map.136 = bf16[2,640,512]{2,1,0:T(8,128)(2,1)} custom-call(s32[4]{0:T(128)} %pad_add_fusion.idx, bf16[640,1024]{1,0:T(8,128)(2,1)} %get-tuple-element.75.grad, bf16[2048,1024]{1,0:T(8,128)(2,1)} %bitcast.19), custom_call_target="tpu_custom_call" | custom-call | flops 1342177280 | bytes 8388608 | tf_op jit(solution)/shard_map/pallas_call | solution.py:45
  126.1 2.2 %fusion.1 = bf16[640,512]{1,0:T(8,128)(2,1)} fusion(bf16[2,640,512]{2,1,0:T(8,128)(2,1)S(1)} %collective-permute-done.27, bf16[2,640,512]{2,1,0:T(8,128)(2,1)} %shard_map.136), kind=kLoop, calls=%fused_computation.3 | loop fusion | flops 1310720 | bytes 1966080 | tf_op jit(solution)/shard_map/convert_element_type | solution.py:418
  133.2 12.0 %collective-permute-done.28 = bf16[640,512]{1,0:T(8,128)(2,1)S(1)} collective-permute-done((bf16[640,512]{1,0:T(8,128)(2,1)}, bf16[640,512]{1,0:T(8,128)(2,1)S(1)}, u32[]{:S(2)}, u32[]{:S(2)}) %collective-permute-start.28) | collective-permute-done | bytes 655392 | tf_op jit(solution)/shard_map/ppermute | solution.py:39
  150.9 2.2 %collective-permute-start.35 = (bf16[320,128]{1,0:T(8,128)(2,1)S(1)}, bf16[320,128]{1,0:T(8,128)(2,1)S(1)}, u32[]{:S(2)}, u32[]{:S(2)}) collective-permute-start(bf16[320,128]{1,0:T(8,128)(2,1)S(1)} %get-tuple-element.107), channel_id=1, source_target_pairs={{0,28},{4,24},{8,20},{12,16},{16,12},{20,8},{24,4},{28,0},{1,29},{... | collective-permute-start | bytes 245768 | tf_op jit(solution)/shard_map/ppermute | solution.py:39
  157.5 7.5 %shard_map.140 = bf16[2048,1024]{1,0:T(8,128)(2,1)} custom-call(s32[4]{0:T(128)} %pad_add_fusion.idx, bf16[640,1024]{1,0:T(8,128)(2,1)} %get-tuple-element.75.grad, bf16[640,512]{1,0:T(8,128)(2,1)} %shard_map.130.refs_0_, bf16[640,512]{1,0:T(8,128)(2,1)} %copy-done.1, bf16[640,512]{1,0:T(8,128)(2,1)} %copy-done.3, bf16[640,512]{1,0:T(8,128)(2,1)} %copy-done.4), custom_call_target="tpu_custom_call" | custom-call | flops 2684354560 | bytes 10485760 | tf_op jit(solution)/shard_map/pallas_call | solution.py:45
  165.9 8.0 %shard_map.138 = (bf16[256,128]{1,0:T(8,128)(2,1)}, bf16[256,128]{1,0:T(8,128)(2,1)}, bf16[256,128]{1,0:T(8,128)(2,1)}, bf16[256,128]{1,0:T(8,128)(2,1)}, bf16[5...) custom-call(s32[4]{0:T(128)} %pad_add_fusion.idx, ...), custom_call_target="tpu_custom_call" | custom-call | flops 2147483648 | bytes 10485760 | tf_op jit(solution)/shard_map/pallas_call | solution.py:45
  175.3 7.9 %shard_map.141 = bf16[1024,2048]{1,0:T(8,128)(2,1)} custom-call(s32[4]{0:T(128)} %pad_add_fusion.idx, bf16[640,1024]{1,0:T(8,128)(2,1)} %get-tuple-element.104.hidden, bf16[640,512]{1,0:T(8,128)(2,1)} %shard_map.133.refs_0_, bf16[640,512]{1,0:T(8,128)(2,1)} %copy-done.34, bf16[640,512]{1,0:T(8,128)(2,1)} %copy-done.33, bf16[640,512]{1,0:T(8,128)(2,1)} %copy-done.35), custom_call_target="tpu_custom_call" | custom-call | flops 2684354560 | bytes 10485760 | tf_op jit(solution)/shard_map/pallas_call | solution.py:45
  190.5 2.5 %collective-permute-start.48 = (bf16[512,128]{1,0:T(8,128)(2,1)S(1)}, bf16[512,128]{1,0:T(8,128)(2,1)S(1)}, u32[]{:S(2)}, u32[]{:S(2)}) collective-permute-start(bf16[512,128]{1,0:T(8,128)(2,1)S(1)} %add_convert_fusion.1), channel_id=1, source_target_pairs={{0,24},{4,28},{8,16},{12,20},{16,8},{20,12},{24,0},{28,4},{1,25},{... | collective-permute-start | bytes 393224 | tf_op jit(solution)/shard_map/ppermute | solution.py:39
  195.8 2.5 %collective-permute-done.40.refs_2_ = bf16[256,128]{1,0:T(8,128)(2,1)S(1)} collective-permute-done((bf16[256,128]{1,0:T(8,128)(2,1)S(1)}, bf16[256,128]{1,0:T(8,128)(2,1)S(1)}, u32[]{:S(2)}, u32[]{:S(2)}) %collective-permute-start.40) | collective-permute-done | bytes 65568 | tf_op jit(solution)/shard_map/ppermute | solution.py:39
  198.6 6.1 %collective-permute-done.46.refs_6_ = bf16[512,128]{1,0:T(8,128)(2,1)S(1)} collective-permute-done((bf16[512,128]{1,0:T(8,128)(2,1)S(1)}, bf16[512,128]{1,0:T(8,128)(2,1)S(1)}, u32[]{:S(2)}, u32[]{:S(2)}) %collective-permute-start.46) | collective-permute-done | bytes 131104 | tf_op jit(solution)/shard_map/ppermute | solution.py:39
  205.4 2.2 %shard_map.139 = (bf16[256,512]{1,0:T(8,128)(2,1)}, bf16[256,512]{1,0:T(8,128)(2,1)}, bf16[256,512]{1,0:T(8,128)(2,1)}) custom-call(s32[4]{0:T(128)} %pad_add_fusion.idx, bf16[256,128]{1,0:T(8,128)(2,1)} %get-tuple-element.89.refs_0_, bf16[256,128]{1,0:T(8,128)(2,1)} %copy-done.30, bf16[256,128]{1,0:T(8,128)(2,1)} %copy-done.31, ...), custom_call_target="tpu_custom_call" | custom-call | bytes 1572864 | tf_op jit(solution)/shard_map/pallas_call | solution.py:45
  (212 shorter events, 59.8 us)
Async XLA Ops:
  4.7 16.2 %collective-permute-start = (bf16[784,128]{1,0:T(8,128)(2,1)}, bf16[784,128]{1,0:T(8,128)(2,1)S(1)}, u32[]{:S(2)}, u32[]{:S(2)}) collective-permute-start(bf16[784,128]{1,0:T(8,128)(2,1)} %get-tuple-element.56), channel_id=1, source_target_pairs={{0,8},{4,12},{8,0},{12,4},{16,24},{20,28},{24,16},{28,20},{1,9},{5... | collective-permute-start | bytes 602120 | tf_op jit(solution)/shard_map/ppermute | solution.py:39
  7.8 17.7 %collective-permute-start.1 = (bf16[784,128]{1,0:T(8,128)(2,1)}, bf16[784,128]{1,0:T(8,128)(2,1)S(1)}, u32[]{:S(2)}, u32[]{:S(2)}) collective-permute-start(bf16[784,128]{1,0:T(8,128)(2,1)} %get-tuple-element.57), channel_id=1, source_target_pairs={{0,16},{4,20},{8,24},{12,28},{16,0},{20,4},{24,8},{28,12},{1,17},{... | collective-permute-start | bytes 602120 | tf_op jit(solution)/shard_map/ppermute | solution.py:39
  10.4 15.5 %collective-permute-start.2 = (bf16[784,128]{1,0:T(8,128)(2,1)}, bf16[784,128]{1,0:T(8,128)(2,1)S(1)}, u32[]{:S(2)}, u32[]{:S(2)}) collective-permute-start(bf16[784,128]{1,0:T(8,128)(2,1)} %get-tuple-element.58), channel_id=1, source_target_pairs={{0,24},{4,28},{8,16},{12,20},{16,8},{20,12},{24,0},{28,4},{1,25},{... | collective-permute-start | bytes 602120 | tf_op jit(solution)/shard_map/ppermute | solution.py:39
  16.1 12.3 %collective-permute-start.18 = (bf16[80,512]{1,0:T(8,128)(2,1)}, bf16[80,512]{1,0:T(8,128)(2,1)S(1)}, u32[]{:S(2)}, u32[]{:S(2)}) collective-permute-start(bf16[80,512]{1,0:T(8,128)(2,1)} %get-tuple-element.69), channel_id=1, source_target_pairs={{0,8},{4,12},{8,0},{12,4},{16,24},{20,28},{24,16},{28,20},{1,9},{5... | collective-permute-start | bytes 245768 | tf_op jit(solution)/shard_map/ppermute | solution.py:39
  19.1 10.9 %collective-permute-start.19 = (bf16[80,512]{1,0:T(8,128)(2,1)}, bf16[80,512]{1,0:T(8,128)(2,1)S(1)}, u32[]{:S(2)}, u32[]{:S(2)}) collective-permute-start(bf16[80,512]{1,0:T(8,128)(2,1)} %get-tuple-element.70), channel_id=1, source_target_pairs={{0,12},{4,8},{8,4},{12,0},{16,28},{20,24},{24,20},{28,16},{1,13},{... | collective-permute-start | bytes 245768 | tf_op jit(solution)/shard_map/ppermute | solution.py:39
  20.9 15.8 %collective-permute-start.20 = (bf16[80,512]{1,0:T(8,128)(2,1)}, bf16[80,512]{1,0:T(8,128)(2,1)S(1)}, u32[]{:S(2)}, u32[]{:S(2)}) collective-permute-start(bf16[80,512]{1,0:T(8,128)(2,1)} %get-tuple-element.71), channel_id=1, source_target_pairs={{0,16},{4,20},{8,24},{12,28},{16,0},{20,4},{24,8},{28,12},{1,17},{... | collective-permute-start | bytes 245768 | tf_op jit(solution)/shard_map/ppermute | solution.py:39
  25.4 13.5 %collective-permute-start.21 = (bf16[80,512]{1,0:T(8,128)(2,1)}, bf16[80,512]{1,0:T(8,128)(2,1)S(1)}, u32[]{:S(2)}, u32[]{:S(2)}) collective-permute-start(bf16[80,512]{1,0:T(8,128)(2,1)} %get-tuple-element.72), channel_id=1, source_target_pairs={{0,20},{4,16},{8,28},{12,24},{16,4},{20,0},{24,12},{28,8},{1,21},{... | collective-permute-start | bytes 245768 | tf_op jit(solution)/shard_map/ppermute | solution.py:39
  25.9 13.7 %collective-permute-start.22 = (bf16[80,512]{1,0:T(8,128)(2,1)}, bf16[80,512]{1,0:T(8,128)(2,1)S(1)}, u32[]{:S(2)}, u32[]{:S(2)}) collective-permute-start(bf16[80,512]{1,0:T(8,128)(2,1)} %get-tuple-element.73), channel_id=1, source_target_pairs={{0,24},{4,28},{8,16},{12,20},{16,8},{20,12},{24,0},{28,4},{1,25},{... | collective-permute-start | bytes 245768 | tf_op jit(solution)/shard_map/ppermute | solution.py:39
  28.4 22.8 %collective-permute-start.3 = (bf16[512,128]{1,0:T(8,128)(2,1)S(1)}, bf16[512,128]{1,0:T(8,128)(2,1)S(1)}, u32[]{:S(2)}, u32[]{:S(2)}) collective-permute-start(bf16[512,128]{1,0:T(8,128)(2,1)S(1)} %slice.38), channel_id=1, source_target_pairs={{0,4},{4,0},{8,12},{12,8},{16,20},{20,16},{24,28},{28,24},{1,5},{5... | collective-permute-start | bytes 393224 | tf_op jit(solution)/shard_map/ppermute | solution.py:39
  30.0 21.3 %collective-permute-start.4 = (bf16[512,128]{1,0:T(8,128)(2,1)S(1)}, bf16[512,128]{1,0:T(8,128)(2,1)S(1)}, u32[]{:S(2)}, u32[]{:S(2)}) collective-permute-start(bf16[512,128]{1,0:T(8,128)(2,1)S(1)} %slice.48), channel_id=1, source_target_pairs={{0,4},{4,0},{8,12},{12,8},{16,20},{20,16},{24,28},{28,24},{1,5},{5... | collective-permute-start | bytes 393224 | tf_op jit(solution)/shard_map/ppermute | solution.py:39
  36.8 14.5 %collective-permute-start.5 = (bf16[512,128]{1,0:T(8,128)(2,1)S(1)}, bf16[512,128]{1,0:T(8,128)(2,1)S(1)}, u32[]{:S(2)}, u32[]{:S(2)}) collective-permute-start(bf16[512,128]{1,0:T(8,128)(2,1)S(1)} %slice.49), channel_id=1, source_target_pairs={{0,4},{4,0},{8,12},{12,8},{16,20},{20,16},{24,28},{28,24},{1,5},{5... | collective-permute-start | bytes 393224 | tf_op jit(solution)/shard_map/ppermute | solution.py:39
  38.9 12.4 %collective-permute-start.6 = (bf16[512,128]{1,0:T(8,128)(2,1)S(1)}, bf16[512,128]{1,0:T(8,128)(2,1)S(1)}, u32[]{:S(2)}, u32[]{:S(2)}) collective-permute-start(bf16[512,128]{1,0:T(8,128)(2,1)S(1)} %slice.50), channel_id=1, source_target_pairs={{0,4},{4,0},{8,12},{12,8},{16,20},{20,16},{24,28},{28,24},{1,5},{5... | collective-permute-start | bytes 393224 | tf_op jit(solution)/shard_map/ppermute | solution.py:39
  49.7 31.6 %collective-permute-start.25 = (bf16[640,512]{1,0:T(8,128)(2,1)}, bf16[640,512]{1,0:T(8,128)(2,1)S(1)}, u32[]{:S(2)}, u32[]{:S(2)}) collective-permute-start(bf16[640,512]{1,0:T(8,128)(2,1)} %shard_map.133.refs_0_), channel_id=1, source_target_pairs={{0,2},{1,3},{2,0},{3,1},{4,6},{5,7},{6,4},{7,5},{8,10},{9,11},{10,... | collective-permute-start | bytes 1966088 | tf_op jit(solution)/shard_map/ppermute | solution.py:39
  60.3 11.5 %collective-permute-start.11 = (bf16[320,128]{1,0:T(8,128)(2,1)}, bf16[320,128]{1,0:T(8,128)(2,1)S(1)}, u32[]{:S(2)}, u32[]{:S(2)}) collective-permute-start(bf16[320,128]{1,0:T(8,128)(2,1)} %get-tuple-element.64), channel_id=1, source_target_pairs={{0,20},{4,16},{8,28},{12,24},{16,4},{20,0},{24,12},{28,8},{1,21},{... | collective-permute-start | bytes 245768 | tf_op jit(solution)/shard_map/ppermute | solution.py:39
  80.2 10.8 %collective-permute-start.14 = (bf16[640,512]{1,0:T(8,128)(2,1)}, bf16[640,512]{1,0:T(8,128)(2,1)S(1)}, u32[]{:S(2)}, u32[]{:S(2)}) collective-permute-start(bf16[640,512]{1,0:T(8,128)(2,1)} %shard_map.130.refs_0_), channel_id=1, source_target_pairs={{0,2},{1,3},{2,0},{3,1},{4,6},{5,7},{6,4},{7,5},{8,10},{9,11},{10,... | collective-permute-start | bytes 1966088 | tf_op jit(solution)/shard_map/ppermute | solution.py:39
  80.7 10.3 %collective-permute-start.16 = (bf16[640,512]{1,0:T(8,128)(2,1)}, bf16[640,512]{1,0:T(8,128)(2,1)S(1)}, u32[]{:S(2)}, u32[]{:S(2)}) collective-permute-start(bf16[640,512]{1,0:T(8,128)(2,1)} %shard_map.130.refs_0_), channel_id=1, source_target_pairs={{0,1},{1,0},{2,3},{3,2},{4,5},{5,4},{6,7},{7,6},{8,9},{9,8},{10,11... | collective-permute-start | bytes 1966088 | tf_op jit(solution)/shard_map/ppermute | solution.py:39
  80.8 16.8 %collective-permute-start.24 = (bf16[640,512]{1,0:T(8,128)(2,1)S(1)}, bf16[640,512]{1,0:T(8,128)(2,1)S(1)}, u32[]{:S(2)}, u32[]{:S(2)}) collective-permute-start(bf16[640,512]{1,0:T(8,128)(2,1)S(1)} %copy-done.2), channel_id=1, source_target_pairs={{0,1},{1,0},{2,3},{3,2},{4,5},{5,4},{6,7},{7,6},{8,9},{9,8},{10,11... | collective-permute-start | bytes 1966088 | tf_op jit(solution)/shard_map/ppermute | solution.py:39
  81.3 16.3 %collective-permute-start.26 = (bf16[640,512]{1,0:T(8,128)(2,1)S(1)}, bf16[640,512]{1,0:T(8,128)(2,1)S(1)}, u32[]{:S(2)}, u32[]{:S(2)}) collective-permute-start(bf16[640,512]{1,0:T(8,128)(2,1)S(1)} %collective-permute-done.25.refs_2_), channel_id=1, source_target_pairs={{0,1},{1,0},{2,3},{3,2},{4,5},{5,4},{6,7},{7,6},{8,9},{9,8},{10,11... | collective-permute-start | bytes 1966088 | tf_op jit(solution)/shard_map/ppermute | solution.py:39
  91.0 15.1 %collective-permute-start.15 = (bf16[640,512]{1,0:T(8,128)(2,1)S(1)}, bf16[640,512]{1,0:T(8,128)(2,1)S(1)}, u32[]{:S(2)}, u32[]{:S(2)}) collective-permute-start(bf16[640,512]{1,0:T(8,128)(2,1)S(1)} %collective-permute-done.14.refs_0_.refs_2_), channel_id=1, source_target_pairs={{0,1},{1,0},{2,3},{3,2},{4,5},{5,4},{6,7},{7,6},{8,9},{9,8},{10,11... | collective-permute-start | bytes 1966088 | tf_op jit(solution)/shard_map/ppermute | solution.py:39
  128.3 16.9 %collective-permute-start.28 = (bf16[640,512]{1,0:T(8,128)(2,1)}, bf16[640,512]{1,0:T(8,128)(2,1)S(1)}, u32[]{:S(2)}, u32[]{:S(2)}) collective-permute-start(bf16[640,512]{1,0:T(8,128)(2,1)} %fusion.1), channel_id=1, source_target_pairs={{0,2},{1,3},{2,0},{3,1},{4,6},{5,7},{6,4},{7,5},{8,10},{9,11},{10,... | collective-permute-start | bytes 1966088 | tf_op jit(solution)/shard_map/ppermute | solution.py:39
  128.8 21.0 %collective-permute-start.36 = (bf16[256,128]{1,0:T(8,128)(2,1)S(1)}, bf16[256,128]{1,0:T(8,128)(2,1)S(1)}, u32[]{:S(2)}, u32[]{:S(2)}) collective-permute-start(bf16[256,128]{1,0:T(8,128)(2,1)S(1)} %copy-done.52), channel_id=1, source_target_pairs={{0,8},{4,12},{8,0},{12,4},{16,24},{20,28},{24,16},{28,20},{1,9},{5... | collective-permute-start | bytes 196616 | tf_op jit(solution)/shard_map/ppermute | solution.py:39
  130.7 20.2 %collective-permute-start.37 = (bf16[256,128]{1,0:T(8,128)(2,1)S(1)}, bf16[256,128]{1,0:T(8,128)(2,1)}, u32[]{:S(2)}, u32[]{:S(2)}) collective-permute-start(bf16[256,128]{1,0:T(8,128)(2,1)S(1)} %copy-done.51), channel_id=1, source_target_pairs={{0,16},{4,20},{8,24},{12,28},{16,0},{20,4},{24,8},{28,12},{1,17},{... | collective-permute-start | bytes 196616 | tf_op jit(solution)/shard_map/ppermute | solution.py:39
  131.8 21.3 %collective-permute-start.38 = (bf16[256,128]{1,0:T(8,128)(2,1)S(1)}, bf16[256,128]{1,0:T(8,128)(2,1)}, u32[]{:S(2)}, u32[]{:S(2)}) collective-permute-start(bf16[256,128]{1,0:T(8,128)(2,1)S(1)} %copy-done.50), channel_id=1, source_target_pairs={{0,24},{4,28},{8,16},{12,20},{16,8},{20,12},{24,0},{28,4},{1,25},{... | collective-permute-start | bytes 196616 | tf_op jit(solution)/shard_map/ppermute | solution.py:39
  149.8 15.3 %collective-permute-start.33 = (bf16[320,128]{1,0:T(8,128)(2,1)S(1)}, bf16[320,128]{1,0:T(8,128)(2,1)S(1)}, u32[]{:S(2)}, u32[]{:S(2)}) collective-permute-start(bf16[320,128]{1,0:T(8,128)(2,1)S(1)} %get-tuple-element.108), channel_id=1, source_target_pairs={{0,20},{4,16},{8,28},{12,24},{16,4},{20,0},{24,12},{28,8},{1,21},{... | collective-permute-start | bytes 245768 | tf_op jit(solution)/shard_map/ppermute | solution.py:39
  150.9 14.2 %collective-permute-start.35 = (bf16[320,128]{1,0:T(8,128)(2,1)S(1)}, bf16[320,128]{1,0:T(8,128)(2,1)S(1)}, u32[]{:S(2)}, u32[]{:S(2)}) collective-permute-start(bf16[320,128]{1,0:T(8,128)(2,1)S(1)} %get-tuple-element.107), channel_id=1, source_target_pairs={{0,28},{4,24},{8,20},{12,16},{16,12},{20,8},{24,4},{28,0},{1,29},{... | collective-permute-start | bytes 245768 | tf_op jit(solution)/shard_map/ppermute | solution.py:39
  153.1 12.0 %collective-permute-start.30 = (bf16[320,128]{1,0:T(8,128)(2,1)S(1)}, bf16[320,128]{1,0:T(8,128)(2,1)S(1)}, u32[]{:S(2)}, u32[]{:S(2)}) collective-permute-start(bf16[320,128]{1,0:T(8,128)(2,1)S(1)} %get-tuple-element.113), channel_id=1, source_target_pairs={{0,8},{4,12},{8,0},{12,4},{16,24},{20,28},{24,16},{28,20},{1,9},{5... | collective-permute-start | bytes 245768 | tf_op jit(solution)/shard_map/ppermute | solution.py:39
  154.2 11.0 %collective-permute-start.32 = (bf16[320,128]{1,0:T(8,128)(2,1)S(1)}, bf16[320,128]{1,0:T(8,128)(2,1)S(1)}, u32[]{:S(2)}, u32[]{:S(2)}) collective-permute-start(bf16[320,128]{1,0:T(8,128)(2,1)S(1)} %get-tuple-element.112), channel_id=1, source_target_pairs={{0,16},{4,20},{8,24},{12,28},{16,0},{20,4},{24,8},{28,12},{1,17},{... | collective-permute-start | bytes 245768 | tf_op jit(solution)/shard_map/ppermute | solution.py:39
  173.8 13.5 %collective-permute-start.47 = (bf16[512,128]{1,0:T(8,128)(2,1)}, bf16[512,128]{1,0:T(8,128)(2,1)S(1)}, u32[]{:S(2)}, u32[]{:S(2)}) collective-permute-start(bf16[512,128]{1,0:T(8,128)(2,1)} %get-tuple-element.100), channel_id=1, source_target_pairs={{0,4},{4,0},{8,12},{12,8},{16,20},{20,16},{24,28},{28,24},{1,5},{5... | collective-permute-start | bytes 393224 | tf_op jit(solution)/shard_map/ppermute | solution.py:39
  187.3 11.0 %collective-permute-start.40 = (bf16[256,128]{1,0:T(8,128)(2,1)S(1)}, bf16[256,128]{1,0:T(8,128)(2,1)S(1)}, u32[]{:S(2)}, u32[]{:S(2)}) collective-permute-start(bf16[256,128]{1,0:T(8,128)(2,1)S(1)} %copy-done.55), channel_id=1, source_target_pairs={{0,16},{4,20},{8,24},{12,28},{16,0},{20,4},{24,8},{28,12},{1,17},{... | collective-permute-start | bytes 196616 | tf_op jit(solution)/shard_map/ppermute | solution.py:39
  189.0 9.2 %collective-permute-start.41 = (bf16[256,128]{1,0:T(8,128)(2,1)S(1)}, bf16[256,128]{1,0:T(8,128)(2,1)S(1)}, u32[]{:S(2)}, u32[]{:S(2)}) collective-permute-start(bf16[256,128]{1,0:T(8,128)(2,1)S(1)} %copy-done.54), channel_id=1, source_target_pairs={{0,24},{4,28},{8,16},{12,20},{16,8},{20,12},{24,0},{28,4},{1,25},{... | collective-permute-start | bytes 196616 | tf_op jit(solution)/shard_map/ppermute | solution.py:39
  193.1 11.6 %collective-permute-start.46 = (bf16[512,128]{1,0:T(8,128)(2,1)S(1)}, bf16[512,128]{1,0:T(8,128)(2,1)S(1)}, u32[]{:S(2)}, u32[]{:S(2)}) collective-permute-start(bf16[512,128]{1,0:T(8,128)(2,1)S(1)} %add_convert_fusion.2), channel_id=1, source_target_pairs={{0,16},{4,20},{8,24},{12,28},{16,0},{20,4},{24,8},{28,12},{1,17},{... | collective-permute-start | bytes 393224 | tf_op jit(solution)/shard_map/ppermute | solution.py:39
  193.7 11.0 %collective-permute-start.44 = (bf16[512,128]{1,0:T(8,128)(2,1)S(1)}, bf16[512,128]{1,0:T(8,128)(2,1)S(1)}, u32[]{:S(2)}, u32[]{:S(2)}) collective-permute-start(bf16[512,128]{1,0:T(8,128)(2,1)S(1)} %add_convert_fusion.3), channel_id=1, source_target_pairs={{0,8},{4,12},{8,0},{12,4},{16,24},{20,28},{24,16},{28,20},{1,9},{5... | collective-permute-start | bytes 393224 | tf_op jit(solution)/shard_map/ppermute | solution.py:39
  (74 other events, 625.6 us)

commit v2 on v0

v2 whole, which is shorter than its diff:
```python
import functools
import math

import jax
import jax.numpy as jnp
from jax import lax
from jax.experimental import pallas as pl
from jax.experimental.pallas import tpu as pltpu
from jax.sharding import PartitionSpec as P

HD = 128
WCH = 16
LOG2E = math.log2(math.e)
BF16 = jnp.bfloat16
F32 = jnp.float32
MIB = 1024 * 1024
VMEM_LIMIT = 14 * MIB


def on(pair, dims):
    return lax.dot_general(pair[0], pair[1], ((dims[0], dims[1]), ((), ())), preferred_element_type=F32)


def rows_by_rows(a, b):
    return on((a, b), ((1,), (1,)))


def cols_by_cols(a, b):
    return on((a, b), ((0,), (0,)))


def plain(a, b):
    return on((a, b), ((1,), (0,)))


def swap(block, axis, distance):
    if distance == 0:
        return block
    devices = range(lax.axis_size(axis))
    return lax.ppermute(block, axis, [(i, i ^ distance) for i in devices])


def local_call(body, out_shapes, arrays, scalars=(), after=(), far=(), into=(), aliases=None, scratch=(), flops=0, nbytes=0, limit=VMEM_LIMIT):
    smem = pl.BlockSpec(memory_space=pltpu.SMEM)
    vmem = pl.BlockSpec(memory_space=pltpu.VMEM)
    anywhere = pl.BlockSpec(memory_space=pl.ANY)
    hbm = pl.BlockSpec(memory_space=pltpu.HBM)
    lead = len(scalars)
    grid = (1,) if any(isinstance(x, tuple) for x in arrays) else ()
    specs = [pl.BlockSpec(x[1], lambda j, at=x[2]: at) if isinstance(x, tuple) else vmem for x in arrays] + [hbm] * len(into)
    arrays = [x[0] if isinstance(x, tuple) else x for x in arrays]

    def kernel(*refs):
        body(*refs[:lead], *refs[lead + len(after) :])

    return pl.pallas_call(
        kernel,
        out_shape=[jax.ShapeDtypeStruct(x[0], x[1]) for x in out_shapes],
        grid=grid,
        in_specs=[smem] * lead + [anywhere] * len(after) + [hbm] * len(far) + specs,
        out_specs=[pl.BlockSpec(memory_space=x[2]) if len(x) > 2 else vmem for x in out_shapes],
        scratch_shapes=list(scratch),
        input_output_aliases=aliases or {},
        compiler_params=pltpu.CompilerParams(vmem_limit_bytes=limit),
        cost_estimate=pl.CostEstimate(flops=flops, bytes_accessed=nbytes, transcendentals=0),
    )(*scalars, *after, *far, *arrays, *into)


def hold(arrays, after):
    def body(*refs):
        pass

    anywhere = pl.BlockSpec(memory_space=pl.ANY)
    lead = len(after)
    return list(
        pl.pallas_call(
            body,
            out_shape=[jax.ShapeDtypeStruct(x.shape, x.dtype) for x in arrays],
            in_specs=[anywhere] * (lead + len(arrays)),
            out_specs=[anywhere] * len(arrays),
            input_output_aliases={lead + at: at for at in range(len(arrays))},
            compiler_params=pltpu.CompilerParams(vmem_limit_bytes=MIB),
        )(*after, *arrays)
    )


def grid_call(body, steps, exp_index, ins, outs, after=(), flops=0, nbytes=0, limit=VMEM_LIMIT):
    anywhere = pl.BlockSpec(memory_space=pl.ANY)

    def kernel(place, *refs):
        body(place[0], *refs[len(after) :])

    return pl.pallas_call(
        kernel,
        out_shape=[jax.ShapeDtypeStruct(shape, dtype) for shape, dtype, _, _ in outs],
        grid_spec=pltpu.PrefetchScalarGridSpec(
            num_scalar_prefetch=1,
            grid=(steps,),
            in_specs=[anywhere] * len(after) + [pl.BlockSpec(block, index) for _, block, index in ins],
            out_specs=[pl.BlockSpec(block, index) for _, _, block, index in outs],
        ),
        compiler_params=pltpu.CompilerParams(vmem_limit_bytes=limit),
        cost_estimate=pl.CostEstimate(flops=flops, bytes_accessed=nbytes, transcendentals=0),
    )(exp_index, *after, *[array for array, _, _ in ins])


def attention_limit(block_len, total):
    return min(60 * MIB, 4 * MIB + 6 * block_len * total * 4)


def id_rows_of(ids):
    return [ids[j : j + 1, at : at + 128].astype(F32) for j in range(2) for at in range(0, ids.shape[1], 128)]


def relative_slots(id_rows, place, experts, capacity, stride):
    flat = jnp.concatenate(id_rows, axis=1).astype(jnp.int32)
    entries = flat.shape[1]
    lanes = max(experts, 8)
    one_hot = lax.broadcasted_iota(jnp.int32, (lanes, entries), 0) == flat
    one_hot = one_hot.astype(F32)
    earlier = lax.broadcasted_iota(jnp.int32, (entries, entries), 0) < lax.broadcasted_iota(
        jnp.int32, (entries, entries), 1
    )
    before = plain(one_hot.astype(BF16), earlier.astype(F32).astype(BF16))
    position = jnp.sum(before * one_hot, axis=0, keepdims=True).astype(jnp.int32)
    return jnp.where(position < capacity, (flat ^ place) * stride + position, -1)


def pack_body(sizes, q, k, v, og, ids, gates, *refs):
    G, R, BL = sizes[:3]
    outs, sent, place, held, sems = refs[:G], refs[G : G + R], *refs[G + R :]
    g = lax.axis_index("seq") // R
    place[0] = lax.axis_index("exp")

    moves = [pltpu.make_async_copy(source, held.at[at], sems.at[at]) for at, source in enumerate((k, v, q, og))]
    for move in moves:
        move.start()
    rows = id_rows_of(ids)
    rows.append(jnp.zeros((16 - len(rows), 128), F32))
    rows = jnp.concatenate(rows, axis=0).astype(BF16)
    for d in range(G):
        outs[d][3 * BL : 3 * BL + 16] = rows
    for at, move in enumerate(moves[:3]):
        move.wait()
        for d in range(G):
            cols = pl.ds(pl.multiple_of((g ^ d) * HD, HD), HD)
            outs[d][at * BL : (at + 1) * BL] = held[at, :, cols]
    moves[3].wait()
    route_grads(sizes, held[3], gates, ids, sent)


def upper_body(sizes, og, *refs):
    G, R, BL = sizes
    outs, sems = refs[:G], refs[G]
    g = lax.axis_index("seq") // R
    moves = []
    for d in range(G):
        cols = pl.ds(pl.multiple_of((g ^ d) * HD, HD), HD)
        moves.append(pltpu.make_async_copy(og.at[:, cols], outs[d], sems.at[d]))
    for move in moves:
        move.start()
    for move in moves:
        move.wait()


def route_grads(sizes, block, gates, ids, outs):
    G, R, BL, cap, stride = sizes
    n = G * R
    slots = relative_slots(id_rows_of(ids), lax.axis_index("seq"), n, cap, stride)
    routing = lax.broadcasted_iota(jnp.int32, (n * stride, 2 * BL), 0) == slots
    diagonal = lax.broadcasted_iota(jnp.int32, (BL, BL), 0) == lax.broadcasted_iota(jnp.int32, (BL, BL), 1)
    block = block.astype(F32)
    scaled = []
    for j in range(2):
        gate = jnp.sum(jnp.where(diagonal, gates[j : j + 1], 0.0), axis=1, keepdims=True)
        scaled.append((gate * block).astype(BF16))
    routed = plain(routing.astype(F32).astype(BF16), jnp.concatenate(scaled, axis=0)).astype(BF16)
    for dg in range(G):
        for dr in range(R):
            d = dg * R + dr
            outs[dr][dg * stride : (dg + 1) * stride] = routed[d * stride : (d + 1) * stride]


def routing_body(sizes, *refs):
    G, R, BL, cap, stride = sizes
    n = G * R
    s = lax.axis_index("seq")
    own, out = refs[:G], refs[G]
    for d in range(G):
        rows = own[d][...].astype(F32)
        slots = relative_slots([rows[k : k + 1] for k in range(2 * BL // 128)], s, n, cap, stride)
        slot_rows = lax.broadcasted_iota(jnp.int32, (n * stride, BL), 0)
        chosen = (slot_rows == slots[:, :BL]) | (slot_rows == slots[:, BL:])
        out[pl.ds((s // R) ^ d, 1)] = chosen.astype(F32).astype(BF16)[None]


def pair_groups(G):
    return [members for members in ([0], [1], list(range(2, G))) if members and members[-1] < G]


def forward_body(sizes, slopes, *refs):
    G, R, BL, cap, stride = sizes
    n = G * R
    total = n * BL
    s = lax.axis_index("seq")
    g, r = s // R, s % R
    own, refs = refs[:G], refs[G:]
    groups = pair_groups(G)
    others, refs = refs[: len(groups) * (R - 1)], refs[len(groups) * (R - 1) :]
    far, refs = refs[: G + 4], refs[G + 4 :]
    attn_out, refs = refs[0], refs[1:]
    near, sems = refs[: G + 4], refs[G + 4]
    probs = near[:G]
    attn, keys, values, queries = near[G:]

    def kept(at):
        return pltpu.make_async_copy(near[at], far[at], sems.at[at])

    for d in range(G):
        i = g ^ d
        queries[pl.ds(pl.multiple_of(i * BL, BL), BL)] = own[d][2 * BL : 3 * BL]
        for dr in range(R):
            piece, at = own[d], 0
            if dr:
                group = next(k for k, members in enumerate(groups) if d in members)
                piece = others[(dr - 1) * len(groups) + group]
                at = groups[group].index(d) * 2 * BL
            rows = pl.ds(pl.multiple_of((i * R + (r ^ dr)) * BL, BL), BL)
            keys[rows] = piece[at : at + BL]
            values[rows] = piece[at + BL : at + 2 * BL]
    for at in range(G + 1, G + 4):
        kept(at).start()
    slope = slopes[g]
    span = R * BL
    for i in range(G):
        N = (i + 1) * span
        scores = rows_by_rows(queries[i * BL : (i + 1) * BL], keys[0:N])
        col = lax.broadcasted_iota(jnp.int32, (1, N), 1)
        bias = (col - N).astype(F32) * (slope * LOG2E)
        scores = scores * (HD**-0.5 * LOG2E) + bias
        if total > WCH * BL:
            distance = (
                lax.broadcasted_iota(jnp.int32, (BL, N), 0) + (i * R + r) * BL - lax.broadcasted_iota(jnp.int32, (BL, N), 1)
            )
            scores = jnp.where((distance >= 0) & (distance < WCH * BL), scores, -jnp.inf)
        else:
            ahead = lax.broadcasted_iota(jnp.int32, (BL, span), 1) - lax.broadcasted_iota(jnp.int32, (BL, span), 0)
            last = jnp.where(ahead <= r * BL, scores[:, N - span :], -jnp.inf)
            scores = last if i == 0 else jnp.concatenate([scores[:, : N - span], last], axis=1)
        top = jnp.max(scores, axis=1, keepdims=True)
        grown = jnp.exp2(scores - top)
        norm = jnp.sum(grown, axis=1, keepdims=True)
        weights = (grown * (1.0 / norm)).astype(BF16)
        probs[i][...] = weights
        kept(i).start()
        out = plain(weights, values[0:N]).astype(BF16)
        attn[i * BL : (i + 1) * BL] = out
        attn_out[i * BL : (i + 1) * BL] = out
    kept(G).start()
    for at in range(G + 4):
        kept(at).wait()


def dispatch_body(sizes, attn, routing, *sent):
    G, R, BL, cap, stride = sizes
    for i in range(G):
        routed = plain(routing[i], attn[i * BL : (i + 1) * BL]).astype(BF16)
        for dg in range(G):
            for dr in range(R):
                d = dg * R + dr
                at = (dr * G + i) * stride
                sent[dg][at : at + stride] = routed[d * stride : (d + 1) * stride]


def value_body(sizes, *refs):
    G, R, BL, cap, stride = sizes
    n = G * R
    s = lax.axis_index("seq")
    g, r = s // R, s % R
    back, refs = refs[:G], refs[G:]
    upper, refs = refs[:G], refs[G:]
    probs, refs = refs[:G], refs[G:]
    routing, attn_grad, refs = refs[0], refs[1], refs[2:]
    outs, total, upper_rows = refs[:R], refs[R], refs[R + 1]
    for d in range(G):
        upper_rows[pl.ds(pl.multiple_of((g ^ d) * BL, BL), BL)] = upper[d][...]
    for i in reversed(range(G)):
        N = (i + 1) * R * BL
        mine = slice(i * BL, (i + 1) * BL)
        starts = [(dr * G + i) * stride for dr in range(R)]
        rows = jnp.concatenate([back[dg][at : at + stride] for dg in range(G) for at in starts], axis=0)
        picked = cols_by_cols(routing[i], rows)
        grad = (upper_rows[mine].astype(F32) + picked).astype(BF16)
        attn_grad[mine] = grad
        part = cols_by_cols(probs[i][...], grad)
        if i == G - 1:
            total[...] = part
        else:
            total[0:N] += part
    spread(sizes, total, outs)


def spread(sizes, total, outs):
    G, R, BL = sizes[:3]
    s = lax.axis_index("seq")
    g, r = s // R, s % R
    for d in range(G):
        for dr in range(R):
            rows = pl.ds(pl.multiple_of(((g ^ d) * R + (r ^ dr)) * BL, BL), BL)
            outs[dr][d * BL : (d + 1) * BL] = total[rows].astype(BF16)


def score_body(sizes, *refs):
    G, R, BL = sizes[:3]
    s = lax.axis_index("seq")
    g = s // R
    probs, refs = refs[:G], refs[G:]
    attn_grad, attn, keys, values, queries = refs[:5]
    refs = refs[5:]
    query_out, refs = refs[:G], refs[G:]
    outs, query_rows, total = refs[:R], refs[R], refs[R + 1]
    scale = HD**-0.5
    for i in reversed(range(G)):
        N = (i + 1) * R * BL
        mine = slice(i * BL, (i + 1) * BL)
        grad = attn_grad[mine]
        delta = jnp.sum(grad.astype(F32) * attn[mine].astype(F32), axis=1, keepdims=True)
        dprob = rows_by_rows(grad, values[0:N])
        dscore = (probs[i][...].astype(F32) * (dprob - delta)).astype(BF16)
        query_rows[mine] = (plain(dscore, keys[0:N]) * scale).astype(BF16)
        part = cols_by_cols(dscore, queries[mine]) * scale
        if i == G - 1:
            total[...] = part
        else:
            total[0:N] += part
    for d in range(G):
        query_out[d][...] = query_rows[pl.ds(pl.multiple_of((g ^ d) * BL, BL), BL)]
    spread(sizes, total, outs)


def unpack_body(sizes, *refs):
    G, R, BL = sizes
    g = lax.axis_index("seq") // R
    pieces, outs = refs[: 3 * G], refs[3 * G :]
    for at in range(3):
        for d in range(G):
            cols = pl.ds(pl.multiple_of((g ^ d) * HD, HD), HD)
            outs[at][:, cols] = pieces[at * G + d][...]


def turn_tokens_body(sizes, *refs):
    G, R, count = sizes
    g = lax.axis_index("seq") // R
    for dg in range(G):
        cols = pl.ds(pl.multiple_of((g ^ dg) * HD, HD), HD)
        for dr in range(R):
            refs[G + dr][:, cols] = refs[dg][dr * count : (dr + 1) * count]


def column_body(sizes, *refs):
    G, R, stride = sizes
    for dg in range(G):
        for dr in range(R):
            refs[R + dg][dr * stride : (dr + 1) * stride] = refs[dr][dg * stride : (dg + 1) * stride]


def turn_grads_body(sizes, *refs):
    G, R, stride = sizes
    g = lax.axis_index("seq") // R
    for dg in range(G):
        for dr in range(R):
            at = pl.ds(pl.multiple_of((dr * G + (g ^ dg)) * stride, 16), stride)
            refs[-1][at] = refs[dg][dr * stride : (dr + 1) * stride]


def turn_back_body(sizes, near, arrived, *refs):
    G, R, count = sizes
    g = lax.axis_index("seq") // R
    moved, outs = refs[: R - 1], refs[R - 1 :]
    for dg in range(G):
        cols = pl.ds(pl.multiple_of((g ^ dg) * HD, HD), HD)
        outs[dg][0:count] = (near[0:count, cols] + arrived[0:count, cols].astype(F32)).astype(BF16)
        for dr in range(1, R):
            outs[dg][dr * count : (dr + 1) * count] = moved[dr - 1][:, cols]


def keep_moves(parts, first, shards, full, sems):
    place = lax.axis_index("exp")
    rows, width = shards[0].shape
    moves = []
    for at, shard in enumerate(shards):
        k, h = first + at // parts, at % parts
        cols = pl.ds(pl.multiple_of((place ^ k) * width, 128), width)
        moves.append(pltpu.make_async_copy(shard, full.at[pl.ds(h * rows, rows), cols], sems.at[at]))
    return moves


def through_body(parts, weight, *refs):
    shards, out, full, held, sems, own_sems = refs[:-5], *refs[-5:]
    place = lax.axis_index("exp")
    rows, width = shards[0].shape
    steps = sems.shape[0]
    kept = keep_moves(parts, 0, shards, full, own_sems)
    tall = weight.shape[0] // steps

    def fetch(c):
        mine = pl.ds(c * tall, tall)
        return pltpu.make_async_copy(weight.at[mine], held.at[mine], sems.at[c])

    for c in range(steps):
        fetch(c).start()
    for move in kept:
        move.start()
    for c in range(steps):
        fetch(c).wait()
        for h in range(parts):
            total = None
            for k in range(len(shards) // parts):
                cols = pl.ds(pl.multiple_of((place ^ k) * width, 128), width)
                part = rows_by_rows(shards[k * parts + h][...], held[c * tall : (c + 1) * tall, cols])
                total = part if total is None else total + part
            out[h * rows : (h + 1) * rows, c * tall : (c + 1) * tall] = total
    for move in kept:
        move.wait()


def pre_body(parts, first, weight, *refs):
    held, sems, own_sems = refs[-3:]
    if first:
        shards, begun, through, full, hidden, hidden_grad = refs[:-9], *refs[-9:-7], *refs[-6:-3]
    else:
        shards, out, full = refs[:-5], *refs[-5:-3]
    kept = keep_moves(parts, first, shards, full, own_sems)
    place = lax.axis_index("exp")
    rows, width = shards[0].shape
    count, steps = sems.shape
    wide = weight.shape[1] // steps

    def fetch(k, c):
        source = weight.at[pl.ds(pl.multiple_of((place ^ (first + k)) * width, 128), width), pl.ds(c * wide, wide)]
        return pltpu.make_async_copy(source, held.at[c, pl.ds(k * width, width)], sems.at[k, c])

    for c in range(steps):
        for k in range(count):
            fetch(k, c).start()
    for move in kept:
        move.start()
    for c in range(steps):
        cols = slice(c * wide, (c + 1) * wide)
        for k in range(count):
            fetch(k, c).wait()
        for h in range(parts):
            mine = slice(h * rows, (h + 1) * rows)
            total = begun[mine, cols] if first else None
            for k in range(count):
                part = plain(shards[k * parts + h][...], held[c, k * width : (k + 1) * width])
                total = part if total is None else total + part
            if not first:
                out[mine, cols] = total
            else:
                logistic = 1.0 / (1.0 + jnp.exp(-total))
                hidden[mine, cols] = (total * logistic).astype(BF16)
                grad = through[mine, cols] * logistic * (1.0 + total * (1.0 - logistic))
                hidden_grad[mine, cols] = grad.astype(BF16)
    for move in kept:
        move.wait()


def back_body(added, place, grad, weight, *refs):
    part = rows_by_rows(grad[...], weight[...])
    if added:
        part = part + refs[0][...].astype(F32)
    outs = refs[added:]
    rows = part.shape[0] // len(outs)
    for h, out in enumerate(outs):
        out[...] = part[h * rows : (h + 1) * rows].astype(out.dtype)


def weight_grad_body(place, left, right, out, mark):
    mark[...] = jnp.zeros_like(mark)
    out[...] = cols_by_cols(left[...], right[...]).astype(BF16)


def gather_exp(block, size):
    distance = size // 2
    by_place = {0: block}
    while distance:
        for place in list(by_place):
            by_place[place ^ distance] = swap(by_place[place], "exp", distance)
        distance //= 2
    return [by_place[k] for k in range(size)]


def per_device(
    queries,
    key_rows,
    value_rows,
    out_grad,
    expert_ids,
    gate_values,
    alibi_slope,
    expert_in,
    expert_out,
):
    BL, features = queries.shape
    G = features // HD
    n = lax.axis_size("seq")
    E = lax.axis_size("exp")
    R = n // G
    cap = 5 * BL // (2 * n)
    stride = -(-cap // 16) * 16
    rows = n * stride
    FFL = expert_in.shape[2]
    L = n * BL
    parts = 2
    each = R // parts
    tall = rows // parts
    half = E // 2
    sizes = (G, R, BL, cap, stride)
    limit = attention_limit(BL, L)
    weight_in = expert_in[0]
    weight_out = expert_out[0]

    ids, gates = expert_ids.T, gate_values.T
    arrays_of = lambda arrays: [
        arrays[h * each] if each == 1 else jnp.concatenate(arrays[h * each : (h + 1) * each], axis=0) for h in range(parts)
    ]

    made = local_call(
        functools.partial(pack_body, sizes),
        [((3 * BL + 16, HD), BF16)] * G + [((G * stride, features), BF16)] * R + [((1,), jnp.int32, pltpu.SMEM)],
        [ids, gates],
        far=[queries, key_rows, value_rows, out_grad],
        scratch=[pltpu.VMEM((4, BL, features), BF16), pltpu.SemaphoreType.DMA((4,))],
        limit=57 * MIB,
        nbytes=6 * BL * features * 2,
    )
    place = made[G + R]
    grad_sent = [swap(made[G + dr], "seq", dr) for dr in range(R)]
    own = [swap(made[d], "seq", d * R) for d in range(G)]
    pairs = [
        own[members[0]][: 2 * BL] if len(members) == 1 else jnp.concatenate([own[d][: 2 * BL] for d in members], axis=0)
        for members in pair_groups(G)
    ]
    others = [swap(piece, "seq", dr) for dr in range(1, R) for piece in pairs]
    block = ((16, HD), (3 * BL // 16, 0))
    routing = local_call(
        functools.partial(routing_body, sizes),
        [((G, rows, BL), BF16)],
        [(own[d], *block) for d in range(G)],
        flops=2 * G * 8 * 4 * BL * BL,
        nbytes=rows * BL * G * 2,
    )[0]

    grad_pieces = local_call(
        functools.partial(column_body, (G, R, stride)),
        [((R * stride, features), BF16)] * G,
        grad_sent,
        after=own[1:],
        nbytes=rows * features * 4,
    )
    kept = [((BL, (i + 1) * R * BL), BF16, pltpu.HBM) for i in range(G)]
    kept += [(shape, BF16, pltpu.HBM) for shape in ((G * BL, HD), (L, HD), (L, HD), (G * BL, HD))]
    shapes = kept + [((G * BL, HD), BF16)]
    made = local_call(
        functools.partial(forward_body, sizes),
        shapes,
        own + others,
        scalars=[alibi_slope],
        scratch=[pltpu.VMEM(x[0], x[1]) for x in kept] + [pltpu.SemaphoreType.DMA((G + 4,))],
        flops=0,
        nbytes=0,
        limit=limit,
    )
    probs = list(made[:G])
    attn, keys, values, query_rows = made[G : G + 4]
    grads = local_call(
        functools.partial(turn_grads_body, (G, R, stride)),
        [((rows, features), BF16)],
        [swap(grad_pieces[dg], "seq", dg * R) for dg in range(G)],
        after=[routing, made[G + 4]],
        nbytes=rows * features * 4,
    )[0]
    grads_far = swap(grads, "exp", half)
    token_sent = local_call(
        functools.partial(dispatch_body, sizes),
        [((R * G * stride, HD), BF16)] * G,
        [made[G + 4], routing],
        flops=2 * rows * BL * HD * G,
        nbytes=2 * MIB,
    )
    token_pieces = [swap(token_sent[dg], "seq", dg * R) for dg in range(G)]
    grad_shards = gather_exp(grads, half) + gather_exp(hold([grads_far], token_pieces[1:] or token_pieces)[0], half)
    width = min(256, FFL)
    steps = FFL // width
    whole = lambda array: (array, array.shape, lambda j, p: (0, 0))
    column_of = lambda array: (array, (array.shape[0], width), lambda j, p: (0, j))
    work = 2 * rows * FFL * features
    through, full_grads = local_call(
        functools.partial(through_body, 1),
        [((rows, FFL), F32), ((rows, E * features), BF16, pltpu.HBM)],
        grad_shards,
        far=[weight_out],
        scratch=[
            pltpu.VMEM((FFL, E * features), BF16),
            pltpu.SemaphoreType.DMA((steps,)),
            pltpu.SemaphoreType.DMA((E,)),
        ],
        flops=work * E,
        nbytes=10 * MIB,
    )

    tokens = local_call(
        functools.partial(turn_tokens_body, (G, R, G * stride)),
        [((G * stride, features), BF16)] * R,
        token_pieces,
        after=[grads_far],
        nbytes=rows * features * 4,
    )
    upper = local_call(
        functools.partial(upper_body, (G, R, BL)),
        [((BL, HD), BF16)] * G,
        [],
        after=tokens[:1],
        far=[out_grad],
        scratch=[pltpu.SemaphoreType.DMA((G,))],
        nbytes=2 * BL * features * 2,
    )
    upper = [swap(upper[d], "seq", d * R) for d in range(G)]

    token_parts = arrays_of([swap(tokens[dr], "seq", dr) for dr in range(R)])
    if G > 1:
        token_parts[1:] = hold(token_parts[1:], upper[1:] + [through])
    far_parts = [swap(part, "exp", half) for part in token_parts]
    near_shards = [gather_exp(part, half) for part in token_parts]
    near_shards = [near_shards[h][k] for k in range(half) for h in range(parts)]
    streamed = [
        pltpu.VMEM((steps, half * features, width), BF16),
        pltpu.SemaphoreType.DMA((half, steps)),
        pltpu.SemaphoreType.DMA((half * parts,)),
    ]
    begun, full_tokens = local_call(
        functools.partial(pre_body, parts, 0),
        [((rows, FFL), F32), ((rows, E * features), BF16, pltpu.HBM)],
        near_shards,
        far=[weight_in],
        scratch=streamed,
        flops=work * half,
        nbytes=8 * MIB,
    )
    far_parts[1:] = hold(far_parts[1:], [begun])
    far_shards = [gather_exp(part, half) for part in far_parts]
    far_shards = [far_shards[h][k] for k in range(half) for h in range(parts)]
    full_tokens, hidden, hidden_grad = local_call(
        functools.partial(pre_body, parts, half),
        [((rows, E * features), BF16, pltpu.HBM)] + [((rows, FFL), BF16)] * 2,
        far_shards + [begun, through],
        into=[full_tokens],
        far=[weight_in],
        aliases={half * parts + 3: 0},
        scratch=streamed,
        flops=work * half,
        nbytes=8 * MIB,
    )

    def back_part(k, moved, count, dtype):
        piece = min(256, features)
        per = features // piece
        added = [] if moved is None else [(moved, (rows, piece), lambda j, p: (0, j))]
        return grid_call(
            functools.partial(back_body, len(added)),
            per,
            place,
            [whole(hidden_grad), (weight_in, (piece, FFL), lambda j, p: ((p[0] ^ k) * per + j, 0))] + added,
            [((rows // count, features), dtype, (rows // count, piece), lambda j, p: (0, j))] * count,
            flops=work,
            nbytes=3 * MIB,
        )

    def summed(first, dtype):
        moved = [swap(back_part(k + 1, None, 1, BF16)[0], "exp", 1) for k in range(first, first + half, 2)]
        return [back_part(first + 2 * at, piece, parts, dtype) for at, piece in enumerate(moved)]

    far = summed(half, BF16)
    arrived = [[swap(piece[h], "exp", half) for h in range(parts)] for piece in far]
    near = summed(0, F32)
    distance = half // 2
    while len(near) > 1:
        count = len(near) // 2
        total = [[near[k][h] + arrived[k][h].astype(F32) for h in range(parts)] for k in range(2 * count)]
        arrived = [[swap(total[count + k][h].astype(BF16), "exp", distance) for h in range(parts)] for k in range(count)]
        near = total[:count]
        distance //= 2

    mark_out = ((8, 128), F32, (8, 128), lambda j, p: (0, 0))
    out_weight_grad, out_mark = grid_call(
        weight_grad_body,
        steps,
        place,
        [column_of(hidden), whole(full_grads)],
        [((FFL, features * E), BF16, (width, features * E), lambda j, p: (j, 0)), mark_out],
        flops=work * E,
        nbytes=10 * MIB,
    )
    count = G * stride
    away = []
    for dr in range(1, R):
        mine = slice((dr % each) * count, (dr % each + 1) * count)
        total = near[0][dr // each][mine] + arrived[0][dr // each][mine].astype(F32)
        away.append(swap(total.astype(BF16), "seq", dr))
    back_sent = local_call(
        functools.partial(turn_back_body, (G, R, count)),
        [((R * count, HD), BF16)] * G,
        [near[0][0], arrived[0][0]] + away,
        after=[out_mark],
        nbytes=tall * features * 8,
    )
    returned = [swap(back_sent[dg], "seq", dg * R) for dg in range(G)]
    in_weight_grad, in_mark = grid_call(
        weight_grad_body,
        E,
        place,
        [(full_tokens, (rows, features), lambda j, p: (0, j)), whole(hidden_grad)],
        [((features * E, FFL), BF16, (features, FFL), lambda j, p: (j, 0)), mark_out],
        flops=work * E,
        nbytes=10 * MIB,
    )

    made = local_call(
        functools.partial(value_body, sizes),
        [((G * BL, HD), BF16)] * (1 + R),
        returned + upper + probs + [routing],
        after=[in_mark],
        scratch=[pltpu.VMEM((L, HD), F32), pltpu.VMEM((G * BL, HD), BF16)],
        flops=2 * G * BL * L * HD,
        nbytes=6 * MIB,
        limit=limit,
    )
    attn_grad, value_parts = made[0], made[1:]
    made = local_call(
        functools.partial(score_body, sizes),
        [((BL, HD), BF16)] * G + [((G * BL, HD), BF16)] * R,
        probs + [attn_grad, attn, keys, values, query_rows],
        scratch=[pltpu.VMEM((G * BL, HD), BF16), pltpu.VMEM((L, HD), F32)],
        flops=6 * G * BL * L * HD,
        nbytes=6 * MIB,
        limit=limit,
    )
    query_pieces, key_parts = made[:G], made[G:]

    def home(pair_parts):
        moved = [swap(pair_parts[dr], "seq", dr) for dr in range(1, R)]
        pieces = []
        for d in range(G):
            mine = slice(d * BL, (d + 1) * BL)
            total = pair_parts[0][mine].astype(F32)
            for piece in moved:
                total = total + piece[mine].astype(F32)
            pieces.append(swap(total.astype(BF16), "seq", d * R))
        return pieces

    value_home = home(value_parts)
    query_home = [swap(query_pieces[d], "seq", d * R) for d in range(G)]
    key_home = home(key_parts)
    query_grad, key_grad, value_grad = local_call(
        functools.partial(unpack_body, (G, R, BL)),
        [((BL, features), BF16)] * 3,
        query_home + key_home + value_home,
        nbytes=6 * BL * features * 2,
    )
    return query_grad, key_grad, value_grad, in_weight_grad[None], out_weight_grad[None]


def solution(mesh):
    return jax.shard_map(
        per_device,
        mesh=mesh,
        in_specs=(
            P("seq", "exp"),
            P("seq", "exp"),
            P("seq", "exp"),
            P("seq", "exp"),
            P("seq", None),
            P("seq", None),
            P("exp"),
            P("seq", None, "exp"),
            P("seq", "exp", None),
        ),
        out_specs=(
            P("seq", "exp"),
            P("seq", "exp"),
            P("seq", "exp"),
            P("seq", None, "exp"),
            P("seq", "exp", None),
        ),
        check_vma=False,
    )
```

time: 824 us -> 168 us (0.20); the launches traced: 811 us -> 168 us
  waiting for transfers between devices: 316 us -> 55.8 us
  starting transfers between devices: 194 us -> 61.7 us
  local copies, waits for them, and re-layouts: 107 us -> 1.94 us
  matrix products: 84.8 us -> 0 us
  other arithmetic: 55.1 us -> 0.25 us
  Pallas kernels: 0 us -> 47.4 us
  blocking collectives: 38.7 us -> 0 us
  between operations: 14.5 us -> 0.98 us
    ppermute x64 -> x45, waiting for transfers between devices: 248 us -> 55.8 us  [swap(): return lax.ppermute(block, axis, [(i, i ^ distance) for i in devices])]
    ppermute x64 -> x45, starting transfers between devices: 188 us -> 61.7 us  [swap(): return lax.ppermute(block, axis, [(i, i ^ distance) for i in devices])]
    dot_general x14 -> x0, matrix products: 84.8 us -> none  [the longest x1 12.7 us: per_device(): jnp.einsum('hij,ihd->jhd', weights, grad_heads, preferred_element_type=jn...]
    reshape x6 -> x0, local copies, waits for them, and re-layouts: 48.8 us -> none  [the longest x2 17 us: per_device(): key_block = key_stack.reshape(stretches * block_len, head_count, HD)]
    pallas_call x0 -> x24, Pallas kernels: none -> 47.4 us  [the longest x15 28.4 us: local_call(): pl.pallas_call(kernel, out_shape=[jax.ShapeDtypeStruct(x[0], x[1]) for x...]
    all_to_all x2 -> x0, blocking collectives: 38.7 us -> none  [the longest x1 23.5 us: per_device(): lax.all_to_all(send_tokens, 'seq', split_axis=0, concat_axis=0, tiled=True)]
    add x35 -> x0, other arithmetic: 35.6 us -> none  [the longest x16 17.8 us: relay_grads(): value_acc + lax.dynamic_index_in_dim(value_parts, index, 0, keepdims=False)]
    reduce_scatter x1 -> x0, waiting for transfers between devices: 34.8 us -> none  [per_device(): lax.psum_scatter(lax.dot_general(weight_in, hidden_grad, (((1,), (1,)), (...]
  transfers between devices with their start and end apart: 68 -> 45, of which waited for: 66 -> 17; matrix products, arithmetic and copies ran while one was open for 5% -> 1% of each run, Pallas kernels for 0% -> 20%
where the time goes in v2:
time: 168 us
  starting transfers between devices  61.7 us (37%)
  waiting for transfers between devices  55.8 us (33%)
  Pallas kernels  47.4 us (28%)
  local copies, waits for them, and re-layouts  1.94 us (1%)
    ppermute x45, starting transfers between devices, swap(): return lax.ppermute(block, axis, [(i, i ^ distance) for i in devices])  61.7 us
    ppermute x45, waiting for transfers between devices, swap(): return lax.ppermute(block, axis, [(i, i ^ distance) for i in devices])  55.8 us
    pallas_call x15, Pallas kernels, local_call(): pl.pallas_call(kernel, out_shape=[jax.ShapeDtypeStruct(x[0], x[1]) for x...  28.4 us
    pallas_call x6, Pallas kernels, grid_call(): pl.pallas_call(kernel, out_shape=[jax.ShapeDtypeStruct(shape, dtype) for...  19 us
  transfers between devices with their start and end apart: 45, of which 17 were waited for; matrix products, arithmetic and copies ran while one was open for 1% of the time, Pallas kernels for 20%

profile of v2, /device:TPU:0, one launch (start us, length us, event | category | flops | bytes accessed | tf_op | source)
XLA Modules:
  0.0 168.1 jit_solution(11680375204128317506)
XLA Ops:
  0.6 3.4 %shard_map.128 = (bf16[784,128]{1,0:T(8,128)(2,1)}, bf16[784,128]{1,0:T(8,128)(2,1)}, bf16[784,128]{1,0:T(8,128)(2,1)}, bf16[784,128]{1,0:T(8,128)(2,1)}, bf16[3...) custom-call(bf16[256,512]{1,0:T(8,128)(2,1)} %refs_0_.2, bf16[256,512]{1,0:T(8,128)(2,1)} %refs_1_.2, ...), custom_call_target="tpu_custom_call" | custom-call | bytes 1572864 | tf_op jit(solution)/shard_map/pallas_call | solution.py:56
  4.1 4.1 %collective-permute-start.1 = (bf16[784,128]{1,0:T(8,128)(2,1)}, bf16[784,128]{1,0:T(8,128)(2,1)S(1)}, u32[]{:S(2)}, u32[]{:S(2)}) collective-permute-start(bf16[784,128]{1,0:T(8,128)(2,1)} %get-tuple-element.68), channel_id=1, source_target_pairs={{0,16},{4,20},{8,24},{12,28},{16,0},{20,4},{24,8},{28,12},{1,17},{... | collective-permute-start | bytes 602120 | tf_op jit(solution)/shard_map/ppermute | solution.py:40
  12.8 10.1 %collective-permute-done.1.refs_3_.refs_2_.refs_1_ = bf16[784,128]{1,0:T(8,128)(2,1)S(1)} collective-permute-done((bf16[784,128]{1,0:T(8,128)(2,1)}, bf16[784,128]{1,0:T(8,128)(2,1)S(1)}, u32[]{:S(2)}, u32[]{:S(2)}) %collective-permute-start.1) | collective-permute-done | bytes 200736 | tf_op jit(solution)/shard_map/ppermute | solution.py:40
  22.9 1.9 %collective-permute-start.5 = (bf16[1024,128]{1,0:T(8,128)(2,1)S(1)}, bf16[1024,128]{1,0:T(8,128)(2,1)S(1)}, u32[]{:S(2)}, u32[]{:S(2)}) collective-permute-start(bf16[1024,128]{1,0:T(8,128)(2,1)S(1)} %pad_maximum_fusion), channel_id=1, source_target_pairs={{0,4},{4,0},{8,12},{12,8},{16,20},{20,16},{24,28},{28,24},{1,5},{5... | collective-permute-start | bytes 786440 | tf_op jit(solution)/shard_map/ppermute | solution.py:40
  26.5 3.3 %collective-permute-start.7 = (bf16[160,512]{1,0:T(8,128)(2,1)S(1)}, bf16[160,512]{1,0:T(8,128)(2,1)S(1)}, u32[]{:S(2)}, u32[]{:S(2)}) collective-permute-start(bf16[160,512]{1,0:T(8,128)(2,1)S(1)} %get-tuple-element.79), channel_id=1, source_target_pairs={{0,8},{4,12},{8,0},{12,4},{16,24},{20,28},{24,16},{28,20},{1,9},{5... | collective-permute-start | bytes 491528 | tf_op jit(solution)/shard_map/ppermute | solution.py:40
  29.9 1.9 %collective-permute-start.8 = (bf16[160,512]{1,0:T(8,128)(2,1)S(1)}, bf16[160,512]{1,0:T(8,128)(2,1)S(1)}, u32[]{:S(2)}, u32[]{:S(2)}) collective-permute-start(bf16[160,512]{1,0:T(8,128)(2,1)S(1)} %get-tuple-element.80), channel_id=1, source_target_pairs={{0,16},{4,20},{8,24},{12,28},{16,0},{20,4},{24,8},{28,12},{1,17},{... | collective-permute-start | bytes 491528 | tf_op jit(solution)/shard_map/ppermute | solution.py:40
  34.8 3.4 %collective-permute-done.4.refs_6_ = bf16[512,128]{1,0:T(8,128)(2,1)S(1)} collective-permute-done((bf16[512,128]{1,0:T(8,128)(2,1)S(1)}, bf16[512,128]{1,0:T(8,128)(2,1)S(1)}, u32[]{:S(2)}, u32[]{:S(2)}) %collective-permute-start.4) | collective-permute-done | bytes 131104 | tf_op jit(solution)/shard_map/ppermute | solution.py:40
  38.2 4.7 %shard_map.129 = (bf16[256,512]{1,0:T(8,128)(2,1)S(1)}, bf16[256,1024]{1,0:T(8,128)(2,1)S(1)}, bf16[256,1536]{1,0:T(8,128)(2,1)S(1)}, bf16[256,2048]{1,0:T(8,128...) custom-call(f32[4]{0:T(128)S(1)} %copy-done.4, ...), custom_call_target="tpu_custom_call" | custom-call | tf_op jit(solution)/shard_map/pallas_call | solution.py:56
  42.9 1.9 %collective-permute-done.8.refs_4_ = bf16[160,512]{1,0:T(8,128)(2,1)S(1)} collective-permute-done((bf16[160,512]{1,0:T(8,128)(2,1)S(1)}, bf16[160,512]{1,0:T(8,128)(2,1)S(1)}, u32[]{:S(2)}, u32[]{:S(2)}) %collective-permute-start.8) | collective-permute-done | bytes 163872 | tf_op jit(solution)/shard_map/ppermute | solution.py:40
  47.0 2.7 %collective-permute-start.11 = (bf16[640,128]{1,0:T(8,128)(2,1)S(1)}, bf16[640,128]{1,0:T(8,128)(2,1)S(1)}, u32[]{:S(2)}, u32[]{:S(2)}) collective-permute-start(bf16[640,128]{1,0:T(8,128)(2,1)S(1)} %get-tuple-element.83), channel_id=1, source_target_pairs={{0,8},{4,12},{8,0},{12,4},{16,24},{20,28},{24,16},{28,20},{1,9},{5... | collective-permute-start | bytes 491528 | tf_op jit(solution)/shard_map/ppermute | solution.py:40
  53.0 1.9 %collective-permute-done.11.refs_2_.refs_0_ = bf16[640,128]{1,0:T(8,128)(2,1)S(1)} collective-permute-done((bf16[640,128]{1,0:T(8,128)(2,1)S(1)}, bf16[640,128]{1,0:T(8,128)(2,1)S(1)}, u32[]{:S(2)}, u32[]{:S(2)}) %collective-permute-start.11) | collective-permute-done | bytes 163872 | tf_op jit(solution)/shard_map/ppermute | solution.py:40
  54.9 9.6 %collective-permute-done.12.refs_3_.refs_1_ = bf16[640,128]{1,0:T(8,128)(2,1)S(1)} collective-permute-done((bf16[640,128]{1,0:T(8,128)(2,1)S(1)}, bf16[640,128]{1,0:T(8,128)(2,1)S(1)}, u32[]{:S(2)}, u32[]{:S(2)}) %collective-permute-start.12) | collective-permute-done | bytes 163872 | tf_op jit(solution)/shard_map/ppermute | solution.py:40
  65.6 2.3 %collective-permute-start.15 = (bf16[256,128]{1,0:T(8,128)(2,1)S(1)}, bf16[256,128]{1,0:T(8,128)(2,1)S(1)}, u32[]{:S(2)}, u32[]{:S(2)}) collective-permute-start(bf16[256,128]{1,0:T(8,128)(2,1)S(1)} %get-tuple-element.87), channel_id=1, source_target_pairs={{0,8},{4,12},{8,0},{12,4},{16,24},{20,28},{24,16},{28,20},{1,9},{5... | collective-permute-start | bytes 196616 | tf_op jit(solution)/shard_map/ppermute | solution.py:40
  70.7 6.9 %shard_map.137 = (f32[640,1024]{1,0:T(8,128)S(1)}, bf16[640,2048]{1,0:T(8,128)(2,1)S(1)}) custom-call(bf16[1024,2048]{1,0:T(8,128)(2,1)S(1)} %bitcast.12, bf16[640,512]{1,0:T(8,128)(2,1)S(1)} %shard_map.132.refs_1_, bf16[640,512]{1,0:T(8,128)(2,1)S(1)} %collective-permute-done.18.refs_2_, bf16[640,512]{1,0:T(8,128)(2,1)S(1)} %shard_map.136.refs_3_, ...), custom_call_target="tpu_custom_call" | custom-call | flops 2684354560 | bytes 10485760 | tf_op jit(solution)/shard_map/pallas_call | solution.py:56
  79.9 8.4 %collective-permute-done.14.refs_1_ = bf16[320,512]{1,0:T(8,128)(2,1)S(1)} collective-permute-done((bf16[320,512]{1,0:T(8,128)(2,1)S(1)}, bf16[320,512]{1,0:T(8,128)(2,1)S(1)}, u32[]{:S(2)}, u32[]{:S(2)}) %collective-permute-start.14) | collective-permute-done | bytes 327712 | tf_op jit(solution)/shard_map/ppermute | solution.py:40
  88.3 2.5 %shard_map.139 = (f32[640,1024]{1,0:T(8,128)S(1)}, bf16[640,2048]{1,0:T(8,128)(2,1)S(1)}) custom-call(bf16[2048,1024]{1,0:T(8,128)(2,1)S(1)} %bitcast.6, bf16[320,512]{1,0:T(8,128)(2,1)S(1)} %get-tuple-element.86.refs_0_.refs_1_, bf16[320,512]{1,0:T(8,128)(2,1)S(1)} %shard_map.138.refs_2_, bf16[320,512]{1,0:T(8,128)(2,1)S(1)} %collective-permute-done.21.refs_3_, ...), custom_call_target="tpu_custom_call" | custom-call | flops 1342177280 | bytes 8388608 | tf_op jit(solution)/shard_map/pallas_call | solution.py:56
  90.8 3.3 %collective-permute-done.23.refs_1_ = bf16[320,512]{1,0:T(8,128)(2,1)S(1)} collective-permute-done((bf16[320,512]{1,0:T(8,128)(2,1)S(1)}, bf16[320,512]{1,0:T(8,128)(2,1)S(1)}, u32[]{:S(2)}, u32[]{:S(2)}) %collective-permute-start.23) | collective-permute-done | bytes 327712 | tf_op jit(solution)/shard_map/ppermute | solution.py:40
  95.7 3.4 %shard_map.141 = (bf16[640,2048]{1,0:T(8,128)(2,1)S(1)}, bf16[640,1024]{1,0:T(8,128)(2,1)S(1)}, bf16[640,1024]{1,0:T(8,128)(2,1)S(1)}) custom-call(bf16[2048,1024]{1,0:T(8,128)(2,1)S(1)} %bitcast.7, bf16[320,512]{1,0:T(8,128)(2,1)S(1)} %collective-permute-done.14.refs_1_, bf16[320,512]{1,0:T(8,128)(2,1)S(1)} %shard_map.140.refs_2_, ...), custom_call_target="tpu_custom_call", output_to_operand_aliasing={{0}: (7, {})} | custom-call | flops 1342177280 | bytes 8388608 | tf_op jit(solution)/shard_map/pallas_call | solution.py:56
  99.1 2.0 %shard_map.146 = bf16[640,512]{1,0:T(8,128)(2,1)S(1)} custom-call(s32[1]{0:T(128)} %get-tuple-element.74.place, bf16[640,1024]{1,0:T(8,128)(2,1)S(1)} %get-tuple-element.95.refs_1_.refs_0_, bf16[2048,1024]{1,0:T(8,128)(2,1)S(1)} %bitcast.8), custom_call_target="tpu_custom_call" | custom-call | flops 671088640 | bytes 3145728 | tf_op jit(solution)/shard_map/pallas_call | solution.py:93
  107.4 1.9 %shard_map.145 = (f32[320,512]{1,0:T(8,128)S(1)}, f32[320,512]{1,0:T(8,128)S(1)}) custom-call(s32[1]{0:T(128)} %get-tuple-element.74.place, bf16[640,1024]{1,0:T(8,128)(2,1)S(1)} %get-tuple-element.95.refs_1_.refs_0_, bf16[2048,1024]{1,0:T(8,128)(2,1)S(1)} %bitcast.11, bf16[640,512]{1,0:T(8,128)(2,1)S(1)} %collective-permute-done.26.refs_2_), custom_call_target="tpu_custom_call" | custom-call | flops 671088640 | bytes 3145728 | tf_op jit(solution)/shard_map/pallas_call | solution.py:93
  109.3 6.7 %collective-permute-done.29 = bf16[320,512]{1,0:T(8,128)(2,1)S(1)} collective-permute-done((bf16[320,512]{1,0:T(8,128)(2,1)S(1)}, bf16[320,512]{1,0:T(8,128)(2,1)S(1)}, u32[]{:S(2)}, u32[]{:S(2)}) %collective-permute-start.29) | collective-permute-done | bytes 327712 | tf_op jit(solution)/shard_map/ppermute | solution.py:40
  117.6 5.8 %shard_map.143 = (bf16[1024,2048]{1,0:T(8,128)(2,1)}, f32[8,128]{1,0:T(8,128)S(1)}) custom-call(s32[1]{0:T(128)} %get-tuple-element.74.place, bf16[640,1024]{1,0:T(8,128)(2,1)S(1)} %get-tuple-element.97.refs_0_, bf16[640,2048]{1,0:T(8,128)(2,1)S(1)} %get-tuple-element.98.refs_1_), custom_call_target="tpu_custom_call" | custom-call | flops 2684354560 | bytes 10485760 | tf_op jit(solution)/shard_map/pallas_call | solution.py:93
  125.0 2.3 %collective-permute-start.32 = (bf16[640,128]{1,0:T(8,128)(2,1)S(1)}, bf16[640,128]{1,0:T(8,128)(2,1)S(1)}, u32[]{:S(2)}, u32[]{:S(2)}) collective-permute-start(bf16[640,128]{1,0:T(8,128)(2,1)S(1)} %get-tuple-element.106), channel_id=1, source_target_pairs={{0,16},{4,20},{8,24},{12,28},{16,0},{20,4},{24,8},{28,12},{1,17},{... | collective-permute-start | bytes 491528 | tf_op jit(solution)/shard_map/ppermute | solution.py:40
  128.9 5.8 %shard_map.142 = (bf16[2048,1024]{1,0:T(8,128)(2,1)}, f32[8,128]{1,0:T(8,128)S(1)}) custom-call(s32[1]{0:T(128)} %get-tuple-element.74.place, bf16[640,2048]{1,0:T(8,128)(2,1)S(1)} %get-tuple-element.94.refs_0_, bf16[640,1024]{1,0:T(8,128)(2,1)S(1)} %get-tuple-element.95.refs_1_.refs_0_), custom_call_target="tpu_custom_call" | custom-call | flops 2684354560 | bytes 10485760 | tf_op jit(solution)/shard_map/pallas_call | solution.py:93
  134.7 3.4 %collective-permute-done.32.refs_3_ = bf16[640,128]{1,0:T(8,128)(2,1)S(1)} collective-permute-done((bf16[640,128]{1,0:T(8,128)(2,1)S(1)}, bf16[640,128]{1,0:T(8,128)(2,1)S(1)}, u32[]{:S(2)}, u32[]{:S(2)}) %collective-permute-start.32) | collective-permute-done | bytes 163872 | tf_op jit(solution)/shard_map/ppermute | solution.py:40
  138.1 2.0 %shard_map.149 = (bf16[1024,128]{1,0:T(8,128)(2,1)S(1)}, bf16[1024,128]{1,0:T(8,128)(2,1)S(1)}, bf16[1024,128]{1,0:T(8,128)(2,1)S(1)}) custom-call(f32[8,128]{1,0:T(8,128)S(1)} %get-tuple-element.96.refs_0_, bf16[640,128]{1,0:T(8,128)(2,1)S(1)} %get-tuple-element.104.refs_1_, bf16[640,128]{1,0:T(8,128)(2,1)S(1)} %collective-permute-done.31.refs_2_, ...), custom_call_target="tpu_custom_call" | custom-call | flops 536870912 | bytes 6291456 | tf_op jit(solution)/shard_map/pallas_call | solution.py:56
  140.1 2.4 %shard_map.150 = (bf16[256,128]{1,0:T(8,128)(2,1)S(1)}, bf16[256,128]{1,0:T(8,128)(2,1)S(1)}, bf16[256,128]{1,0:T(8,128)(2,1)S(1)}, bf16[256,128]{1,0:T(8,128)(2...) custom-call(bf16[256,512]{1,0:T(8,128)(2,1)S(1)} %get-tuple-element.70.refs_9_.refs_0_, ...), custom_call_target="tpu_custom_call" | custom-call | flops 1610612736 | bytes 6291456 | tf_op jit(solution)/shard_map/pallas_call | solution.py:56
  144.6 2.3 %collective-permute-start.34 = (bf16[256,128]{1,0:T(8,128)(2,1)S(1)}, bf16[256,128]{1,0:T(8,128)(2,1)S(1)}, u32[]{:S(2)}, u32[]{:S(2)}) collective-permute-start(bf16[256,128]{1,0:T(8,128)(2,1)S(1)} %get-tuple-element.115), channel_id=1, source_target_pairs={{0,8},{4,12},{8,0},{12,4},{16,24},{20,28},{24,16},{28,20},{1,9},{5... | collective-permute-start | bytes 196616 | tf_op jit(solution)/shard_map/ppermute | solution.py:40
  149.6 2.4 %collective-permute-start.40 = (bf16[256,128]{1,0:T(8,128)(2,1)S(1)}, bf16[256,128]{1,0:T(8,128)(2,1)S(1)}, u32[]{:S(2)}, u32[]{:S(2)}) collective-permute-start(bf16[256,128]{1,0:T(8,128)(2,1)S(1)} %get-tuple-element.131), channel_id=1, source_target_pairs={{0,24},{4,28},{8,16},{12,20},{16,8},{20,12},{24,0},{28,4},{1,25},{... | collective-permute-start | bytes 196616 | tf_op jit(solution)/shard_map/ppermute | solution.py:40
  152.0 6.4 %collective-permute-start.39 = (bf16[256,128]{1,0:T(8,128)(2,1)S(1)}, bf16[256,128]{1,0:T(8,128)(2,1)S(1)}, u32[]{:S(2)}, u32[]{:S(2)}) collective-permute-start(bf16[256,128]{1,0:T(8,128)(2,1)S(1)} %get-tuple-element.132), channel_id=1, source_target_pairs={{0,16},{4,20},{8,24},{12,28},{16,0},{20,4},{24,8},{28,12},{1,17},{... | collective-permute-start | bytes 196616 | tf_op jit(solution)/shard_map/ppermute | solution.py:40
  160.0 2.0 %collective-permute-start.43 = (bf16[256,128]{1,0:T(8,128)(2,1)S(1)}, bf16[256,128]{1,0:T(8,128)(2,1)S(1)}, u32[]{:S(2)}, u32[]{:S(2)}) collective-permute-start(bf16[256,128]{1,0:T(8,128)(2,1)S(1)} %get-tuple-element.128), channel_id=1, source_target_pairs={{0,16},{4,20},{8,24},{12,28},{16,0},{20,4},{24,8},{28,12},{1,17},{... | collective-permute-start | bytes 196616 | tf_op jit(solution)/shard_map/ppermute | solution.py:40
  164.8 2.0 %collective-permute-done.43.refs_10_ = bf16[256,128]{1,0:T(8,128)(2,1)S(1)} collective-permute-done((bf16[256,128]{1,0:T(8,128)(2,1)S(1)}, bf16[256,128]{1,0:T(8,128)(2,1)S(1)}, u32[]{:S(2)}, u32[]{:S(2)}) %collective-permute-start.43) | collective-permute-done | bytes 65568 | tf_op jit(solution)/shard_map/ppermute | solution.py:40
  (102 shorter events, 44.0 us)
Async XLA Ops:
  4.1 18.8 %collective-permute-start.1 = (bf16[784,128]{1,0:T(8,128)(2,1)}, bf16[784,128]{1,0:T(8,128)(2,1)S(1)}, u32[]{:S(2)}, u32[]{:S(2)}) collective-permute-start(bf16[784,128]{1,0:T(8,128)(2,1)} %get-tuple-element.68), channel_id=1, source_target_pairs={{0,16},{4,20},{8,24},{12,28},{16,0},{20,4},{24,8},{28,12},{1,17},{... | collective-permute-start | bytes 602120 | tf_op jit(solution)/shard_map/ppermute | solution.py:40
  8.2 14.7 %collective-permute-start.2 = (bf16[784,128]{1,0:T(8,128)(2,1)}, bf16[784,128]{1,0:T(8,128)(2,1)S(1)}, u32[]{:S(2)}, u32[]{:S(2)}) collective-permute-start(bf16[784,128]{1,0:T(8,128)(2,1)} %get-tuple-element.69), channel_id=1, source_target_pairs={{0,24},{4,28},{8,16},{12,20},{16,8},{20,12},{24,0},{28,4},{1,25},{... | collective-permute-start | bytes 602120 | tf_op jit(solution)/shard_map/ppermute | solution.py:40
  9.5 16.0 %collective-permute-start.6 = (bf16[320,512]{1,0:T(8,128)(2,1)}, bf16[320,512]{1,0:T(8,128)(2,1)S(1)}, u32[]{:S(2)}, u32[]{:S(2)}) collective-permute-start(bf16[320,512]{1,0:T(8,128)(2,1)} %get-tuple-element.77), channel_id=1, source_target_pairs={{0,4},{4,0},{8,12},{12,8},{16,20},{20,16},{24,28},{28,24},{1,5},{5... | collective-permute-start | bytes 983048 | tf_op jit(solution)/shard_map/ppermute | solution.py:40
  11.9 21.2 %collective-permute-start.3 = (bf16[512,128]{1,0:T(8,128)(2,1)S(1)}, bf16[512,128]{1,0:T(8,128)(2,1)S(1)}, u32[]{:S(2)}, u32[]{:S(2)}) collective-permute-start(bf16[512,128]{1,0:T(8,128)(2,1)S(1)} %slice.60), channel_id=1, source_target_pairs={{0,4},{4,0},{8,12},{12,8},{16,20},{20,16},{24,28},{28,24},{1,5},{5... | collective-permute-start | bytes 393224 | tf_op jit(solution)/shard_map/ppermute | solution.py:40
  12.5 13.0 %collective-permute-start = (bf16[784,128]{1,0:T(8,128)(2,1)}, bf16[784,128]{1,0:T(8,128)(2,1)S(1)}, u32[]{:S(2)}, u32[]{:S(2)}) collective-permute-start(bf16[784,128]{1,0:T(8,128)(2,1)} %get-tuple-element.67), channel_id=1, source_target_pairs={{0,8},{4,12},{8,0},{12,4},{16,24},{20,28},{24,16},{28,20},{1,9},{5... | collective-permute-start | bytes 602120 | tf_op jit(solution)/shard_map/ppermute | solution.py:40
  22.9 15.3 %collective-permute-start.5 = (bf16[1024,128]{1,0:T(8,128)(2,1)S(1)}, bf16[1024,128]{1,0:T(8,128)(2,1)S(1)}, u32[]{:S(2)}, u32[]{:S(2)}) collective-permute-start(bf16[1024,128]{1,0:T(8,128)(2,1)S(1)} %pad_maximum_fusion), channel_id=1, source_target_pairs={{0,4},{4,0},{8,12},{12,8},{16,20},{20,16},{24,28},{28,24},{1,5},{5... | collective-permute-start | bytes 786440 | tf_op jit(solution)/shard_map/ppermute | solution.py:40
  26.5 16.4 %collective-permute-start.7 = (bf16[160,512]{1,0:T(8,128)(2,1)S(1)}, bf16[160,512]{1,0:T(8,128)(2,1)S(1)}, u32[]{:S(2)}, u32[]{:S(2)}) collective-permute-start(bf16[160,512]{1,0:T(8,128)(2,1)S(1)} %get-tuple-element.79), channel_id=1, source_target_pairs={{0,8},{4,12},{8,0},{12,4},{16,24},{20,28},{24,16},{28,20},{1,9},{5... | collective-permute-start | bytes 491528 | tf_op jit(solution)/shard_map/ppermute | solution.py:40
  29.9 15.0 %collective-permute-start.8 = (bf16[160,512]{1,0:T(8,128)(2,1)S(1)}, bf16[160,512]{1,0:T(8,128)(2,1)S(1)}, u32[]{:S(2)}, u32[]{:S(2)}) collective-permute-start(bf16[160,512]{1,0:T(8,128)(2,1)S(1)} %get-tuple-element.80), channel_id=1, source_target_pairs={{0,16},{4,20},{8,24},{12,28},{16,0},{20,4},{24,8},{28,12},{1,17},{... | collective-permute-start | bytes 491528 | tf_op jit(solution)/shard_map/ppermute | solution.py:40
  31.7 13.1 %collective-permute-start.9 = (bf16[160,512]{1,0:T(8,128)(2,1)S(1)}, bf16[160,512]{1,0:T(8,128)(2,1)S(1)}, u32[]{:S(2)}, u32[]{:S(2)}) collective-permute-start(bf16[160,512]{1,0:T(8,128)(2,1)S(1)} %get-tuple-element.81), channel_id=1, source_target_pairs={{0,24},{4,28},{8,16},{12,20},{16,8},{20,12},{24,0},{28,4},{1,25},{... | collective-permute-start | bytes 491528 | tf_op jit(solution)/shard_map/ppermute | solution.py:40
  44.9 19.5 %collective-permute-start.10 = (bf16[640,512]{1,0:T(8,128)(2,1)S(1)}, bf16[640,512]{1,0:T(8,128)(2,1)S(1)}, u32[]{:S(2)}, u32[]{:S(2)}) collective-permute-start(bf16[640,512]{1,0:T(8,128)(2,1)S(1)} %shard_map.132.refs_1_), channel_id=1, source_target_pairs={{0,2},{1,3},{2,0},{3,1},{4,6},{5,7},{6,4},{7,5},{8,10},{9,11},{10,... | collective-permute-start | bytes 1966088 | tf_op jit(solution)/shard_map/ppermute | solution.py:40
  49.7 14.7 %collective-permute-start.12 = (bf16[640,128]{1,0:T(8,128)(2,1)S(1)}, bf16[640,128]{1,0:T(8,128)(2,1)S(1)}, u32[]{:S(2)}, u32[]{:S(2)}) collective-permute-start(bf16[640,128]{1,0:T(8,128)(2,1)S(1)} %get-tuple-element.84), channel_id=1, source_target_pairs={{0,16},{4,20},{8,24},{12,28},{16,0},{20,4},{24,8},{28,12},{1,17},{... | collective-permute-start | bytes 491528 | tf_op jit(solution)/shard_map/ppermute | solution.py:40
  51.6 12.9 %collective-permute-start.13 = (bf16[640,128]{1,0:T(8,128)(2,1)S(1)}, bf16[640,128]{1,0:T(8,128)(2,1)S(1)}, u32[]{:S(2)}, u32[]{:S(2)}) collective-permute-start(bf16[640,128]{1,0:T(8,128)(2,1)S(1)} %get-tuple-element.85), channel_id=1, source_target_pairs={{0,24},{4,28},{8,16},{12,20},{16,8},{20,12},{24,0},{28,4},{1,25},{... | collective-permute-start | bytes 491528 | tf_op jit(solution)/shard_map/ppermute | solution.py:40
  52.9 15.0 %collective-permute-start.18 = (bf16[640,512]{1,0:T(8,128)(2,1)S(1)}, bf16[640,512]{1,0:T(8,128)(2,1)S(1)}, u32[]{:S(2)}, u32[]{:S(2)}) collective-permute-start(bf16[640,512]{1,0:T(8,128)(2,1)S(1)} %shard_map.132.refs_1_), channel_id=1, source_target_pairs={{0,1},{1,0},{2,3},{3,2},{4,5},{5,4},{6,7},{7,6},{8,9},{9,8},{10,11... | collective-permute-start | bytes 1966088 | tf_op jit(solution)/shard_map/ppermute | solution.py:40
  64.7 13.5 %collective-permute-start.20 = (bf16[320,512]{1,0:T(8,128)(2,1)S(1)}, bf16[320,512]{1,0:T(8,128)(2,1)S(1)}, u32[]{:S(2)}, u32[]{:S(2)}) collective-permute-start(bf16[320,512]{1,0:T(8,128)(2,1)S(1)} %get-tuple-element.91), channel_id=1, source_target_pairs={{0,4},{4,0},{8,12},{12,8},{16,20},{20,16},{24,28},{28,24},{1,5},{5... | collective-permute-start | bytes 983048 | tf_op jit(solution)/shard_map/ppermute | solution.py:40
  65.4 22.9 %collective-permute-start.21 = (bf16[320,512]{1,0:T(8,128)(2,1)S(1)}, bf16[320,512]{1,0:T(8,128)(2,1)S(1)}, u32[]{:S(2)}, u32[]{:S(2)}) collective-permute-start(bf16[320,512]{1,0:T(8,128)(2,1)S(1)} %get-tuple-element.86.refs_0_.refs_1_), channel_id=1, source_target_pairs={{0,1},{1,0},{2,3},{3,2},{4,5},{5,4},{6,7},{7,6},{8,9},{9,8},{10,11... | collective-permute-start | bytes 983048 | tf_op jit(solution)/shard_map/ppermute | solution.py:40
  65.6 12.0 %collective-permute-start.15 = (bf16[256,128]{1,0:T(8,128)(2,1)S(1)}, bf16[256,128]{1,0:T(8,128)(2,1)S(1)}, u32[]{:S(2)}, u32[]{:S(2)}) collective-permute-start(bf16[256,128]{1,0:T(8,128)(2,1)S(1)} %get-tuple-element.87), channel_id=1, source_target_pairs={{0,8},{4,12},{8,0},{12,4},{16,24},{20,28},{24,16},{28,20},{1,9},{5... | collective-permute-start | bytes 196616 | tf_op jit(solution)/shard_map/ppermute | solution.py:40
  67.9 10.3 %collective-permute-start.16 = (bf16[256,128]{1,0:T(8,128)(2,1)S(1)}, bf16[256,128]{1,0:T(8,128)(2,1)S(1)}, u32[]{:S(2)}, u32[]{:S(2)}) collective-permute-start(bf16[256,128]{1,0:T(8,128)(2,1)S(1)} %get-tuple-element.88), channel_id=1, source_target_pairs={{0,16},{4,20},{8,24},{12,28},{16,0},{20,4},{24,8},{28,12},{1,17},{... | collective-permute-start | bytes 196616 | tf_op jit(solution)/shard_map/ppermute | solution.py:40
  69.2 9.0 %collective-permute-start.17 = (bf16[256,128]{1,0:T(8,128)(2,1)S(1)}, bf16[256,128]{1,0:T(8,128)(2,1)S(1)}, u32[]{:S(2)}, u32[]{:S(2)}) collective-permute-start(bf16[256,128]{1,0:T(8,128)(2,1)S(1)} %get-tuple-element.89), channel_id=1, source_target_pairs={{0,24},{4,28},{8,16},{12,20},{16,8},{20,12},{24,0},{28,4},{1,25},{... | collective-permute-start | bytes 196616 | tf_op jit(solution)/shard_map/ppermute | solution.py:40
  77.6 10.7 %collective-permute-start.14 = (bf16[320,512]{1,0:T(8,128)(2,1)S(1)}, bf16[320,512]{1,0:T(8,128)(2,1)S(1)}, u32[]{:S(2)}, u32[]{:S(2)}) collective-permute-start(bf16[320,512]{1,0:T(8,128)(2,1)S(1)} %get-tuple-element.86.refs_0_.refs_1_), channel_id=1, source_target_pairs={{0,2},{1,3},{2,0},{3,1},{4,6},{5,7},{6,4},{7,5},{8,10},{9,11},{10,... | collective-permute-start | bytes 983048 | tf_op jit(solution)/shard_map/ppermute | solution.py:40
  78.2 10.1 %collective-permute-start.22 = (bf16[320,512]{1,0:T(8,128)(2,1)S(1)}, bf16[320,512]{1,0:T(8,128)(2,1)S(1)}, u32[]{:S(2)}, u32[]{:S(2)}) collective-permute-start(bf16[320,512]{1,0:T(8,128)(2,1)S(1)} %shard_map.138.refs_2_), channel_id=1, source_target_pairs={{0,1},{1,0},{2,3},{3,2},{4,5},{5,4},{6,7},{7,6},{8,9},{9,8},{10,11... | collective-permute-start | bytes 983048 | tf_op jit(solution)/shard_map/ppermute | solution.py:40
  78.3 15.8 %collective-permute-start.23 = (bf16[320,512]{1,0:T(8,128)(2,1)S(1)}, bf16[320,512]{1,0:T(8,128)(2,1)S(1)}, u32[]{:S(2)}, u32[]{:S(2)}) collective-permute-start(bf16[320,512]{1,0:T(8,128)(2,1)S(1)} %shard_map.138.refs_2_), channel_id=1, source_target_pairs={{0,2},{1,3},{2,0},{3,1},{4,6},{5,7},{6,4},{7,5},{8,10},{9,11},{10,... | collective-permute-start | bytes 983048 | tf_op jit(solution)/shard_map/ppermute | solution.py:40
  105.3 10.6 %collective-permute-start.29 = (bf16[320,512]{1,0:T(8,128)(2,1)S(1)}, bf16[320,512]{1,0:T(8,128)(2,1)S(1)}, u32[]{:S(2)}, u32[]{:S(2)}) collective-permute-start(bf16[320,512]{1,0:T(8,128)(2,1)S(1)} %get-tuple-element.103), channel_id=1, source_target_pairs={{0,2},{1,3},{2,0},{3,1},{4,6},{5,7},{6,4},{7,5},{8,10},{9,11},{10,... | collective-permute-start | bytes 983048 | tf_op jit(solution)/shard_map/ppermute | solution.py:40
  105.9 17.5 %collective-permute-start.28 = (bf16[320,512]{1,0:T(8,128)(2,1)S(1)}, bf16[320,512]{1,0:T(8,128)(2,1)S(1)}, u32[]{:S(2)}, u32[]{:S(2)}) collective-permute-start(bf16[320,512]{1,0:T(8,128)(2,1)S(1)} %get-tuple-element.101), channel_id=1, source_target_pairs={{0,2},{1,3},{2,0},{3,1},{4,6},{5,7},{6,4},{7,5},{8,10},{9,11},{10,... | collective-permute-start | bytes 983048 | tf_op jit(solution)/shard_map/ppermute | solution.py:40
  116.0 8.2 %collective-permute-start.30 = (bf16[320,512]{1,0:T(8,128)(2,1)S(1)}, bf16[320,512]{1,0:T(8,128)(2,1)S(1)}, u32[]{:S(2)}, u32[]{:S(2)}) collective-permute-start(bf16[320,512]{1,0:T(8,128)(2,1)S(1)} %add_convert_fusion), channel_id=1, source_target_pairs={{0,4},{4,0},{8,12},{12,8},{16,20},{20,16},{24,28},{28,24},{1,5},{5... | collective-permute-start | bytes 983048 | tf_op jit(solution)/shard_map/ppermute | solution.py:40
  124.4 10.3 %collective-permute-start.31 = (bf16[640,128]{1,0:T(8,128)(2,1)S(1)}, bf16[640,128]{1,0:T(8,128)(2,1)S(1)}, u32[]{:S(2)}, u32[]{:S(2)}) collective-permute-start(bf16[640,128]{1,0:T(8,128)(2,1)S(1)} %get-tuple-element.105), channel_id=1, source_target_pairs={{0,8},{4,12},{8,0},{12,4},{16,24},{20,28},{24,16},{28,20},{1,9},{5... | collective-permute-start | bytes 491528 | tf_op jit(solution)/shard_map/ppermute | solution.py:40
  125.0 13.1 %collective-permute-start.32 = (bf16[640,128]{1,0:T(8,128)(2,1)S(1)}, bf16[640,128]{1,0:T(8,128)(2,1)S(1)}, u32[]{:S(2)}, u32[]{:S(2)}) collective-permute-start(bf16[640,128]{1,0:T(8,128)(2,1)S(1)} %get-tuple-element.106), channel_id=1, source_target_pairs={{0,16},{4,20},{8,24},{12,28},{16,0},{20,4},{24,8},{28,12},{1,17},{... | collective-permute-start | bytes 491528 | tf_op jit(solution)/shard_map/ppermute | solution.py:40
  127.3 10.8 %collective-permute-start.33 = (bf16[640,128]{1,0:T(8,128)(2,1)S(1)}, bf16[640,128]{1,0:T(8,128)(2,1)S(1)}, u32[]{:S(2)}, u32[]{:S(2)}) collective-permute-start(bf16[640,128]{1,0:T(8,128)(2,1)S(1)} %get-tuple-element.107), channel_id=1, source_target_pairs={{0,24},{4,28},{8,16},{12,20},{16,8},{20,12},{24,0},{28,4},{1,25},{... | collective-permute-start | bytes 491528 | tf_op jit(solution)/shard_map/ppermute | solution.py:40
  144.6 13.9 %collective-permute-start.34 = (bf16[256,128]{1,0:T(8,128)(2,1)S(1)}, bf16[256,128]{1,0:T(8,128)(2,1)S(1)}, u32[]{:S(2)}, u32[]{:S(2)}) collective-permute-start(bf16[256,128]{1,0:T(8,128)(2,1)S(1)} %get-tuple-element.115), channel_id=1, source_target_pairs={{0,8},{4,12},{8,0},{12,4},{16,24},{20,28},{24,16},{28,20},{1,9},{5... | collective-permute-start | bytes 196616 | tf_op jit(solution)/shard_map/ppermute | solution.py:40
  146.9 11.7 %collective-permute-start.35 = (bf16[256,128]{1,0:T(8,128)(2,1)S(1)}, bf16[256,128]{1,0:T(8,128)(2,1)S(1)}, u32[]{:S(2)}, u32[]{:S(2)}) collective-permute-start(bf16[256,128]{1,0:T(8,128)(2,1)S(1)} %get-tuple-element.116), channel_id=1, source_target_pairs={{0,16},{4,20},{8,24},{12,28},{16,0},{20,4},{24,8},{28,12},{1,17},{... | collective-permute-start | bytes 196616 | tf_op jit(solution)/shard_map/ppermute | solution.py:40
  148.1 12.0 %collective-permute-start.36 = (bf16[256,128]{1,0:T(8,128)(2,1)S(1)}, bf16[256,128]{1,0:T(8,128)(2,1)S(1)}, u32[]{:S(2)}, u32[]{:S(2)}) collective-permute-start(bf16[256,128]{1,0:T(8,128)(2,1)S(1)} %get-tuple-element.117), channel_id=1, source_target_pairs={{0,24},{4,28},{8,16},{12,20},{16,8},{20,12},{24,0},{28,4},{1,25},{... | collective-permute-start | bytes 196616 | tf_op jit(solution)/shard_map/ppermute | solution.py:40
  149.6 12.5 %collective-permute-start.40 = (bf16[256,128]{1,0:T(8,128)(2,1)S(1)}, bf16[256,128]{1,0:T(8,128)(2,1)S(1)}, u32[]{:S(2)}, u32[]{:S(2)}) collective-permute-start(bf16[256,128]{1,0:T(8,128)(2,1)S(1)} %get-tuple-element.131), channel_id=1, source_target_pairs={{0,24},{4,28},{8,16},{12,20},{16,8},{20,12},{24,0},{28,4},{1,25},{... | collective-permute-start | bytes 196616 | tf_op jit(solution)/shard_map/ppermute | solution.py:40
  152.0 11.5 %collective-permute-start.39 = (bf16[256,128]{1,0:T(8,128)(2,1)S(1)}, bf16[256,128]{1,0:T(8,128)(2,1)S(1)}, u32[]{:S(2)}, u32[]{:S(2)}) collective-permute-start(bf16[256,128]{1,0:T(8,128)(2,1)S(1)} %get-tuple-element.132), channel_id=1, source_target_pairs={{0,16},{4,20},{8,24},{12,28},{16,0},{20,4},{24,8},{28,12},{1,17},{... | collective-permute-start | bytes 196616 | tf_op jit(solution)/shard_map/ppermute | solution.py:40
  (19 other events, 198.5 us)

commit v3 on v2

--- a/solution.py
+++ b/solution.py
@@ -195,7 +195,7 @@
 
 
 def pair_groups(G):
-    return [members for members in ([0], [1], list(range(2, G))) if members and members[-1] < G]
+    return [members for members in ([0], list(range(1, G))) if members and members[-1] < G]
 
 
 def forward_body(sizes, slopes, *refs):
@@ -277,7 +277,7 @@
     n = G * R
     s = lax.axis_index("seq")
     g, r = s // R, s % R
-    back, refs = refs[:G], refs[G:]
+    back, refs = refs[:n], refs[n:]
     upper, refs = refs[:G], refs[G:]
     probs, refs = refs[:G], refs[G:]
     routing, attn_grad, refs = refs[0], refs[1], refs[2:]
@@ -287,8 +287,7 @@
     for i in reversed(range(G)):
         N = (i + 1) * R * BL
         mine = slice(i * BL, (i + 1) * BL)
-        starts = [(dr * G + i) * stride for dr in range(R)]
-        rows = jnp.concatenate([back[dg][at : at + stride] for dg in range(G) for at in starts], axis=0)
+        rows = jnp.concatenate([back[d][i * stride : (i + 1) * stride] for d in range(n)], axis=0)
         picked = cols_by_cols(routing[i], rows)
         grad = (upper_rows[mine].astype(F32) + picked).astype(BF16)
         attn_grad[mine] = grad
@@ -373,15 +372,15 @@
             refs[-1][at] = refs[dg][dr * stride : (dr + 1) * stride]
 
 
-def turn_back_body(sizes, near, arrived, *refs):
+def turn_back_body(sizes, near, arrived, *outs):
     G, R, count = sizes
     g = lax.axis_index("seq") // R
-    moved, outs = refs[: R - 1], refs[R - 1 :]
+    each = len(outs) // G
     for dg in range(G):
         cols = pl.ds(pl.multiple_of((g ^ dg) * HD, HD), HD)
-        outs[dg][0:count] = (near[0:count, cols] + arrived[0:count, cols].astype(F32)).astype(BF16)
-        for dr in range(1, R):
-            outs[dg][dr * count : (dr + 1) * count] = moved[dr - 1][:, cols]
+        for at in range(each):
+            rows = slice(at * count, (at + 1) * count)
+            outs[dg * each + at][...] = (near[rows, cols] + arrived[rows, cols].astype(F32)).astype(BF16)
 
 
 def keep_moves(parts, first, shards, full, sems):
@@ -407,12 +406,14 @@
         mine = pl.ds(c * tall, tall)
         return pltpu.make_async_copy(weight.at[mine], held.at[mine], sems.at[c])
 
-    for c in range(steps):
+    for c in range(min(2, steps)):
         fetch(c).start()
     for move in kept:
         move.start()
     for c in range(steps):
         fetch(c).wait()
+        if c + 2 < steps:
+            fetch(c + 2).start()
         for h in range(parts):
             total = None
             for k in range(len(shards) // parts):
@@ -424,44 +425,37 @@
         move.wait()
 
 
-def pre_body(parts, first, weight, *refs):
-    held, sems, own_sems = refs[-3:]
-    if first:
-        shards, begun, through, full, hidden, hidden_grad = refs[:-9], *refs[-9:-7], *refs[-6:-3]
-    else:
-        shards, out, full = refs[:-5], *refs[-5:-3]
-    kept = keep_moves(parts, first, shards, full, own_sems)
+def pre_body(parts, weight, *refs):
+    shards, through, full, hidden, hidden_grad, held, sems, own_sems = refs[:-7], *refs[-7:]
     place = lax.axis_index("exp")
     rows, width = shards[0].shape
-    count, steps = sems.shape
+    steps = sems.shape[0]
     wide = weight.shape[1] // steps
-
-    def fetch(k, c):
-        source = weight.at[pl.ds(pl.multiple_of((place ^ (first + k)) * width, 128), width), pl.ds(c * wide, wide)]
-        return pltpu.make_async_copy(source, held.at[c, pl.ds(k * width, width)], sems.at[k, c])
-
-    for c in range(steps):
-        for k in range(count):
-            fetch(k, c).start()
+    kept = keep_moves(parts, 0, shards, full, own_sems)
+
+    def fetch(c):
+        return pltpu.make_async_copy(weight.at[:, pl.ds(c * wide, wide)], held.at[c], sems.at[c])
+
+    for c in range(min(2, steps)):
+        fetch(c).start()
     for move in kept:
         move.start()
     for c in range(steps):
         cols = slice(c * wide, (c + 1) * wide)
-        for k in range(count):
-            fetch(k, c).wait()
+        fetch(c).wait()
+        if c + 2 < steps:
+            fetch(c + 2).start()
         for h in range(parts):
             mine = slice(h * rows, (h + 1) * rows)
-            total = begun[mine, cols] if first else None
-            for k in range(count):
-                part = plain(shards[k * parts + h][...], held[c, k * width : (k + 1) * width])
+            total = None
+            for k in range(len(shards) // parts):
+                at = pl.ds(pl.multiple_of((place ^ k) * width, 128), width)
+                part = plain(shards[k * parts + h][...], held[c, at, :])
                 total = part if total is None else total + part
-            if not first:
-                out[mine, cols] = total
-            else:
-                logistic = 1.0 / (1.0 + jnp.exp(-total))
-                hidden[mine, cols] = (total * logistic).astype(BF16)
-                grad = through[mine, cols] * logistic * (1.0 + total * (1.0 - logistic))
-                hidden_grad[mine, cols] = grad.astype(BF16)
+            logistic = 1.0 / (1.0 + jnp.exp(-total))
+            hidden[mine, cols] = (total * logistic).astype(BF16)
+            grad = through[mine, cols] * logistic * (1.0 + total * (1.0 - logistic))
+            hidden_grad[mine, cols] = grad.astype(BF16)
     for move in kept:
         move.wait()
 
@@ -617,49 +611,36 @@
         after=[grads_far],
         nbytes=rows * features * 4,
     )
+    token_parts = arrays_of([swap(tokens[dr], "seq", dr) for dr in range(R)])
+    token_parts[1:] = hold(token_parts[1:], [through])
     upper = local_call(
         functools.partial(upper_body, (G, R, BL)),
         [((BL, HD), BF16)] * G,
         [],
-        after=tokens[:1],
+        after=token_parts[1:],
         far=[out_grad],
         scratch=[pltpu.SemaphoreType.DMA((G,))],
         nbytes=2 * BL * features * 2,
     )
     upper = [swap(upper[d], "seq", d * R) for d in range(G)]
-
-    token_parts = arrays_of([swap(tokens[dr], "seq", dr) for dr in range(R)])
+    far_parts = [swap(part, "exp", half) for part in token_parts]
     if G > 1:
-        token_parts[1:] = hold(token_parts[1:], upper[1:] + [through])
-    far_parts = [swap(part, "exp", half) for part in token_parts]
+        far_parts[1:] = hold(far_parts[1:], upper[1:])
     near_shards = [gather_exp(part, half) for part in token_parts]
     near_shards = [near_shards[h][k] for k in range(half) for h in range(parts)]
-    streamed = [
-        pltpu.VMEM((steps, half * features, width), BF16),
-        pltpu.SemaphoreType.DMA((half, steps)),
-        pltpu.SemaphoreType.DMA((half * parts,)),
-    ]
-    begun, full_tokens = local_call(
-        functools.partial(pre_body, parts, 0),
-        [((rows, FFL), F32), ((rows, E * features), BF16, pltpu.HBM)],
-        near_shards,
-        far=[weight_in],
-        scratch=streamed,
-        flops=work * half,
-        nbytes=8 * MIB,
-    )
-    far_parts[1:] = hold(far_parts[1:], [begun])
     far_shards = [gather_exp(part, half) for part in far_parts]
     far_shards = [far_shards[h][k] for k in range(half) for h in range(parts)]
     full_tokens, hidden, hidden_grad = local_call(
-        functools.partial(pre_body, parts, half),
+        functools.partial(pre_body, parts),
         [((rows, E * features), BF16, pltpu.HBM)] + [((rows, FFL), BF16)] * 2,
-        far_shards + [begun, through],
-        into=[full_tokens],
+        near_shards + far_shards + [through],
         far=[weight_in],
-        aliases={half * parts + 3: 0},
-        scratch=streamed,
-        flops=work * half,
+        scratch=[
+            pltpu.VMEM((steps, E * features, width), BF16),
+            pltpu.SemaphoreType.DMA((steps,)),
+            pltpu.SemaphoreType.DMA((E * parts,)),
+        ],
+        flops=work * E,
         nbytes=8 * MIB,
     )
 
@@ -702,20 +683,21 @@
         flops=work * E,
         nbytes=10 * MIB,
     )
-    count = G * stride
-    away = []
-    for dr in range(1, R):
-        mine = slice((dr % each) * count, (dr % each + 1) * count)
-        total = near[0][dr // each][mine] + arrived[0][dr // each][mine].astype(F32)
-        away.append(swap(total.astype(BF16), "seq", dr))
-    back_sent = local_call(
-        functools.partial(turn_back_body, (G, R, count)),
-        [((R * count, HD), BF16)] * G,
-        [near[0][0], arrived[0][0]] + away,
-        after=[out_mark],
-        nbytes=tall * features * 8,
-    )
-    returned = [swap(back_sent[dg], "seq", dg * R) for dg in range(G)]
+    returned = [None] * n
+    ready = [out_mark]
+    for h in range(parts):
+        pieces = local_call(
+            functools.partial(turn_back_body, (G, R, G * stride)),
+            [((G * stride, HD), BF16)] * (G * each),
+            [near[0][h], arrived[0][h]],
+            after=ready,
+            nbytes=tall * features * 8,
+        )
+        for dg in range(G):
+            for at in range(each):
+                d = dg * R + h * each + at
+                returned[d] = swap(pieces[dg * each + at], "seq", d)
+        ready = [x for x in returned[1:] if x is not None]
     in_weight_grad, in_mark = grid_call(
         weight_grad_body,
         E,

time: 168 us -> 157 us (0.935)
  starting transfers between devices: 61.7 us -> 56.1 us
  waiting for transfers between devices: 55.8 us -> 51.4 us
    ppermute x45 -> x47, starting transfers between devices: 61.7 us -> 56.1 us  [swap(): return lax.ppermute(block, axis, [(i, i ^ distance) for i in devices])]
    ppermute x45 -> x47, waiting for transfers between devices: 55.8 us -> 51.4 us  [swap(): return lax.ppermute(block, axis, [(i, i ^ distance) for i in devices])]
  transfers between devices with their start and end apart: 45 -> 47, of which waited for: 17 -> 19; matrix products, arithmetic and copies ran while one was open for 1% -> 0% of each run, Pallas kernels for 20% -> 20%
where the time goes in v3:
time: 157 us
  starting transfers between devices  56.1 us (36%)
  waiting for transfers between devices  51.4 us (33%)
  Pallas kernels  47.1 us (30%)
    ppermute x47, starting transfers between devices, swap(): return lax.ppermute(block, axis, [(i, i ^ distance) for i in devices])  56.1 us
    ppermute x47, waiting for transfers between devices, swap(): return lax.ppermute(block, axis, [(i, i ^ distance) for i in devices])  51.4 us
    pallas_call x15, Pallas kernels, local_call(): pl.pallas_call(kernel, out_shape=[jax.ShapeDtypeStruct(x[0], x[1]) for x...  27.7 us
    pallas_call x6, Pallas kernels, grid_call(): pl.pallas_call(kernel, out_shape=[jax.ShapeDtypeStruct(shape, dtype) for...  19.4 us
  transfers between devices with their start and end apart: 47, of which 19 were waited for; matrix products, arithmetic and copies ran while one was open for 0% of the time, Pallas kernels for 20%

profile of v3, /device:TPU:0, one launch (start us, length us, event | category | flops | bytes accessed | tf_op | source)
XLA Modules:
  0.0 156.8 jit_solution(8714136751855260160)
XLA Ops:
  0.6 3.4 %shard_map.128 = (bf16[784,128]{1,0:T(8,128)(2,1)}, bf16[784,128]{1,0:T(8,128)(2,1)}, bf16[784,128]{1,0:T(8,128)(2,1)}, bf16[784,128]{1,0:T(8,128)(2,1)}, bf16[3...) custom-call(bf16[256,512]{1,0:T(8,128)(2,1)} %refs_0_.2, bf16[256,512]{1,0:T(8,128)(2,1)} %refs_1_.2, ...), custom_call_target="tpu_custom_call" | custom-call | bytes 1572864 | tf_op jit(solution)/shard_map/pallas_call | solution.py:56
  4.1 5.1 %collective-permute-start.2 = (bf16[784,128]{1,0:T(8,128)(2,1)}, bf16[784,128]{1,0:T(8,128)(2,1)S(1)}, u32[]{:S(2)}, u32[]{:S(2)}) collective-permute-start(bf16[784,128]{1,0:T(8,128)(2,1)} %get-tuple-element.71), channel_id=1, source_target_pairs={{0,24},{4,28},{8,16},{12,20},{16,8},{20,12},{24,0},{28,4},{1,25},{... | collective-permute-start | bytes 602120 | tf_op jit(solution)/shard_map/ppermute | solution.py:40
  11.5 3.9 %collective-permute-done.2.refs_4_.refs_3_.refs_2_ = bf16[784,128]{1,0:T(8,128)(2,1)S(1)} collective-permute-done((bf16[784,128]{1,0:T(8,128)(2,1)}, bf16[784,128]{1,0:T(8,128)(2,1)S(1)}, u32[]{:S(2)}, u32[]{:S(2)}) %collective-permute-start.2) | collective-permute-done | bytes 200736 | tf_op jit(solution)/shard_map/ppermute | solution.py:40
  15.4 11.1 %collective-permute-done.1.refs_3_.refs_2_.refs_1_ = bf16[784,128]{1,0:T(8,128)(2,1)S(1)} collective-permute-done((bf16[784,128]{1,0:T(8,128)(2,1)}, bf16[784,128]{1,0:T(8,128)(2,1)S(1)}, u32[]{:S(2)}, u32[]{:S(2)}) %collective-permute-start.1) | collective-permute-done | bytes 200736 | tf_op jit(solution)/shard_map/ppermute | solution.py:40
  29.2 3.0 %collective-permute-start.7 = (bf16[160,512]{1,0:T(8,128)(2,1)S(1)}, bf16[160,512]{1,0:T(8,128)(2,1)S(1)}, u32[]{:S(2)}, u32[]{:S(2)}) collective-permute-start(bf16[160,512]{1,0:T(8,128)(2,1)S(1)} %get-tuple-element.82), channel_id=1, source_target_pairs={{0,16},{4,20},{8,24},{12,28},{16,0},{20,4},{24,8},{28,12},{1,17},{... | collective-permute-start | bytes 491528 | tf_op jit(solution)/shard_map/ppermute | solution.py:40
  35.2 4.3 %collective-permute-done.3.refs_5_ = bf16[512,128]{1,0:T(8,128)(2,1)S(1)} collective-permute-done((bf16[512,128]{1,0:T(8,128)(2,1)S(1)}, bf16[512,128]{1,0:T(8,128)(2,1)S(1)}, u32[]{:S(2)}, u32[]{:S(2)}) %collective-permute-start.3) | collective-permute-done | bytes 131104 | tf_op jit(solution)/shard_map/ppermute | solution.py:40
  39.6 4.7 %shard_map.129 = (bf16[256,512]{1,0:T(8,128)(2,1)S(1)}, bf16[256,1024]{1,0:T(8,128)(2,1)S(1)}, bf16[256,1536]{1,0:T(8,128)(2,1)S(1)}, bf16[256,2048]{1,0:T(8,128...) custom-call(f32[4]{0:T(128)S(1)} %copy-done.4, ...), custom_call_target="tpu_custom_call" | custom-call | tf_op jit(solution)/shard_map/pallas_call | solution.py:56
  46.5 2.0 %collective-permute-start.10 = (bf16[640,128]{1,0:T(8,128)(2,1)S(1)}, bf16[640,128]{1,0:T(8,128)(2,1)S(1)}, u32[]{:S(2)}, u32[]{:S(2)}) collective-permute-start(bf16[640,128]{1,0:T(8,128)(2,1)S(1)} %get-tuple-element.85), channel_id=1, source_target_pairs={{0,8},{4,12},{8,0},{12,4},{16,24},{20,28},{24,16},{28,20},{1,9},{5... | collective-permute-start | bytes 491528 | tf_op jit(solution)/shard_map/ppermute | solution.py:40
  51.0 2.7 %collective-permute-done.10.refs_2_.refs_0_ = bf16[640,128]{1,0:T(8,128)(2,1)S(1)} collective-permute-done((bf16[640,128]{1,0:T(8,128)(2,1)S(1)}, bf16[640,128]{1,0:T(8,128)(2,1)S(1)}, u32[]{:S(2)}, u32[]{:S(2)}) %collective-permute-start.10) | collective-permute-done | bytes 163872 | tf_op jit(solution)/shard_map/ppermute | solution.py:40
  53.6 8.6 %collective-permute-done.11.refs_3_.refs_1_ = bf16[640,128]{1,0:T(8,128)(2,1)S(1)} collective-permute-done((bf16[640,128]{1,0:T(8,128)(2,1)S(1)}, bf16[640,128]{1,0:T(8,128)(2,1)S(1)}, u32[]{:S(2)}, u32[]{:S(2)}) %collective-permute-start.11) | collective-permute-done | bytes 163872 | tf_op jit(solution)/shard_map/ppermute | solution.py:40
  64.5 6.9 %shard_map.136 = (f32[640,1024]{1,0:T(8,128)S(1)}, bf16[640,2048]{1,0:T(8,128)(2,1)S(1)}) custom-call(bf16[1024,2048]{1,0:T(8,128)(2,1)S(1)} %bitcast.11, bf16[640,512]{1,0:T(8,128)(2,1)S(1)} %shard_map.132.refs_1_, bf16[640,512]{1,0:T(8,128)(2,1)S(1)} %collective-permute-done.13.refs_2_, bf16[640,512]{1,0:T(8,128)(2,1)S(1)} %shard_map.135.refs_3_, ...), custom_call_target="tpu_custom_call" | custom-call | flops 2684354560 | bytes 10485760 | tf_op jit(solution)/shard_map/pallas_call | solution.py:56
  73.2 2.4 %collective-permute-start.19 = (bf16[256,128]{1,0:T(8,128)(2,1)S(1)}, bf16[256,128]{1,0:T(8,128)(2,1)S(1)}, u32[]{:S(2)}, u32[]{:S(2)}) collective-permute-start(bf16[256,128]{1,0:T(8,128)(2,1)S(1)} %get-tuple-element.91), channel_id=1, source_target_pairs={{0,8},{4,12},{8,0},{12,4},{16,24},{20,28},{24,16},{28,20},{1,9},{5... | collective-permute-start | bytes 196616 | tf_op jit(solution)/shard_map/ppermute | solution.py:40
  78.6 4.5 %collective-permute-done.20.refs_1_.refs_11_ = bf16[256,128]{1,0:T(8,128)(2,1)S(1)} collective-permute-done((bf16[256,128]{1,0:T(8,128)(2,1)S(1)}, bf16[256,128]{1,0:T(8,128)(2,1)S(1)}, u32[]{:S(2)}, u32[]{:S(2)}) %collective-permute-start.20) | collective-permute-done | bytes 65568 | tf_op jit(solution)/shard_map/ppermute | solution.py:40
  85.2 5.1 %shard_map.140 = (bf16[640,2048]{1,0:T(8,128)(2,1)S(1)}, bf16[640,1024]{1,0:T(8,128)(2,1)S(1)}, bf16[640,1024]{1,0:T(8,128)(2,1)S(1)}) custom-call(bf16[2048,1024]{1,0:T(8,128)(2,1)S(1)} %bitcast.6, bf16[320,512]{1,0:T(8,128)(2,1)S(1)} %get-tuple-element.88.refs_1_, bf16[320,512]{1,0:T(8,128)(2,1)S(1)} %shard_map.137.refs_0_.refs_2_, ...), custom_call_target="tpu_custom_call" | custom-call | flops 2684354560 | bytes 8388608 | tf_op jit(solution)/shard_map/pallas_call | solution.py:56
  90.4 2.0 %shard_map.145 = bf16[640,512]{1,0:T(8,128)(2,1)S(1)} custom-call(s32[1]{0:T(128)} %get-tuple-element.76.place, bf16[640,1024]{1,0:T(8,128)(2,1)S(1)} %get-tuple-element.95.refs_1_.refs_0_, bf16[2048,1024]{1,0:T(8,128)(2,1)S(1)} %bitcast.7), custom_call_target="tpu_custom_call" | custom-call | flops 671088640 | bytes 3145728 | tf_op jit(solution)/shard_map/pallas_call | solution.py:93
  92.6 1.8 %shard_map.143 = bf16[640,512]{1,0:T(8,128)(2,1)S(1)} custom-call(s32[1]{0:T(128)} %get-tuple-element.76.place, bf16[640,1024]{1,0:T(8,128)(2,1)S(1)} %get-tuple-element.95.refs_1_.refs_0_, bf16[2048,1024]{1,0:T(8,128)(2,1)S(1)} %bitcast.8), custom_call_target="tpu_custom_call" | custom-call | flops 671088640 | bytes 3145728 | tf_op jit(solution)/shard_map/pallas_call | solution.py:93
  94.8 1.9 %shard_map.146 = (bf16[320,512]{1,0:T(8,128)(2,1)S(1)}, bf16[320,512]{1,0:T(8,128)(2,1)S(1)}) custom-call(s32[1]{0:T(128)} %get-tuple-element.76.place, bf16[640,1024]{1,0:T(8,128)(2,1)S(1)} %get-tuple-element.95.refs_1_.refs_0_, bf16[2048,1024]{1,0:T(8,128)(2,1)S(1)} %bitcast.9, bf16[640,512]{1,0:T(8,128)(2,1)S(1)} %collective-permute-done.26.refs_2_), custom_call_target="tpu_custom_call" | custom-call | flops 671088640 | bytes 3145728 | tf_op jit(solution)/shard_map/pallas_call | solution.py:93
  98.8 5.9 %shard_map.142 = (bf16[1024,2048]{1,0:T(8,128)(2,1)}, f32[8,128]{1,0:T(8,128)S(1)}) custom-call(s32[1]{0:T(128)} %get-tuple-element.76.place, bf16[640,1024]{1,0:T(8,128)(2,1)S(1)} %get-tuple-element.97.refs_0_, bf16[640,2048]{1,0:T(8,128)(2,1)S(1)} %get-tuple-element.98.refs_1_), custom_call_target="tpu_custom_call" | custom-call | flops 2684354560 | bytes 10485760 | tf_op jit(solution)/shard_map/pallas_call | solution.py:93
  104.7 1.9 %shard_map.144 = (f32[320,512]{1,0:T(8,128)S(1)}, f32[320,512]{1,0:T(8,128)S(1)}) custom-call(s32[1]{0:T(128)} %get-tuple-element.76.place, bf16[640,1024]{1,0:T(8,128)(2,1)S(1)} %get-tuple-element.95.refs_1_.refs_0_, bf16[2048,1024]{1,0:T(8,128)(2,1)S(1)} %bitcast.10, bf16[640,512]{1,0:T(8,128)(2,1)S(1)} %collective-permute-done.25.refs_2_), custom_call_target="tpu_custom_call" | custom-call | flops 671088640 | bytes 3145728 | tf_op jit(solution)/shard_map/pallas_call | solution.py:93
  110.1 1.8 %collective-permute-start.30 = (bf16[320,128]{1,0:T(8,128)(2,1)S(1)}, bf16[320,128]{1,0:T(8,128)(2,1)S(1)}, u32[]{:S(2)}, u32[]{:S(2)}) collective-permute-start(bf16[320,128]{1,0:T(8,128)(2,1)S(1)} %get-tuple-element.105), channel_id=1, source_target_pairs={{0,24},{4,28},{8,16},{12,20},{16,8},{20,12},{24,0},{28,4},{1,25},{... | collective-permute-start | bytes 245768 | tf_op jit(solution)/shard_map/ppermute | solution.py:40
  113.5 3.0 %collective-permute-done.29.refs_1_.refs_5_ = bf16[320,128]{1,0:T(8,128)(2,1)S(1)} collective-permute-done((bf16[320,128]{1,0:T(8,128)(2,1)S(1)}, bf16[320,128]{1,0:T(8,128)(2,1)S(1)}, u32[]{:S(2)}, u32[]{:S(2)}) %collective-permute-start.29) | collective-permute-done | bytes 81952 | tf_op jit(solution)/shard_map/ppermute | solution.py:40
  117.5 2.2 %collective-permute-start.33 = (bf16[320,128]{1,0:T(8,128)(2,1)S(1)}, bf16[320,128]{1,0:T(8,128)(2,1)S(1)}, u32[]{:S(2)}, u32[]{:S(2)}) collective-permute-start(bf16[320,128]{1,0:T(8,128)(2,1)S(1)} %get-tuple-element.109), channel_id=1, source_target_pairs={{0,12},{4,8},{8,4},{12,0},{16,28},{20,24},{24,20},{28,16},{1,13},{... | collective-permute-start | bytes 245768 | tf_op jit(solution)/shard_map/ppermute | solution.py:40
  120.9 2.5 %collective-permute-start.35 = (bf16[320,128]{1,0:T(8,128)(2,1)S(1)}, bf16[320,128]{1,0:T(8,128)(2,1)S(1)}, u32[]{:S(2)}, u32[]{:S(2)}) collective-permute-start(bf16[320,128]{1,0:T(8,128)(2,1)S(1)} %get-tuple-element.111), channel_id=1, source_target_pairs={{0,28},{4,24},{8,20},{12,16},{16,12},{20,8},{24,4},{28,0},{1,29},{... | collective-permute-start | bytes 245768 | tf_op jit(solution)/shard_map/ppermute | solution.py:40
  123.5 5.9 %shard_map.141 = (bf16[2048,1024]{1,0:T(8,128)(2,1)}, f32[8,128]{1,0:T(8,128)S(1)}) custom-call(s32[1]{0:T(128)} %get-tuple-element.76.place, bf16[640,2048]{1,0:T(8,128)(2,1)S(1)} %get-tuple-element.94.refs_0_, bf16[640,1024]{1,0:T(8,128)(2,1)S(1)} %get-tuple-element.95.refs_1_.refs_0_), custom_call_target="tpu_custom_call" | custom-call | flops 2684354560 | bytes 10485760 | tf_op jit(solution)/shard_map/pallas_call | solution.py:93
  129.4 2.0 %shard_map.149 = (bf16[1024,128]{1,0:T(8,128)(2,1)S(1)}, bf16[1024,128]{1,0:T(8,128)(2,1)S(1)}, bf16[1024,128]{1,0:T(8,128)(2,1)S(1)}) custom-call(f32[8,128]{1,0:T(8,128)S(1)} %get-tuple-element.96.refs_0_, bf16[320,128]{1,0:T(8,128)(2,1)S(1)} %get-tuple-element.102.refs_1_, bf16[320,128]{1,0:T(8,128)(2,1)S(1)} %collective-permute-done.32.refs_2_, ...), custom_call_target="tpu_custom_call" | custom-call | flops 536870912 | bytes 6291456 | tf_op jit(solution)/shard_map/pallas_call | solution.py:56
  131.4 2.4 %shard_map.150 = (bf16[256,128]{1,0:T(8,128)(2,1)S(1)}, bf16[256,128]{1,0:T(8,128)(2,1)S(1)}, bf16[256,128]{1,0:T(8,128)(2,1)S(1)}, bf16[256,128]{1,0:T(8,128)(2...) custom-call(bf16[256,512]{1,0:T(8,128)(2,1)S(1)} %get-tuple-element.72.refs_13_.refs_0_, ...), custom_call_target="tpu_custom_call" | custom-call | flops 1610612736 | bytes 6291456 | tf_op jit(solution)/shard_map/pallas_call | solution.py:56
  136.5 2.0 %collective-permute-start.37 = (bf16[256,128]{1,0:T(8,128)(2,1)S(1)}, bf16[256,128]{1,0:T(8,128)(2,1)S(1)}, u32[]{:S(2)}, u32[]{:S(2)}) collective-permute-start(bf16[256,128]{1,0:T(8,128)(2,1)S(1)} %get-tuple-element.120), channel_id=1, source_target_pairs={{0,16},{4,20},{8,24},{12,28},{16,0},{20,4},{24,8},{28,12},{1,17},{... | collective-permute-start | bytes 196616 | tf_op jit(solution)/shard_map/ppermute | solution.py:40
  138.5 1.8 %collective-permute-start.38 = (bf16[256,128]{1,0:T(8,128)(2,1)S(1)}, bf16[256,128]{1,0:T(8,128)(2,1)S(1)}, u32[]{:S(2)}, u32[]{:S(2)}) collective-permute-start(bf16[256,128]{1,0:T(8,128)(2,1)S(1)} %get-tuple-element.121), channel_id=1, source_target_pairs={{0,24},{4,28},{8,16},{12,20},{16,8},{20,12},{24,0},{28,4},{1,25},{... | collective-permute-start | bytes 196616 | tf_op jit(solution)/shard_map/ppermute | solution.py:40
  141.8 2.1 %collective-permute-done.43 = bf16[1024,128]{1,0:T(8,128)(2,1)S(1)} collective-permute-done((bf16[1024,128]{1,0:T(8,128)(2,1)S(1)}, bf16[1024,128]{1,0:T(8,128)(2,1)S(1)}, u32[]{:S(2)}, u32[]{:S(2)}) %collective-permute-start.43) | collective-permute-done | bytes 262176 | tf_op jit(solution)/shard_map/ppermute | solution.py:40
  145.2 1.8 %collective-permute-start.42 = (bf16[256,128]{1,0:T(8,128)(2,1)S(1)}, bf16[256,128]{1,0:T(8,128)(2,1)S(1)}, u32[]{:S(2)}, u32[]{:S(2)}) collective-permute-start(bf16[256,128]{1,0:T(8,128)(2,1)S(1)} %get-tuple-element.135), channel_id=1, source_target_pairs={{0,24},{4,28},{8,16},{12,20},{16,8},{20,12},{24,0},{28,4},{1,25},{... | collective-permute-start | bytes 196616 | tf_op jit(solution)/shard_map/ppermute | solution.py:40
  147.6 2.1 %collective-permute-start.45 = (bf16[256,128]{1,0:T(8,128)(2,1)S(1)}, bf16[256,128]{1,0:T(8,128)(2,1)S(1)}, u32[]{:S(2)}, u32[]{:S(2)}) collective-permute-start(bf16[256,128]{1,0:T(8,128)(2,1)S(1)} %get-tuple-element.132), channel_id=1, source_target_pairs={{0,16},{4,20},{8,24},{12,28},{16,0},{20,4},{24,8},{28,12},{1,17},{... | collective-permute-start | bytes 196616 | tf_op jit(solution)/shard_map/ppermute | solution.py:40
  153.8 1.9 %collective-permute-done.46.refs_11_ = bf16[256,128]{1,0:T(8,128)(2,1)S(1)} collective-permute-done((bf16[256,128]{1,0:T(8,128)(2,1)S(1)}, bf16[256,128]{1,0:T(8,128)(2,1)S(1)}, u32[]{:S(2)}, u32[]{:S(2)}) %collective-permute-start.46) | collective-permute-done | bytes 65568 | tf_op jit(solution)/shard_map/ppermute | solution.py:40
  (105 shorter events, 42.9 us)
Async XLA Ops:
  4.1 11.3 %collective-permute-start.2 = (bf16[784,128]{1,0:T(8,128)(2,1)}, bf16[784,128]{1,0:T(8,128)(2,1)S(1)}, u32[]{:S(2)}, u32[]{:S(2)}) collective-permute-start(bf16[784,128]{1,0:T(8,128)(2,1)} %get-tuple-element.71), channel_id=1, source_target_pairs={{0,24},{4,28},{8,16},{12,20},{16,8},{20,12},{24,0},{28,4},{1,25},{... | collective-permute-start | bytes 602120 | tf_op jit(solution)/shard_map/ppermute | solution.py:40
  9.2 17.3 %collective-permute-start.1 = (bf16[784,128]{1,0:T(8,128)(2,1)}, bf16[784,128]{1,0:T(8,128)(2,1)S(1)}, u32[]{:S(2)}, u32[]{:S(2)}) collective-permute-start(bf16[784,128]{1,0:T(8,128)(2,1)} %get-tuple-element.70), channel_id=1, source_target_pairs={{0,16},{4,20},{8,24},{12,28},{16,0},{20,4},{24,8},{28,12},{1,17},{... | collective-permute-start | bytes 602120 | tf_op jit(solution)/shard_map/ppermute | solution.py:40
  9.2 17.3 %collective-permute-start = (bf16[784,128]{1,0:T(8,128)(2,1)}, bf16[784,128]{1,0:T(8,128)(2,1)S(1)}, u32[]{:S(2)}, u32[]{:S(2)}) collective-permute-start(bf16[784,128]{1,0:T(8,128)(2,1)} %get-tuple-element.69), channel_id=1, source_target_pairs={{0,8},{4,12},{8,0},{12,4},{16,24},{20,28},{24,16},{28,20},{1,9},{5... | collective-permute-start | bytes 602120 | tf_op jit(solution)/shard_map/ppermute | solution.py:40
  9.8 18.3 %collective-permute-start.5 = (bf16[320,512]{1,0:T(8,128)(2,1)}, bf16[320,512]{1,0:T(8,128)(2,1)S(1)}, u32[]{:S(2)}, u32[]{:S(2)}) collective-permute-start(bf16[320,512]{1,0:T(8,128)(2,1)} %get-tuple-element.79), channel_id=1, source_target_pairs={{0,4},{4,0},{8,12},{12,8},{16,20},{20,16},{24,28},{28,24},{1,5},{5... | collective-permute-start | bytes 983048 | tf_op jit(solution)/shard_map/ppermute | solution.py:40
  26.5 13.0 %collective-permute-start.4 = (bf16[1536,128]{1,0:T(8,128)(2,1)S(1)}, bf16[1536,128]{1,0:T(8,128)(2,1)S(1)}, u32[]{:S(2)}, u32[]{:S(2)}) collective-permute-start(bf16[1536,128]{1,0:T(8,128)(2,1)S(1)} %pad_maximum_fusion), channel_id=1, source_target_pairs={{0,4},{4,0},{8,12},{12,8},{16,20},{20,16},{24,28},{28,24},{1,5},{5... | collective-permute-start | bytes 1179656 | tf_op jit(solution)/shard_map/ppermute | solution.py:40
  29.1 15.2 %collective-permute-start.6 = (bf16[160,512]{1,0:T(8,128)(2,1)S(1)}, bf16[160,512]{1,0:T(8,128)(2,1)S(1)}, u32[]{:S(2)}, u32[]{:S(2)}) collective-permute-start(bf16[160,512]{1,0:T(8,128)(2,1)S(1)} %get-tuple-element.81), channel_id=1, source_target_pairs={{0,8},{4,12},{8,0},{12,4},{16,24},{20,28},{24,16},{28,20},{1,9},{5... | collective-permute-start | bytes 491528 | tf_op jit(solution)/shard_map/ppermute | solution.py:40
  29.2 15.1 %collective-permute-start.7 = (bf16[160,512]{1,0:T(8,128)(2,1)S(1)}, bf16[160,512]{1,0:T(8,128)(2,1)S(1)}, u32[]{:S(2)}, u32[]{:S(2)}) collective-permute-start(bf16[160,512]{1,0:T(8,128)(2,1)S(1)} %get-tuple-element.82), channel_id=1, source_target_pairs={{0,16},{4,20},{8,24},{12,28},{16,0},{20,4},{24,8},{28,12},{1,17},{... | collective-permute-start | bytes 491528 | tf_op jit(solution)/shard_map/ppermute | solution.py:40
  32.2 12.1 %collective-permute-start.8 = (bf16[160,512]{1,0:T(8,128)(2,1)S(1)}, bf16[160,512]{1,0:T(8,128)(2,1)S(1)}, u32[]{:S(2)}, u32[]{:S(2)}) collective-permute-start(bf16[160,512]{1,0:T(8,128)(2,1)S(1)} %get-tuple-element.83), channel_id=1, source_target_pairs={{0,24},{4,28},{8,16},{12,20},{16,8},{20,12},{24,0},{28,4},{1,25},{... | collective-permute-start | bytes 491528 | tf_op jit(solution)/shard_map/ppermute | solution.py:40
  44.4 17.8 %collective-permute-start.9 = (bf16[640,512]{1,0:T(8,128)(2,1)S(1)}, bf16[640,512]{1,0:T(8,128)(2,1)S(1)}, u32[]{:S(2)}, u32[]{:S(2)}) collective-permute-start(bf16[640,512]{1,0:T(8,128)(2,1)S(1)} %shard_map.132.refs_1_), channel_id=1, source_target_pairs={{0,2},{1,3},{2,0},{3,1},{4,6},{5,7},{6,4},{7,5},{8,10},{9,11},{10,... | collective-permute-start | bytes 1966088 | tf_op jit(solution)/shard_map/ppermute | solution.py:40
  46.5 7.1 %collective-permute-start.10 = (bf16[640,128]{1,0:T(8,128)(2,1)S(1)}, bf16[640,128]{1,0:T(8,128)(2,1)S(1)}, u32[]{:S(2)}, u32[]{:S(2)}) collective-permute-start(bf16[640,128]{1,0:T(8,128)(2,1)S(1)} %get-tuple-element.85), channel_id=1, source_target_pairs={{0,8},{4,12},{8,0},{12,4},{16,24},{20,28},{24,16},{28,20},{1,9},{5... | collective-permute-start | bytes 491528 | tf_op jit(solution)/shard_map/ppermute | solution.py:40
  48.5 13.7 %collective-permute-start.11 = (bf16[640,128]{1,0:T(8,128)(2,1)S(1)}, bf16[640,128]{1,0:T(8,128)(2,1)S(1)}, u32[]{:S(2)}, u32[]{:S(2)}) collective-permute-start(bf16[640,128]{1,0:T(8,128)(2,1)S(1)} %get-tuple-element.86), channel_id=1, source_target_pairs={{0,16},{4,20},{8,24},{12,28},{16,0},{20,4},{24,8},{28,12},{1,17},{... | collective-permute-start | bytes 491528 | tf_op jit(solution)/shard_map/ppermute | solution.py:40
  49.4 12.8 %collective-permute-start.12 = (bf16[640,128]{1,0:T(8,128)(2,1)S(1)}, bf16[640,128]{1,0:T(8,128)(2,1)S(1)}, u32[]{:S(2)}, u32[]{:S(2)}) collective-permute-start(bf16[640,128]{1,0:T(8,128)(2,1)S(1)} %get-tuple-element.87), channel_id=1, source_target_pairs={{0,24},{4,28},{8,16},{12,20},{16,8},{20,12},{24,0},{28,4},{1,25},{... | collective-permute-start | bytes 491528 | tf_op jit(solution)/shard_map/ppermute | solution.py:40
  51.0 12.6 %collective-permute-start.13 = (bf16[640,512]{1,0:T(8,128)(2,1)S(1)}, bf16[640,512]{1,0:T(8,128)(2,1)S(1)}, u32[]{:S(2)}, u32[]{:S(2)}) collective-permute-start(bf16[640,512]{1,0:T(8,128)(2,1)S(1)} %shard_map.132.refs_1_), channel_id=1, source_target_pairs={{0,1},{1,0},{2,3},{3,2},{4,5},{5,4},{6,7},{7,6},{8,9},{9,8},{10,11... | collective-permute-start | bytes 1966088 | tf_op jit(solution)/shard_map/ppermute | solution.py:40
  62.4 10.1 %collective-permute-start.15 = (bf16[320,512]{1,0:T(8,128)(2,1)S(1)}, bf16[320,512]{1,0:T(8,128)(2,1)S(1)}, u32[]{:S(2)}, u32[]{:S(2)}) collective-permute-start(bf16[320,512]{1,0:T(8,128)(2,1)S(1)} %get-tuple-element.90), channel_id=1, source_target_pairs={{0,4},{4,0},{8,12},{12,8},{16,20},{20,16},{24,28},{28,24},{1,5},{5... | collective-permute-start | bytes 983048 | tf_op jit(solution)/shard_map/ppermute | solution.py:40
  63.0 15.0 %collective-permute-start.18 = (bf16[320,512]{1,0:T(8,128)(2,1)S(1)}, bf16[320,512]{1,0:T(8,128)(2,1)S(1)}, u32[]{:S(2)}, u32[]{:S(2)}) collective-permute-start(bf16[320,512]{1,0:T(8,128)(2,1)S(1)} %get-tuple-element.88.refs_1_), channel_id=1, source_target_pairs={{0,2},{1,3},{2,0},{3,1},{4,6},{5,7},{6,4},{7,5},{8,10},{9,11},{10,... | collective-permute-start | bytes 983048 | tf_op jit(solution)/shard_map/ppermute | solution.py:40
  72.6 10.6 %collective-permute-start.22 = (bf16[320,512]{1,0:T(8,128)(2,1)S(1)}, bf16[320,512]{1,0:T(8,128)(2,1)S(1)}, u32[]{:S(2)}, u32[]{:S(2)}) collective-permute-start(bf16[320,512]{1,0:T(8,128)(2,1)S(1)} %shard_map.137.refs_0_.refs_2_), channel_id=1, source_target_pairs={{0,2},{1,3},{2,0},{3,1},{4,6},{5,7},{6,4},{7,5},{8,10},{9,11},{10,... | collective-permute-start | bytes 983048 | tf_op jit(solution)/shard_map/ppermute | solution.py:40
  75.6 7.5 %collective-permute-start.20 = (bf16[256,128]{1,0:T(8,128)(2,1)S(1)}, bf16[256,128]{1,0:T(8,128)(2,1)S(1)}, u32[]{:S(2)}, u32[]{:S(2)}) collective-permute-start(bf16[256,128]{1,0:T(8,128)(2,1)S(1)} %get-tuple-element.92), channel_id=1, source_target_pairs={{0,16},{4,20},{8,24},{12,28},{16,0},{20,4},{24,8},{28,12},{1,17},{... | collective-permute-start | bytes 196616 | tf_op jit(solution)/shard_map/ppermute | solution.py:40
  94.4 10.3 %collective-permute-start.25 = (bf16[640,512]{1,0:T(8,128)(2,1)S(1)}, bf16[640,512]{1,0:T(8,128)(2,1)S(1)}, u32[]{:S(2)}, u32[]{:S(2)}) collective-permute-start(bf16[640,512]{1,0:T(8,128)(2,1)S(1)} %shard_map.143), channel_id=1, source_target_pairs={{0,1},{1,0},{2,3},{3,2},{4,5},{5,4},{6,7},{7,6},{8,9},{9,8},{10,11... | collective-permute-start | bytes 1966088 | tf_op jit(solution)/shard_map/ppermute | solution.py:40
  96.7 10.6 %collective-permute-start.27 = (bf16[320,512]{1,0:T(8,128)(2,1)S(1)}, bf16[320,512]{1,0:T(8,128)(2,1)S(1)}, u32[]{:S(2)}, u32[]{:S(2)}) collective-permute-start(bf16[320,512]{1,0:T(8,128)(2,1)S(1)} %get-tuple-element.101), channel_id=1, source_target_pairs={{0,2},{1,3},{2,0},{3,1},{4,6},{5,7},{6,4},{7,5},{8,10},{9,11},{10,... | collective-permute-start | bytes 983048 | tf_op jit(solution)/shard_map/ppermute | solution.py:40
  98.3 15.2 %collective-permute-start.31 = (bf16[320,512]{1,0:T(8,128)(2,1)S(1)}, bf16[320,512]{1,0:T(8,128)(2,1)S(1)}, u32[]{:S(2)}, u32[]{:S(2)}) collective-permute-start(bf16[320,512]{1,0:T(8,128)(2,1)S(1)} %get-tuple-element.107), channel_id=1, source_target_pairs={{0,2},{1,3},{2,0},{3,1},{4,6},{5,7},{6,4},{7,5},{8,10},{9,11},{10,... | collective-permute-start | bytes 983048 | tf_op jit(solution)/shard_map/ppermute | solution.py:40
  108.3 8.2 %collective-permute-start.29 = (bf16[320,128]{1,0:T(8,128)(2,1)S(1)}, bf16[320,128]{1,0:T(8,128)(2,1)S(1)}, u32[]{:S(2)}, u32[]{:S(2)}) collective-permute-start(bf16[320,128]{1,0:T(8,128)(2,1)S(1)} %get-tuple-element.104), channel_id=1, source_target_pairs={{0,16},{4,20},{8,24},{12,28},{16,0},{20,4},{24,8},{28,12},{1,17},{... | collective-permute-start | bytes 245768 | tf_op jit(solution)/shard_map/ppermute | solution.py:40
  116.7 12.7 %collective-permute-start.32 = (bf16[320,128]{1,0:T(8,128)(2,1)S(1)}, bf16[320,128]{1,0:T(8,128)(2,1)S(1)}, u32[]{:S(2)}, u32[]{:S(2)}) collective-permute-start(bf16[320,128]{1,0:T(8,128)(2,1)S(1)} %get-tuple-element.108), channel_id=1, source_target_pairs={{0,4},{4,0},{8,12},{12,8},{16,20},{20,16},{24,28},{28,24},{1,5},{5... | collective-permute-start | bytes 245768 | tf_op jit(solution)/shard_map/ppermute | solution.py:40
  117.5 11.9 %collective-permute-start.33 = (bf16[320,128]{1,0:T(8,128)(2,1)S(1)}, bf16[320,128]{1,0:T(8,128)(2,1)S(1)}, u32[]{:S(2)}, u32[]{:S(2)}) collective-permute-start(bf16[320,128]{1,0:T(8,128)(2,1)S(1)} %get-tuple-element.109), channel_id=1, source_target_pairs={{0,12},{4,8},{8,4},{12,0},{16,28},{20,24},{24,20},{28,16},{1,13},{... | collective-permute-start | bytes 245768 | tf_op jit(solution)/shard_map/ppermute | solution.py:40
  119.6 9.8 %collective-permute-start.34 = (bf16[320,128]{1,0:T(8,128)(2,1)S(1)}, bf16[320,128]{1,0:T(8,128)(2,1)S(1)}, u32[]{:S(2)}, u32[]{:S(2)}) collective-permute-start(bf16[320,128]{1,0:T(8,128)(2,1)S(1)} %get-tuple-element.110), channel_id=1, source_target_pairs={{0,20},{4,16},{8,28},{12,24},{16,4},{20,0},{24,12},{28,8},{1,21},{... | collective-permute-start | bytes 245768 | tf_op jit(solution)/shard_map/ppermute | solution.py:40
  120.9 8.5 %collective-permute-start.35 = (bf16[320,128]{1,0:T(8,128)(2,1)S(1)}, bf16[320,128]{1,0:T(8,128)(2,1)S(1)}, u32[]{:S(2)}, u32[]{:S(2)}) collective-permute-start(bf16[320,128]{1,0:T(8,128)(2,1)S(1)} %get-tuple-element.111), channel_id=1, source_target_pairs={{0,28},{4,24},{8,20},{12,16},{16,12},{20,8},{24,4},{28,0},{1,29},{... | collective-permute-start | bytes 245768 | tf_op jit(solution)/shard_map/ppermute | solution.py:40
  133.8 7.3 %collective-permute-start.39 = (bf16[1024,128]{1,0:T(8,128)(2,1)S(1)}, bf16[1024,128]{1,0:T(8,128)(2,1)S(1)}, u32[]{:S(2)}, u32[]{:S(2)}) collective-permute-start(bf16[1024,128]{1,0:T(8,128)(2,1)S(1)} %get-tuple-element.123), channel_id=1, source_target_pairs={{0,4},{4,0},{8,12},{12,8},{16,20},{20,16},{24,28},{28,24},{1,5},{5... | collective-permute-start | bytes 786440 | tf_op jit(solution)/shard_map/ppermute | solution.py:40
  134.6 9.3 %collective-permute-start.43 = (bf16[1024,128]{1,0:T(8,128)(2,1)S(1)}, bf16[1024,128]{1,0:T(8,128)(2,1)S(1)}, u32[]{:S(2)}, u32[]{:S(2)}) collective-permute-start(bf16[1024,128]{1,0:T(8,128)(2,1)S(1)} %get-tuple-element.125), channel_id=1, source_target_pairs={{0,4},{4,0},{8,12},{12,8},{16,20},{20,16},{24,28},{28,24},{1,5},{5... | collective-permute-start | bytes 786440 | tf_op jit(solution)/shard_map/ppermute | solution.py:40
  135.9 9.3 %collective-permute-start.36 = (bf16[256,128]{1,0:T(8,128)(2,1)S(1)}, bf16[256,128]{1,0:T(8,128)(2,1)S(1)}, u32[]{:S(2)}, u32[]{:S(2)}) collective-permute-start(bf16[256,128]{1,0:T(8,128)(2,1)S(1)} %get-tuple-element.119), channel_id=1, source_target_pairs={{0,8},{4,12},{8,0},{12,4},{16,24},{20,28},{24,16},{28,20},{1,9},{5... | collective-permute-start | bytes 196616 | tf_op jit(solution)/shard_map/ppermute | solution.py:40
  136.5 10.6 %collective-permute-start.37 = (bf16[256,128]{1,0:T(8,128)(2,1)S(1)}, bf16[256,128]{1,0:T(8,128)(2,1)S(1)}, u32[]{:S(2)}, u32[]{:S(2)}) collective-permute-start(bf16[256,128]{1,0:T(8,128)(2,1)S(1)} %get-tuple-element.120), channel_id=1, source_target_pairs={{0,16},{4,20},{8,24},{12,28},{16,0},{20,4},{24,8},{28,12},{1,17},{... | collective-permute-start | bytes 196616 | tf_op jit(solution)/shard_map/ppermute | solution.py:40
  138.5 9.1 %collective-permute-start.38 = (bf16[256,128]{1,0:T(8,128)(2,1)S(1)}, bf16[256,128]{1,0:T(8,128)(2,1)S(1)}, u32[]{:S(2)}, u32[]{:S(2)}) collective-permute-start(bf16[256,128]{1,0:T(8,128)(2,1)S(1)} %get-tuple-element.121), channel_id=1, source_target_pairs={{0,24},{4,28},{8,16},{12,20},{16,8},{20,12},{24,0},{28,4},{1,25},{... | collective-permute-start | bytes 196616 | tf_op jit(solution)/shard_map/ppermute | solution.py:40
  141.2 8.5 %collective-permute-start.40 = (bf16[256,128]{1,0:T(8,128)(2,1)S(1)}, bf16[256,128]{1,0:T(8,128)(2,1)S(1)}, u32[]{:S(2)}, u32[]{:S(2)}) collective-permute-start(bf16[256,128]{1,0:T(8,128)(2,1)S(1)} %get-tuple-element.137), channel_id=1, source_target_pairs={{0,8},{4,12},{8,0},{12,4},{16,24},{20,28},{24,16},{28,20},{1,9},{5... | collective-permute-start | bytes 196616 | tf_op jit(solution)/shard_map/ppermute | solution.py:40
  143.9 7.8 %collective-permute-start.41 = (bf16[256,128]{1,0:T(8,128)(2,1)S(1)}, bf16[256,128]{1,0:T(8,128)(2,1)S(1)}, u32[]{:S(2)}, u32[]{:S(2)}) collective-permute-start(bf16[256,128]{1,0:T(8,128)(2,1)S(1)} %get-tuple-element.136), channel_id=1, source_target_pairs={{0,16},{4,20},{8,24},{12,28},{16,0},{20,4},{24,8},{28,12},{1,17},{... | collective-permute-start | bytes 196616 | tf_op jit(solution)/shard_map/ppermute | solution.py:40
  (21 other events, 182.2 us)

commit v4 on v3

--- a/solution.py
+++ b/solution.py
@@ -372,15 +372,18 @@
             refs[-1][at] = refs[dg][dr * stride : (dr + 1) * stride]
 
 
-def turn_back_body(sizes, near, arrived, *outs):
+def turn_back_body(sizes, start, arrived, *refs):
     G, R, count = sizes
     g = lax.axis_index("seq") // R
-    each = len(outs) // G
+    each = arrived.shape[0] // count
+    near, outs = refs[: len(refs) - G * each], refs[len(refs) - G * each :]
     for dg in range(G):
         cols = pl.ds(pl.multiple_of((g ^ dg) * HD, HD), HD)
         for at in range(each):
-            rows = slice(at * count, (at + 1) * count)
-            outs[dg * each + at][...] = (near[rows, cols] + arrived[rows, cols].astype(F32)).astype(BF16)
+            total = arrived[at * count : (at + 1) * count, cols].astype(F32)
+            for piece in near:
+                total = total + piece[start + at * count : start + (at + 1) * count, cols].astype(F32)
+            outs[dg * each + at][...] = total.astype(BF16)
 
 
 def keep_moves(parts, first, shards, full, sems):
@@ -426,7 +429,10 @@
 
 
 def pre_body(parts, weight, *refs):
-    shards, through, full, hidden, hidden_grad, held, sems, own_sems = refs[:-7], *refs[-7:]
+    held, sems, own_sems = refs[-3:]
+    count = (len(refs) - 7) // (parts + 1)
+    shards, refs = refs[: count * parts], refs[count * parts : -3]
+    through, full, hidden, hidden_grad, back = *refs[:4], refs[4:]
     place = lax.axis_index("exp")
     rows, width = shards[0].shape
     steps = sems.shape[0]
@@ -438,11 +444,12 @@
 
     for c in range(min(2, steps)):
         fetch(c).start()
-    for move in kept:
-        move.start()
     for c in range(steps):
         cols = slice(c * wide, (c + 1) * wide)
         fetch(c).wait()
+        if c == 0:
+            for move in kept:
+                move.start()
         if c + 2 < steps:
             fetch(c + 2).start()
         for h in range(parts):
@@ -456,18 +463,22 @@
             hidden[mine, cols] = (total * logistic).astype(BF16)
             grad = through[mine, cols] * logistic * (1.0 + total * (1.0 - logistic))
             hidden_grad[mine, cols] = grad.astype(BF16)
+    for k, out in enumerate(back):
+        at = pl.ds(pl.multiple_of((place ^ k) * width, 128), width)
+        total = None
+        for c in range(steps):
+            part = rows_by_rows(hidden_grad[:, c * wide : (c + 1) * wide], held[c, at, :])
+            total = part if total is None else total + part
+        out[...] = total.astype(out.dtype)
     for move in kept:
         move.wait()
 
 
-def back_body(added, place, grad, weight, *refs):
-    part = rows_by_rows(grad[...], weight[...])
-    if added:
-        part = part + refs[0][...].astype(F32)
-    outs = refs[added:]
-    rows = part.shape[0] // len(outs)
+def far_body(kept, moved, *outs):
+    rows = outs[0].shape[0]
     for h, out in enumerate(outs):
-        out[...] = part[h * rows : (h + 1) * rows].astype(out.dtype)
+        mine = slice(h * rows, (h + 1) * rows)
+        out[...] = (kept[mine] + moved[mine].astype(F32)).astype(BF16)
 
 
 def weight_grad_body(place, left, right, out, mark):
@@ -630,9 +641,11 @@
     near_shards = [near_shards[h][k] for k in range(half) for h in range(parts)]
     far_shards = [gather_exp(part, half) for part in far_parts]
     far_shards = [far_shards[h][k] for k in range(half) for h in range(parts)]
-    full_tokens, hidden, hidden_grad = local_call(
+    full_tokens, hidden, hidden_grad, *back = local_call(
         functools.partial(pre_body, parts),
-        [((rows, E * features), BF16, pltpu.HBM)] + [((rows, FFL), BF16)] * 2,
+        [((rows, E * features), BF16, pltpu.HBM)]
+        + [((rows, FFL), BF16)] * 2
+        + [((rows, features), BF16 if k % 2 else F32) for k in range(E)],
         near_shards + far_shards + [through],
         far=[weight_in],
         scratch=[
@@ -640,37 +653,27 @@
             pltpu.SemaphoreType.DMA((steps,)),
             pltpu.SemaphoreType.DMA((E * parts,)),
         ],
-        flops=work * E,
+        flops=2 * work * E,
         nbytes=8 * MIB,
-    )
-
-    def back_part(k, moved, count, dtype):
-        piece = min(256, features)
-        per = features // piece
-        added = [] if moved is None else [(moved, (rows, piece), lambda j, p: (0, j))]
-        return grid_call(
-            functools.partial(back_body, len(added)),
-            per,
-            place,
-            [whole(hidden_grad), (weight_in, (piece, FFL), lambda j, p: ((p[0] ^ k) * per + j, 0))] + added,
-            [((rows // count, features), dtype, (rows // count, piece), lambda j, p: (0, j))] * count,
-            flops=work,
-            nbytes=3 * MIB,
-        )
-
-    def summed(first, dtype):
-        moved = [swap(back_part(k + 1, None, 1, BF16)[0], "exp", 1) for k in range(first, first + half, 2)]
-        return [back_part(first + 2 * at, piece, parts, dtype) for at, piece in enumerate(moved)]
-
-    far = summed(half, BF16)
+        limit=20 * MIB,
+    )
+
+    moved = [swap(back[k], "exp", 1) for k in range(1, E, 2)]
+    kept = back[::2]
+    pairs = half // 2
+    far = [
+        local_call(far_body, [((tall, features), BF16)] * parts, [kept[k], moved[k]], nbytes=rows * features * 8)
+        for k in range(pairs, 2 * pairs)
+    ]
     arrived = [[swap(piece[h], "exp", half) for h in range(parts)] for piece in far]
-    near = summed(0, F32)
+    near = [[kept[k], moved[k]] for k in range(pairs)]
     distance = half // 2
     while len(near) > 1:
         count = len(near) // 2
-        total = [[near[k][h] + arrived[k][h].astype(F32) for h in range(parts)] for k in range(2 * count)]
-        arrived = [[swap(total[count + k][h].astype(BF16), "exp", distance) for h in range(parts)] for k in range(count)]
-        near = total[:count]
+        total = [sum(x.astype(F32) for x in near[k]) + jnp.concatenate(arrived[k], axis=0) for k in range(2 * count)]
+        sent = [total[count + k].astype(BF16) for k in range(count)]
+        arrived = [[swap(x[h * tall : (h + 1) * tall], "exp", distance) for h in range(parts)] for x in sent]
+        near = [[x] for x in total[:count]]
         distance //= 2
 
     mark_out = ((8, 128), F32, (8, 128), lambda j, p: (0, 0))
@@ -687,9 +690,9 @@
     ready = [out_mark]
     for h in range(parts):
         pieces = local_call(
-            functools.partial(turn_back_body, (G, R, G * stride)),
+            functools.partial(turn_back_body, (G, R, G * stride), h * tall),
             [((G * stride, HD), BF16)] * (G * each),
-            [near[0][h], arrived[0][h]],
+            [arrived[0][h]] + near[0],
             after=ready,
             nbytes=tall * features * 8,
         )
@@ -697,7 +700,7 @@
             for at in range(each):
                 d = dg * R + h * each + at
                 returned[d] = swap(pieces[dg * each + at], "seq", d)
-        ready = [x for x in returned[1:] if x is not None]
+        ready = returned[R : R + 1]
     in_weight_grad, in_mark = grid_call(
         weight_grad_body,
         E,

time: 157 us -> 155 us (0.987)
  Pallas kernels: 47.1 us -> 42.5 us
  starting transfers between devices: 56.1 us -> 60 us
  waiting for transfers between devices: 51.4 us -> 49.7 us
    pallas_call x6 -> x2, Pallas kernels: 19.4 us -> 11.7 us  [grid_call(): pl.pallas_call(kernel, out_shape=[jax.ShapeDtypeStruct(shape, dtype) for...]
    ppermute x47, starting transfers between devices: 56.1 us -> 60 us  [swap(): return lax.ppermute(block, axis, [(i, i ^ distance) for i in devices])]
    pallas_call x15 -> x16, Pallas kernels: 27.7 us -> 30.8 us  [local_call(): pl.pallas_call(kernel, out_shape=[jax.ShapeDtypeStruct(x[0], x[1]) for x...]
    ppermute x47, waiting for transfers between devices: 51.4 us -> 49.7 us  [swap(): return lax.ppermute(block, axis, [(i, i ^ distance) for i in devices])]
  transfers between devices with their start and end apart: 47 -> 47, of which waited for: 19 -> 20; matrix products, arithmetic and copies ran while one was open for 0% -> 0% of each run, Pallas kernels for 20% -> 17%
where the time goes in v4:
time: 155 us; the launch traced here: 154 us
  starting transfers between devices  60 us (39%)
  waiting for transfers between devices  49.7 us (32%)
  Pallas kernels  42.5 us (27%)
    ppermute x47, starting transfers between devices, swap(): return lax.ppermute(block, axis, [(i, i ^ distance) for i in devices])  60 us
    ppermute x47, waiting for transfers between devices, swap(): return lax.ppermute(block, axis, [(i, i ^ distance) for i in devices])  49.7 us
    pallas_call x16, Pallas kernels, local_call(): pl.pallas_call(kernel, out_shape=[jax.ShapeDtypeStruct(x[0], x[1]) for x...  30.8 us
    pallas_call x2, Pallas kernels, grid_call(): pl.pallas_call(kernel, out_shape=[jax.ShapeDtypeStruct(shape, dtype) for...  11.7 us
  transfers between devices with their start and end apart: 47, of which 20 were waited for; matrix products, arithmetic and copies ran while one was open for 0% of the time, Pallas kernels for 17%

profile of v4, /device:TPU:0, one launch (start us, length us, event | category | flops | bytes accessed | tf_op | source)
XLA Modules:
  0.0 154.4 jit_solution(70279214920634092)
XLA Ops:
  0.6 3.4 %shard_map.128 = (bf16[784,128]{1,0:T(8,128)(2,1)}, bf16[784,128]{1,0:T(8,128)(2,1)}, bf16[784,128]{1,0:T(8,128)(2,1)}, bf16[784,128]{1,0:T(8,128)(2,1)}, bf16[3...) custom-call(bf16[256,512]{1,0:T(8,128)(2,1)} %refs_0_.2, bf16[256,512]{1,0:T(8,128)(2,1)} %refs_1_.2, ...), custom_call_target="tpu_custom_call" | custom-call | bytes 1572864 | tf_op jit(solution)/shard_map/pallas_call | solution.py:56
  4.1 3.1 %collective-permute-start = (bf16[784,128]{1,0:T(8,128)(2,1)}, bf16[784,128]{1,0:T(8,128)(2,1)S(1)}, u32[]{:S(2)}, u32[]{:S(2)}) collective-permute-start(bf16[784,128]{1,0:T(8,128)(2,1)} %get-tuple-element.71), channel_id=1, source_target_pairs={{0,8},{4,12},{8,0},{12,4},{16,24},{20,28},{24,16},{28,20},{1,9},{5... | collective-permute-start | bytes 602120 | tf_op jit(solution)/shard_map/ppermute | solution.py:40
  7.2 2.6 %collective-permute-start.1 = (bf16[784,128]{1,0:T(8,128)(2,1)}, bf16[784,128]{1,0:T(8,128)(2,1)S(1)}, u32[]{:S(2)}, u32[]{:S(2)}) collective-permute-start(bf16[784,128]{1,0:T(8,128)(2,1)} %get-tuple-element.72), channel_id=1, source_target_pairs={{0,16},{4,20},{8,24},{12,28},{16,0},{20,4},{24,8},{28,12},{1,17},{... | collective-permute-start | bytes 602120 | tf_op jit(solution)/shard_map/ppermute | solution.py:40
  9.8 1.7 %collective-permute-start.5 = (bf16[320,512]{1,0:T(8,128)(2,1)}, bf16[320,512]{1,0:T(8,128)(2,1)S(1)}, u32[]{:S(2)}, u32[]{:S(2)}) collective-permute-start(bf16[320,512]{1,0:T(8,128)(2,1)} %get-tuple-element.81), channel_id=1, source_target_pairs={{0,4},{4,0},{8,12},{12,8},{16,20},{20,16},{24,28},{28,24},{1,5},{5... | collective-permute-start | bytes 983048 | tf_op jit(solution)/shard_map/ppermute | solution.py:40
  11.5 4.4 %collective-permute-done.refs_2_.refs_1_.refs_0_ = bf16[784,128]{1,0:T(8,128)(2,1)S(1)} collective-permute-done((bf16[784,128]{1,0:T(8,128)(2,1)}, bf16[784,128]{1,0:T(8,128)(2,1)S(1)}, u32[]{:S(2)}, u32[]{:S(2)}) %collective-permute-start) | collective-permute-done | bytes 200736 | tf_op jit(solution)/shard_map/ppermute | solution.py:40
  15.9 8.9 %collective-permute-done.1.refs_3_.refs_2_.refs_1_ = bf16[784,128]{1,0:T(8,128)(2,1)S(1)} collective-permute-done((bf16[784,128]{1,0:T(8,128)(2,1)}, bf16[784,128]{1,0:T(8,128)(2,1)S(1)}, u32[]{:S(2)}, u32[]{:S(2)}) %collective-permute-start.1) | collective-permute-done | bytes 200736 | tf_op jit(solution)/shard_map/ppermute | solution.py:40
  27.5 3.5 %collective-permute-start.6 = (bf16[160,512]{1,0:T(8,128)(2,1)S(1)}, bf16[160,512]{1,0:T(8,128)(2,1)S(1)}, u32[]{:S(2)}, u32[]{:S(2)}) collective-permute-start(bf16[160,512]{1,0:T(8,128)(2,1)S(1)} %get-tuple-element.83), channel_id=1, source_target_pairs={{0,8},{4,12},{8,0},{12,4},{16,24},{20,28},{24,16},{28,20},{1,9},{5... | collective-permute-start | bytes 491528 | tf_op jit(solution)/shard_map/ppermute | solution.py:40
  35.1 3.4 %collective-permute-done.3.refs_5_ = bf16[512,128]{1,0:T(8,128)(2,1)S(1)} collective-permute-done((bf16[512,128]{1,0:T(8,128)(2,1)S(1)}, bf16[512,128]{1,0:T(8,128)(2,1)S(1)}, u32[]{:S(2)}, u32[]{:S(2)}) %collective-permute-start.3) | collective-permute-done | bytes 131104 | tf_op jit(solution)/shard_map/ppermute | solution.py:40
  38.5 4.7 %shard_map.129 = (bf16[256,512]{1,0:T(8,128)(2,1)S(1)}, bf16[256,1024]{1,0:T(8,128)(2,1)S(1)}, bf16[256,1536]{1,0:T(8,128)(2,1)S(1)}, bf16[256,2048]{1,0:T(8,128...) custom-call(f32[4]{0:T(128)S(1)} %copy-done.3, ...), custom_call_target="tpu_custom_call" | custom-call | tf_op jit(solution)/shard_map/pallas_call | solution.py:56
  43.2 1.7 %collective-permute-done.7.refs_4_ = bf16[160,512]{1,0:T(8,128)(2,1)S(1)} collective-permute-done((bf16[160,512]{1,0:T(8,128)(2,1)S(1)}, bf16[160,512]{1,0:T(8,128)(2,1)S(1)}, u32[]{:S(2)}, u32[]{:S(2)}) %collective-permute-start.7) | collective-permute-done | bytes 163872 | tf_op jit(solution)/shard_map/ppermute | solution.py:40
  45.0 1.6 %collective-permute-start.9 = (bf16[640,512]{1,0:T(8,128)(2,1)S(1)}, bf16[640,512]{1,0:T(8,128)(2,1)S(1)}, u32[]{:S(2)}, u32[]{:S(2)}) collective-permute-start(bf16[640,512]{1,0:T(8,128)(2,1)S(1)} %shard_map.132.refs_1_), channel_id=1, source_target_pairs={{0,2},{1,3},{2,0},{3,1},{4,6},{5,7},{6,4},{7,5},{8,10},{9,11},{10,... | collective-permute-start | bytes 1966088 | tf_op jit(solution)/shard_map/ppermute | solution.py:40
  47.1 2.4 %collective-permute-start.10 = (bf16[640,128]{1,0:T(8,128)(2,1)S(1)}, bf16[640,128]{1,0:T(8,128)(2,1)S(1)}, u32[]{:S(2)}, u32[]{:S(2)}) collective-permute-start(bf16[640,128]{1,0:T(8,128)(2,1)S(1)} %get-tuple-element.87), channel_id=1, source_target_pairs={{0,8},{4,12},{8,0},{12,4},{16,24},{20,28},{24,16},{28,20},{1,9},{5... | collective-permute-start | bytes 491528 | tf_op jit(solution)/shard_map/ppermute | solution.py:40
  51.9 2.2 %collective-permute-done.10.refs_2_.refs_0_ = bf16[640,128]{1,0:T(8,128)(2,1)S(1)} collective-permute-done((bf16[640,128]{1,0:T(8,128)(2,1)S(1)}, bf16[640,128]{1,0:T(8,128)(2,1)S(1)}, u32[]{:S(2)}, u32[]{:S(2)}) %collective-permute-start.10) | collective-permute-done | bytes 163872 | tf_op jit(solution)/shard_map/ppermute | solution.py:40
  54.1 8.9 %collective-permute-done.11.refs_3_.refs_1_ = bf16[640,128]{1,0:T(8,128)(2,1)S(1)} collective-permute-done((bf16[640,128]{1,0:T(8,128)(2,1)S(1)}, bf16[640,128]{1,0:T(8,128)(2,1)S(1)}, u32[]{:S(2)}, u32[]{:S(2)}) %collective-permute-start.11) | collective-permute-done | bytes 163872 | tf_op jit(solution)/shard_map/ppermute | solution.py:40
  65.3 6.9 %shard_map.136 = (f32[640,1024]{1,0:T(8,128)S(1)}, bf16[640,2048]{1,0:T(8,128)(2,1)S(1)}) custom-call(bf16[1024,2048]{1,0:T(8,128)(2,1)S(1)} %bitcast.6, bf16[640,512]{1,0:T(8,128)(2,1)S(1)} %shard_map.132.refs_1_, bf16[640,512]{1,0:T(8,128)(2,1)S(1)} %collective-permute-done.13.refs_2_, bf16[640,512]{1,0:T(8,128)(2,1)S(1)} %shard_map.135.refs_3_, ...), custom_call_target="tpu_custom_call" | custom-call | flops 2684354560 | bytes 10485760 | tf_op jit(solution)/shard_map/pallas_call | solution.py:56
  74.0 2.4 %collective-permute-start.19 = (bf16[256,128]{1,0:T(8,128)(2,1)S(1)}, bf16[256,128]{1,0:T(8,128)(2,1)S(1)}, u32[]{:S(2)}, u32[]{:S(2)}) collective-permute-start(bf16[256,128]{1,0:T(8,128)(2,1)S(1)} %get-tuple-element.93), channel_id=1, source_target_pairs={{0,8},{4,12},{8,0},{12,4},{16,24},{20,28},{24,16},{28,20},{1,9},{5... | collective-permute-start | bytes 196616 | tf_op jit(solution)/shard_map/ppermute | solution.py:40
  79.6 4.5 %collective-permute-done.20.refs_1_.refs_11_ = bf16[256,128]{1,0:T(8,128)(2,1)S(1)} collective-permute-done((bf16[256,128]{1,0:T(8,128)(2,1)S(1)}, bf16[256,128]{1,0:T(8,128)(2,1)S(1)}, u32[]{:S(2)}, u32[]{:S(2)}) %collective-permute-start.20) | collective-permute-done | bytes 65568 | tf_op jit(solution)/shard_map/ppermute | solution.py:40
  86.2 8.0 %shard_map.140 = (bf16[640,2048]{1,0:T(8,128)(2,1)S(1)}, bf16[640,1024]{1,0:T(8,128)(2,1)S(1)}, bf16[640,1024]{1,0:T(8,128)(2,1)S(1)}, f32[640,512]{1,0:T(8,128)...) custom-call(bf16[2048,1024]{1,0:T(8,128)(2,1)S(1)} %bitcast.7, ...), custom_call_target="tpu_custom_call" | custom-call | flops 5368709120 | bytes 8388608 | tf_op jit(solution)/shard_map/pallas_call | solution.py:56
  98.6 5.9 %shard_map.142 = (bf16[1024,2048]{1,0:T(8,128)(2,1)}, f32[8,128]{1,0:T(8,128)S(1)}) custom-call(s32[1]{0:T(128)} %get-tuple-element.78.place, bf16[640,1024]{1,0:T(8,128)(2,1)S(1)} %get-tuple-element.99.refs_0_, bf16[640,2048]{1,0:T(8,128)(2,1)S(1)} %get-tuple-element.100.refs_1_), custom_call_target="tpu_custom_call" | custom-call | flops 2684354560 | bytes 10485760 | tf_op jit(solution)/shard_map/pallas_call | solution.py:93
  104.4 2.7 %collective-permute-done.26.refs_1_ = bf16[320,512]{1,0:T(8,128)(2,1)S(1)} collective-permute-done((bf16[320,512]{1,0:T(8,128)(2,1)S(1)}, bf16[320,512]{1,0:T(8,128)(2,1)S(1)}, u32[]{:S(2)}, u32[]{:S(2)}) %collective-permute-start.26) | collective-permute-done | bytes 327712 | tf_op jit(solution)/shard_map/ppermute | solution.py:40
  108.2 2.2 %collective-permute-start.32 = (bf16[320,128]{1,0:T(8,128)(2,1)S(1)}, bf16[320,128]{1,0:T(8,128)(2,1)S(1)}, u32[]{:S(2)}, u32[]{:S(2)}) collective-permute-start(bf16[320,128]{1,0:T(8,128)(2,1)S(1)} %get-tuple-element.112), channel_id=1, source_target_pairs={{0,16},{4,20},{8,24},{12,28},{16,0},{20,4},{24,8},{28,12},{1,17},{... | collective-permute-start | bytes 245768 | tf_op jit(solution)/shard_map/ppermute | solution.py:40
  111.7 1.6 %collective-permute-done.29.refs_1_ = bf16[320,512]{1,0:T(8,128)(2,1)S(1)} collective-permute-done((bf16[320,512]{1,0:T(8,128)(2,1)S(1)}, bf16[320,512]{1,0:T(8,128)(2,1)S(1)}, u32[]{:S(2)}, u32[]{:S(2)}) %collective-permute-start.29) | collective-permute-done | bytes 327712 | tf_op jit(solution)/shard_map/ppermute | solution.py:40
  115.8 2.3 %collective-permute-start.33 = (bf16[320,128]{1,0:T(8,128)(2,1)S(1)}, bf16[320,128]{1,0:T(8,128)(2,1)S(1)}, u32[]{:S(2)}, u32[]{:S(2)}) collective-permute-start(bf16[320,128]{1,0:T(8,128)(2,1)S(1)} %get-tuple-element.113), channel_id=1, source_target_pairs={{0,20},{4,16},{8,28},{12,24},{16,4},{20,0},{24,12},{28,8},{1,21},{... | collective-permute-start | bytes 245768 | tf_op jit(solution)/shard_map/ppermute | solution.py:40
  118.2 2.1 %collective-permute-start.35 = (bf16[320,128]{1,0:T(8,128)(2,1)S(1)}, bf16[320,128]{1,0:T(8,128)(2,1)S(1)}, u32[]{:S(2)}, u32[]{:S(2)}) collective-permute-start(bf16[320,128]{1,0:T(8,128)(2,1)S(1)} %get-tuple-element.115), channel_id=1, source_target_pairs={{0,28},{4,24},{8,20},{12,16},{16,12},{20,8},{24,4},{28,0},{1,29},{... | collective-permute-start | bytes 245768 | tf_op jit(solution)/shard_map/ppermute | solution.py:40
  120.3 5.9 %shard_map.141 = (bf16[2048,1024]{1,0:T(8,128)(2,1)}, f32[8,128]{1,0:T(8,128)S(1)}) custom-call(s32[1]{0:T(128)} %get-tuple-element.78.place, bf16[640,2048]{1,0:T(8,128)(2,1)S(1)} %get-tuple-element.96.refs_0_, bf16[640,1024]{1,0:T(8,128)(2,1)S(1)} %get-tuple-element.97.refs_1_), custom_call_target="tpu_custom_call" | custom-call | flops 2684354560 | bytes 10485760 | tf_op jit(solution)/shard_map/pallas_call | solution.py:93
  126.3 2.0 %shard_map.146 = (bf16[1024,128]{1,0:T(8,128)(2,1)S(1)}, bf16[1024,128]{1,0:T(8,128)(2,1)S(1)}, bf16[1024,128]{1,0:T(8,128)(2,1)S(1)}) custom-call(f32[8,128]{1,0:T(8,128)S(1)} %get-tuple-element.98.refs_0_, bf16[320,128]{1,0:T(8,128)(2,1)S(1)} %get-tuple-element.107.refs_1_, bf16[320,128]{1,0:T(8,128)(2,1)S(1)} %collective-permute-done.30.refs_2_, ...), custom_call_target="tpu_custom_call" | custom-call | flops 536870912 | bytes 6291456 | tf_op jit(solution)/shard_map/pallas_call | solution.py:56
  128.3 2.4 %shard_map.147 = (bf16[256,128]{1,0:T(8,128)(2,1)S(1)}, bf16[256,128]{1,0:T(8,128)(2,1)S(1)}, bf16[256,128]{1,0:T(8,128)(2,1)S(1)}, bf16[256,128]{1,0:T(8,128)(2...) custom-call(bf16[256,512]{1,0:T(8,128)(2,1)S(1)} %get-tuple-element.74.refs_13_.refs_0_, ...), custom_call_target="tpu_custom_call" | custom-call | flops 1610612736 | bytes 6291456 | tf_op jit(solution)/shard_map/pallas_call | solution.py:56
  133.1 2.7 %collective-permute-start.37 = (bf16[256,128]{1,0:T(8,128)(2,1)S(1)}, bf16[256,128]{1,0:T(8,128)(2,1)S(1)}, u32[]{:S(2)}, u32[]{:S(2)}) collective-permute-start(bf16[256,128]{1,0:T(8,128)(2,1)S(1)} %get-tuple-element.124), channel_id=1, source_target_pairs={{0,16},{4,20},{8,24},{12,28},{16,0},{20,4},{24,8},{28,12},{1,17},{... | collective-permute-start | bytes 196616 | tf_op jit(solution)/shard_map/ppermute | solution.py:40
  137.2 2.8 %collective-permute-done.39 = bf16[1024,128]{1,0:T(8,128)(2,1)S(1)} collective-permute-done((bf16[1024,128]{1,0:T(8,128)(2,1)S(1)}, bf16[1024,128]{1,0:T(8,128)(2,1)S(1)}, u32[]{:S(2)}, u32[]{:S(2)}) %collective-permute-start.39) | collective-permute-done | bytes 262176 | tf_op jit(solution)/shard_map/ppermute | solution.py:40
  140.0 2.5 %collective-permute-start.42 = (bf16[256,128]{1,0:T(8,128)(2,1)S(1)}, bf16[256,128]{1,0:T(8,128)(2,1)S(1)}, u32[]{:S(2)}, u32[]{:S(2)}) collective-permute-start(bf16[256,128]{1,0:T(8,128)(2,1)S(1)} %get-tuple-element.139), channel_id=1, source_target_pairs={{0,24},{4,28},{8,16},{12,20},{16,8},{20,12},{24,0},{28,4},{1,25},{... | collective-permute-start | bytes 196616 | tf_op jit(solution)/shard_map/ppermute | solution.py:40
  142.8 1.7 %collective-permute-start.41 = (bf16[256,128]{1,0:T(8,128)(2,1)S(1)}, bf16[256,128]{1,0:T(8,128)(2,1)S(1)}, u32[]{:S(2)}, u32[]{:S(2)}) collective-permute-start(bf16[256,128]{1,0:T(8,128)(2,1)S(1)} %get-tuple-element.140), channel_id=1, source_target_pairs={{0,16},{4,20},{8,24},{12,28},{16,0},{20,4},{24,8},{28,12},{1,17},{... | collective-permute-start | bytes 196616 | tf_op jit(solution)/shard_map/ppermute | solution.py:40
  148.2 2.1 %collective-permute-start.44 = (bf16[256,128]{1,0:T(8,128)(2,1)S(1)}, bf16[256,128]{1,0:T(8,128)(2,1)S(1)}, u32[]{:S(2)}, u32[]{:S(2)}) collective-permute-start(bf16[256,128]{1,0:T(8,128)(2,1)S(1)} %get-tuple-element.137), channel_id=1, source_target_pairs={{0,8},{4,12},{8,0},{12,4},{16,24},{20,28},{24,16},{28,20},{1,9},{5... | collective-permute-start | bytes 196616 | tf_op jit(solution)/shard_map/ppermute | solution.py:40
  (102 shorter events, 40.4 us)
Async XLA Ops:
  4.1 11.8 %collective-permute-start = (bf16[784,128]{1,0:T(8,128)(2,1)}, bf16[784,128]{1,0:T(8,128)(2,1)S(1)}, u32[]{:S(2)}, u32[]{:S(2)}) collective-permute-start(bf16[784,128]{1,0:T(8,128)(2,1)} %get-tuple-element.71), channel_id=1, source_target_pairs={{0,8},{4,12},{8,0},{12,4},{16,24},{20,28},{24,16},{28,20},{1,9},{5... | collective-permute-start | bytes 602120 | tf_op jit(solution)/shard_map/ppermute | solution.py:40
  7.2 17.6 %collective-permute-start.1 = (bf16[784,128]{1,0:T(8,128)(2,1)}, bf16[784,128]{1,0:T(8,128)(2,1)S(1)}, u32[]{:S(2)}, u32[]{:S(2)}) collective-permute-start(bf16[784,128]{1,0:T(8,128)(2,1)} %get-tuple-element.72), channel_id=1, source_target_pairs={{0,16},{4,20},{8,24},{12,28},{16,0},{20,4},{24,8},{28,12},{1,17},{... | collective-permute-start | bytes 602120 | tf_op jit(solution)/shard_map/ppermute | solution.py:40
  9.8 15.1 %collective-permute-start.2 = (bf16[784,128]{1,0:T(8,128)(2,1)}, bf16[784,128]{1,0:T(8,128)(2,1)S(1)}, u32[]{:S(2)}, u32[]{:S(2)}) collective-permute-start(bf16[784,128]{1,0:T(8,128)(2,1)} %get-tuple-element.73), channel_id=1, source_target_pairs={{0,24},{4,28},{8,16},{12,20},{16,8},{20,12},{24,0},{28,4},{1,25},{... | collective-permute-start | bytes 602120 | tf_op jit(solution)/shard_map/ppermute | solution.py:40
  9.8 16.7 %collective-permute-start.5 = (bf16[320,512]{1,0:T(8,128)(2,1)}, bf16[320,512]{1,0:T(8,128)(2,1)S(1)}, u32[]{:S(2)}, u32[]{:S(2)}) collective-permute-start(bf16[320,512]{1,0:T(8,128)(2,1)} %get-tuple-element.81), channel_id=1, source_target_pairs={{0,4},{4,0},{8,12},{12,8},{16,20},{20,16},{24,28},{28,24},{1,5},{5... | collective-permute-start | bytes 983048 | tf_op jit(solution)/shard_map/ppermute | solution.py:40
  24.9 13.6 %collective-permute-start.4 = (bf16[1536,128]{1,0:T(8,128)(2,1)S(1)}, bf16[1536,128]{1,0:T(8,128)(2,1)S(1)}, u32[]{:S(2)}, u32[]{:S(2)}) collective-permute-start(bf16[1536,128]{1,0:T(8,128)(2,1)S(1)} %pad_maximum_fusion), channel_id=1, source_target_pairs={{0,4},{4,0},{8,12},{12,8},{16,20},{20,16},{24,28},{28,24},{1,5},{5... | collective-permute-start | bytes 1179656 | tf_op jit(solution)/shard_map/ppermute | solution.py:40
  27.5 15.7 %collective-permute-start.6 = (bf16[160,512]{1,0:T(8,128)(2,1)S(1)}, bf16[160,512]{1,0:T(8,128)(2,1)S(1)}, u32[]{:S(2)}, u32[]{:S(2)}) collective-permute-start(bf16[160,512]{1,0:T(8,128)(2,1)S(1)} %get-tuple-element.83), channel_id=1, source_target_pairs={{0,8},{4,12},{8,0},{12,4},{16,24},{20,28},{24,16},{28,20},{1,9},{5... | collective-permute-start | bytes 491528 | tf_op jit(solution)/shard_map/ppermute | solution.py:40
  30.9 14.0 %collective-permute-start.7 = (bf16[160,512]{1,0:T(8,128)(2,1)S(1)}, bf16[160,512]{1,0:T(8,128)(2,1)S(1)}, u32[]{:S(2)}, u32[]{:S(2)}) collective-permute-start(bf16[160,512]{1,0:T(8,128)(2,1)S(1)} %get-tuple-element.84), channel_id=1, source_target_pairs={{0,16},{4,20},{8,24},{12,28},{16,0},{20,4},{24,8},{28,12},{1,17},{... | collective-permute-start | bytes 491528 | tf_op jit(solution)/shard_map/ppermute | solution.py:40
  32.0 12.9 %collective-permute-start.8 = (bf16[160,512]{1,0:T(8,128)(2,1)S(1)}, bf16[160,512]{1,0:T(8,128)(2,1)S(1)}, u32[]{:S(2)}, u32[]{:S(2)}) collective-permute-start(bf16[160,512]{1,0:T(8,128)(2,1)S(1)} %get-tuple-element.85), channel_id=1, source_target_pairs={{0,24},{4,28},{8,16},{12,20},{16,8},{20,12},{24,0},{28,4},{1,25},{... | collective-permute-start | bytes 491528 | tf_op jit(solution)/shard_map/ppermute | solution.py:40
  45.0 18.0 %collective-permute-start.9 = (bf16[640,512]{1,0:T(8,128)(2,1)S(1)}, bf16[640,512]{1,0:T(8,128)(2,1)S(1)}, u32[]{:S(2)}, u32[]{:S(2)}) collective-permute-start(bf16[640,512]{1,0:T(8,128)(2,1)S(1)} %shard_map.132.refs_1_), channel_id=1, source_target_pairs={{0,2},{1,3},{2,0},{3,1},{4,6},{5,7},{6,4},{7,5},{8,10},{9,11},{10,... | collective-permute-start | bytes 1966088 | tf_op jit(solution)/shard_map/ppermute | solution.py:40
  49.5 13.5 %collective-permute-start.11 = (bf16[640,128]{1,0:T(8,128)(2,1)S(1)}, bf16[640,128]{1,0:T(8,128)(2,1)S(1)}, u32[]{:S(2)}, u32[]{:S(2)}) collective-permute-start(bf16[640,128]{1,0:T(8,128)(2,1)S(1)} %get-tuple-element.88), channel_id=1, source_target_pairs={{0,16},{4,20},{8,24},{12,28},{16,0},{20,4},{24,8},{28,12},{1,17},{... | collective-permute-start | bytes 491528 | tf_op jit(solution)/shard_map/ppermute | solution.py:40
  50.5 12.5 %collective-permute-start.12 = (bf16[640,128]{1,0:T(8,128)(2,1)S(1)}, bf16[640,128]{1,0:T(8,128)(2,1)S(1)}, u32[]{:S(2)}, u32[]{:S(2)}) collective-permute-start(bf16[640,128]{1,0:T(8,128)(2,1)S(1)} %get-tuple-element.89), channel_id=1, source_target_pairs={{0,24},{4,28},{8,16},{12,20},{16,8},{20,12},{24,0},{28,4},{1,25},{... | collective-permute-start | bytes 491528 | tf_op jit(solution)/shard_map/ppermute | solution.py:40
  51.9 12.4 %collective-permute-start.13 = (bf16[640,512]{1,0:T(8,128)(2,1)S(1)}, bf16[640,512]{1,0:T(8,128)(2,1)S(1)}, u32[]{:S(2)}, u32[]{:S(2)}) collective-permute-start(bf16[640,512]{1,0:T(8,128)(2,1)S(1)} %shard_map.132.refs_1_), channel_id=1, source_target_pairs={{0,1},{1,0},{2,3},{3,2},{4,5},{5,4},{6,7},{7,6},{8,9},{9,8},{10,11... | collective-permute-start | bytes 1966088 | tf_op jit(solution)/shard_map/ppermute | solution.py:40
  63.2 10.1 %collective-permute-start.15 = (bf16[320,512]{1,0:T(8,128)(2,1)S(1)}, bf16[320,512]{1,0:T(8,128)(2,1)S(1)}, u32[]{:S(2)}, u32[]{:S(2)}) collective-permute-start(bf16[320,512]{1,0:T(8,128)(2,1)S(1)} %get-tuple-element.92), channel_id=1, source_target_pairs={{0,4},{4,0},{8,12},{12,8},{16,20},{20,16},{24,28},{28,24},{1,5},{5... | collective-permute-start | bytes 983048 | tf_op jit(solution)/shard_map/ppermute | solution.py:40
  63.8 15.3 %collective-permute-start.18 = (bf16[320,512]{1,0:T(8,128)(2,1)S(1)}, bf16[320,512]{1,0:T(8,128)(2,1)S(1)}, u32[]{:S(2)}, u32[]{:S(2)}) collective-permute-start(bf16[320,512]{1,0:T(8,128)(2,1)S(1)} %get-tuple-element.90.refs_1_), channel_id=1, source_target_pairs={{0,2},{1,3},{2,0},{3,1},{4,6},{5,7},{6,4},{7,5},{8,10},{9,11},{10,... | collective-permute-start | bytes 983048 | tf_op jit(solution)/shard_map/ppermute | solution.py:40
  73.4 10.7 %collective-permute-start.22 = (bf16[320,512]{1,0:T(8,128)(2,1)S(1)}, bf16[320,512]{1,0:T(8,128)(2,1)S(1)}, u32[]{:S(2)}, u32[]{:S(2)}) collective-permute-start(bf16[320,512]{1,0:T(8,128)(2,1)S(1)} %shard_map.137.refs_0_.refs_2_), channel_id=1, source_target_pairs={{0,2},{1,3},{2,0},{3,1},{4,6},{5,7},{6,4},{7,5},{8,10},{9,11},{10,... | collective-permute-start | bytes 983048 | tf_op jit(solution)/shard_map/ppermute | solution.py:40
  76.3 7.7 %collective-permute-start.20 = (bf16[256,128]{1,0:T(8,128)(2,1)S(1)}, bf16[256,128]{1,0:T(8,128)(2,1)S(1)}, u32[]{:S(2)}, u32[]{:S(2)}) collective-permute-start(bf16[256,128]{1,0:T(8,128)(2,1)S(1)} %get-tuple-element.94), channel_id=1, source_target_pairs={{0,16},{4,20},{8,24},{12,28},{16,0},{20,4},{24,8},{28,12},{1,17},{... | collective-permute-start | bytes 196616 | tf_op jit(solution)/shard_map/ppermute | solution.py:40
  94.4 10.0 %collective-permute-start.27 = (bf16[640,512]{1,0:T(8,128)(2,1)S(1)}, bf16[640,512]{1,0:T(8,128)(2,1)S(1)}, u32[]{:S(2)}, u32[]{:S(2)}) collective-permute-start(bf16[640,512]{1,0:T(8,128)(2,1)S(1)} %get-tuple-element.106), channel_id=1, source_target_pairs={{0,1},{1,0},{2,3},{3,2},{4,5},{5,4},{6,7},{7,6},{8,9},{9,8},{10,11... | collective-permute-start | bytes 1966088 | tf_op jit(solution)/shard_map/ppermute | solution.py:40
  96.5 10.6 %collective-permute-start.26 = (bf16[320,512]{1,0:T(8,128)(2,1)S(1)}, bf16[320,512]{1,0:T(8,128)(2,1)S(1)}, u32[]{:S(2)}, u32[]{:S(2)}) collective-permute-start(bf16[320,512]{1,0:T(8,128)(2,1)S(1)} %get-tuple-element.104), channel_id=1, source_target_pairs={{0,2},{1,3},{2,0},{3,1},{4,6},{5,7},{6,4},{7,5},{8,10},{9,11},{10,... | collective-permute-start | bytes 983048 | tf_op jit(solution)/shard_map/ppermute | solution.py:40
  98.0 15.3 %collective-permute-start.29 = (bf16[320,512]{1,0:T(8,128)(2,1)S(1)}, bf16[320,512]{1,0:T(8,128)(2,1)S(1)}, u32[]{:S(2)}, u32[]{:S(2)}) collective-permute-start(bf16[320,512]{1,0:T(8,128)(2,1)S(1)} %get-tuple-element.109), channel_id=1, source_target_pairs={{0,2},{1,3},{2,0},{3,1},{4,6},{5,7},{6,4},{7,5},{8,10},{9,11},{10,... | collective-permute-start | bytes 983048 | tf_op jit(solution)/shard_map/ppermute | solution.py:40
  108.2 10.0 %collective-permute-start.32 = (bf16[320,128]{1,0:T(8,128)(2,1)S(1)}, bf16[320,128]{1,0:T(8,128)(2,1)S(1)}, u32[]{:S(2)}, u32[]{:S(2)}) collective-permute-start(bf16[320,128]{1,0:T(8,128)(2,1)S(1)} %get-tuple-element.112), channel_id=1, source_target_pairs={{0,16},{4,20},{8,24},{12,28},{16,0},{20,4},{24,8},{28,12},{1,17},{... | collective-permute-start | bytes 245768 | tf_op jit(solution)/shard_map/ppermute | solution.py:40
  110.3 15.9 %collective-permute-start.34 = (bf16[320,128]{1,0:T(8,128)(2,1)S(1)}, bf16[320,128]{1,0:T(8,128)(2,1)S(1)}, u32[]{:S(2)}, u32[]{:S(2)}) collective-permute-start(bf16[320,128]{1,0:T(8,128)(2,1)S(1)} %get-tuple-element.114), channel_id=1, source_target_pairs={{0,24},{4,28},{8,16},{12,20},{16,8},{20,12},{24,0},{28,4},{1,25},{... | collective-permute-start | bytes 245768 | tf_op jit(solution)/shard_map/ppermute | solution.py:40
  113.5 12.7 %collective-permute-start.30 = (bf16[320,128]{1,0:T(8,128)(2,1)S(1)}, bf16[320,128]{1,0:T(8,128)(2,1)S(1)}, u32[]{:S(2)}, u32[]{:S(2)}) collective-permute-start(bf16[320,128]{1,0:T(8,128)(2,1)S(1)} %get-tuple-element.110), channel_id=1, source_target_pairs={{0,4},{4,0},{8,12},{12,8},{16,20},{20,16},{24,28},{28,24},{1,5},{5... | collective-permute-start | bytes 245768 | tf_op jit(solution)/shard_map/ppermute | solution.py:40
  114.3 12.0 %collective-permute-start.31 = (bf16[320,128]{1,0:T(8,128)(2,1)S(1)}, bf16[320,128]{1,0:T(8,128)(2,1)S(1)}, u32[]{:S(2)}, u32[]{:S(2)}) collective-permute-start(bf16[320,128]{1,0:T(8,128)(2,1)S(1)} %get-tuple-element.111), channel_id=1, source_target_pairs={{0,12},{4,8},{8,4},{12,0},{16,28},{20,24},{24,20},{28,16},{1,13},{... | collective-permute-start | bytes 245768 | tf_op jit(solution)/shard_map/ppermute | solution.py:40
  115.8 10.4 %collective-permute-start.33 = (bf16[320,128]{1,0:T(8,128)(2,1)S(1)}, bf16[320,128]{1,0:T(8,128)(2,1)S(1)}, u32[]{:S(2)}, u32[]{:S(2)}) collective-permute-start(bf16[320,128]{1,0:T(8,128)(2,1)S(1)} %get-tuple-element.113), channel_id=1, source_target_pairs={{0,20},{4,16},{8,28},{12,24},{16,4},{20,0},{24,12},{28,8},{1,21},{... | collective-permute-start | bytes 245768 | tf_op jit(solution)/shard_map/ppermute | solution.py:40
  118.2 8.1 %collective-permute-start.35 = (bf16[320,128]{1,0:T(8,128)(2,1)S(1)}, bf16[320,128]{1,0:T(8,128)(2,1)S(1)}, u32[]{:S(2)}, u32[]{:S(2)}) collective-permute-start(bf16[320,128]{1,0:T(8,128)(2,1)S(1)} %get-tuple-element.115), channel_id=1, source_target_pairs={{0,28},{4,24},{8,20},{12,16},{16,12},{20,8},{24,4},{28,0},{1,29},{... | collective-permute-start | bytes 245768 | tf_op jit(solution)/shard_map/ppermute | solution.py:40
  130.7 9.3 %collective-permute-start.39 = (bf16[1024,128]{1,0:T(8,128)(2,1)S(1)}, bf16[1024,128]{1,0:T(8,128)(2,1)S(1)}, u32[]{:S(2)}, u32[]{:S(2)}) collective-permute-start(bf16[1024,128]{1,0:T(8,128)(2,1)S(1)} %get-tuple-element.127), channel_id=1, source_target_pairs={{0,4},{4,0},{8,12},{12,8},{16,20},{20,16},{24,28},{28,24},{1,5},{5... | collective-permute-start | bytes 786440 | tf_op jit(solution)/shard_map/ppermute | solution.py:40
  131.4 11.3 %collective-permute-start.43 = (bf16[1024,128]{1,0:T(8,128)(2,1)S(1)}, bf16[1024,128]{1,0:T(8,128)(2,1)S(1)}, u32[]{:S(2)}, u32[]{:S(2)}) collective-permute-start(bf16[1024,128]{1,0:T(8,128)(2,1)S(1)} %get-tuple-element.129), channel_id=1, source_target_pairs={{0,4},{4,0},{8,12},{12,8},{16,20},{20,16},{24,28},{28,24},{1,5},{5... | collective-permute-start | bytes 786440 | tf_op jit(solution)/shard_map/ppermute | solution.py:40
  132.8 11.8 %collective-permute-start.36 = (bf16[256,128]{1,0:T(8,128)(2,1)S(1)}, bf16[256,128]{1,0:T(8,128)(2,1)S(1)}, u32[]{:S(2)}, u32[]{:S(2)}) collective-permute-start(bf16[256,128]{1,0:T(8,128)(2,1)S(1)} %get-tuple-element.123), channel_id=1, source_target_pairs={{0,8},{4,12},{8,0},{12,4},{16,24},{20,28},{24,16},{28,20},{1,9},{5... | collective-permute-start | bytes 196616 | tf_op jit(solution)/shard_map/ppermute | solution.py:40
  133.1 12.8 %collective-permute-start.37 = (bf16[256,128]{1,0:T(8,128)(2,1)S(1)}, bf16[256,128]{1,0:T(8,128)(2,1)S(1)}, u32[]{:S(2)}, u32[]{:S(2)}) collective-permute-start(bf16[256,128]{1,0:T(8,128)(2,1)S(1)} %get-tuple-element.124), channel_id=1, source_target_pairs={{0,16},{4,20},{8,24},{12,28},{16,0},{20,4},{24,8},{28,12},{1,17},{... | collective-permute-start | bytes 196616 | tf_op jit(solution)/shard_map/ppermute | solution.py:40
  135.7 11.6 %collective-permute-start.38 = (bf16[256,128]{1,0:T(8,128)(2,1)S(1)}, bf16[256,128]{1,0:T(8,128)(2,1)S(1)}, u32[]{:S(2)}, u32[]{:S(2)}) collective-permute-start(bf16[256,128]{1,0:T(8,128)(2,1)S(1)} %get-tuple-element.125), channel_id=1, source_target_pairs={{0,24},{4,28},{8,16},{12,20},{16,8},{20,12},{24,0},{28,4},{1,25},{... | collective-permute-start | bytes 196616 | tf_op jit(solution)/shard_map/ppermute | solution.py:40
  140.0 8.1 %collective-permute-start.42 = (bf16[256,128]{1,0:T(8,128)(2,1)S(1)}, bf16[256,128]{1,0:T(8,128)(2,1)S(1)}, u32[]{:S(2)}, u32[]{:S(2)}) collective-permute-start(bf16[256,128]{1,0:T(8,128)(2,1)S(1)} %get-tuple-element.139), channel_id=1, source_target_pairs={{0,24},{4,28},{8,16},{12,20},{16,8},{20,12},{24,0},{28,4},{1,25},{... | collective-permute-start | bytes 196616 | tf_op jit(solution)/shard_map/ppermute | solution.py:40
  142.8 7.6 %collective-permute-start.41 = (bf16[256,128]{1,0:T(8,128)(2,1)S(1)}, bf16[256,128]{1,0:T(8,128)(2,1)S(1)}, u32[]{:S(2)}, u32[]{:S(2)}) collective-permute-start(bf16[256,128]{1,0:T(8,128)(2,1)S(1)} %get-tuple-element.140), channel_id=1, source_target_pairs={{0,16},{4,20},{8,24},{12,28},{16,0},{20,4},{24,8},{28,12},{1,17},{... | collective-permute-start | bytes 196616 | tf_op jit(solution)/shard_map/ppermute | solution.py:40
  (21 other events, 172.8 us)

commit v5 on v4

--- a/solution.py
+++ b/solution.py
@@ -272,16 +272,28 @@
                 sent[dg][at : at + stride] = routed[d * stride : (d + 1) * stride]
 
 
-def value_body(sizes, *refs):
+def spread(sizes, total, outs):
+    G, R, BL = sizes[:3]
+    s = lax.axis_index("seq")
+    g, r = s // R, s % R
+    for d in range(G):
+        for dr in range(R):
+            rows = pl.ds(pl.multiple_of(((g ^ d) * R + (r ^ dr)) * BL, BL), BL)
+            outs[dr][d * BL : (d + 1) * BL] = total[rows].astype(BF16)
+
+
+def backward_body(sizes, *refs):
     G, R, BL, cap, stride = sizes
     n = G * R
-    s = lax.axis_index("seq")
-    g, r = s // R, s % R
+    g = lax.axis_index("seq") // R
     back, refs = refs[:n], refs[n:]
     upper, refs = refs[:G], refs[G:]
     probs, refs = refs[:G], refs[G:]
-    routing, attn_grad, refs = refs[0], refs[1], refs[2:]
-    outs, total, upper_rows = refs[:R], refs[R], refs[R + 1]
+    routing, attn, keys, values, queries, refs = *refs[:5], refs[5:]
+    query_out, refs = refs[:G], refs[G:]
+    value_out, key_out, refs = refs[:R], refs[R : 2 * R], refs[2 * R :]
+    upper_rows, query_rows, value_sum, key_sum = refs
+    scale = HD**-0.5
     for d in range(G):
         upper_rows[pl.ds(pl.multiple_of((g ^ d) * BL, BL), BL)] = upper[d][...]
     for i in reversed(range(G)):
@@ -290,51 +302,23 @@
         rows = jnp.concatenate([back[d][i * stride : (i + 1) * stride] for d in range(n)], axis=0)
         picked = cols_by_cols(routing[i], rows)
         grad = (upper_rows[mine].astype(F32) + picked).astype(BF16)
-        attn_grad[mine] = grad
-        part = cols_by_cols(probs[i][...], grad)
-        if i == G - 1:
-            total[...] = part
-        else:
-            total[0:N] += part
-    spread(sizes, total, outs)
-
-
-def spread(sizes, total, outs):
-    G, R, BL = sizes[:3]
-    s = lax.axis_index("seq")
-    g, r = s // R, s % R
-    for d in range(G):
-        for dr in range(R):
-            rows = pl.ds(pl.multiple_of(((g ^ d) * R + (r ^ dr)) * BL, BL), BL)
-            outs[dr][d * BL : (d + 1) * BL] = total[rows].astype(BF16)
-
-
-def score_body(sizes, *refs):
-    G, R, BL = sizes[:3]
-    s = lax.axis_index("seq")
-    g = s // R
-    probs, refs = refs[:G], refs[G:]
-    attn_grad, attn, keys, values, queries = refs[:5]
-    refs = refs[5:]
-    query_out, refs = refs[:G], refs[G:]
-    outs, query_rows, total = refs[:R], refs[R], refs[R + 1]
-    scale = HD**-0.5
-    for i in reversed(range(G)):
-        N = (i + 1) * R * BL
-        mine = slice(i * BL, (i + 1) * BL)
-        grad = attn_grad[mine]
+        weights = probs[i][...]
+        value_part = cols_by_cols(weights, grad)
         delta = jnp.sum(grad.astype(F32) * attn[mine].astype(F32), axis=1, keepdims=True)
         dprob = rows_by_rows(grad, values[0:N])
-        dscore = (probs[i][...].astype(F32) * (dprob - delta)).astype(BF16)
+        dscore = (weights.astype(F32) * (dprob - delta)).astype(BF16)
         query_rows[mine] = (plain(dscore, keys[0:N]) * scale).astype(BF16)
-        part = cols_by_cols(dscore, queries[mine]) * scale
+        key_part = cols_by_cols(dscore, queries[mine]) * scale
         if i == G - 1:
-            total[...] = part
+            value_sum[...] = value_part
+            key_sum[...] = key_part
         else:
-            total[0:N] += part
+            value_sum[0:N] += value_part
+            key_sum[0:N] += key_part
     for d in range(G):
         query_out[d][...] = query_rows[pl.ds(pl.multiple_of((g ^ d) * BL, BL), BL)]
-    spread(sizes, total, outs)
+    spread(sizes, value_sum, value_out)
+    spread(sizes, key_sum, key_out)
 
 
 def unpack_body(sizes, *refs):
@@ -579,14 +563,6 @@
     )
     probs = list(made[:G])
     attn, keys, values, query_rows = made[G : G + 4]
-    grads = local_call(
-        functools.partial(turn_grads_body, (G, R, stride)),
-        [((rows, features), BF16)],
-        [swap(grad_pieces[dg], "seq", dg * R) for dg in range(G)],
-        after=[routing, made[G + 4]],
-        nbytes=rows * features * 4,
-    )[0]
-    grads_far = swap(grads, "exp", half)
     token_sent = local_call(
         functools.partial(dispatch_body, sizes),
         [((R * G * stride, HD), BF16)] * G,
@@ -594,6 +570,14 @@
         flops=2 * rows * BL * HD * G,
         nbytes=2 * MIB,
     )
+    grads = local_call(
+        functools.partial(turn_grads_body, (G, R, stride)),
+        [((rows, features), BF16)],
+        [swap(grad_pieces[dg], "seq", dg * R) for dg in range(G)],
+        after=token_sent[:1],
+        nbytes=rows * features * 4,
+    )[0]
+    grads_far = swap(grads, "exp", half)
     token_pieces = [swap(token_sent[dg], "seq", dg * R) for dg in range(G)]
     grad_shards = gather_exp(grads, half) + gather_exp(hold([grads_far], token_pieces[1:] or token_pieces)[0], half)
     width = min(256, FFL)
@@ -712,26 +696,21 @@
     )
 
     made = local_call(
-        functools.partial(value_body, sizes),
-        [((G * BL, HD), BF16)] * (1 + R),
-        returned + upper + probs + [routing],
+        functools.partial(backward_body, sizes),
+        [((BL, HD), BF16)] * G + [((G * BL, HD), BF16)] * (2 * R),
+        returned + upper + probs + [routing, attn, keys, values, query_rows],
         after=[in_mark],
-        scratch=[pltpu.VMEM((L, HD), F32), pltpu.VMEM((G * BL, HD), BF16)],
-        flops=2 * G * BL * L * HD,
-        nbytes=6 * MIB,
+        scratch=[
+            pltpu.VMEM((G * BL, HD), BF16),
+            pltpu.VMEM((G * BL, HD), BF16),
+            pltpu.VMEM((L, HD), F32),
+            pltpu.VMEM((L, HD), F32),
+        ],
+        flops=8 * G * BL * L * HD,
+        nbytes=10 * MIB,
         limit=limit,
     )
-    attn_grad, value_parts = made[0], made[1:]
-    made = local_call(
-        functools.partial(score_body, sizes),
-        [((BL, HD), BF16)] * G + [((G * BL, HD), BF16)] * R,
-        probs + [attn_grad, attn, keys, values, query_rows],
-        scratch=[pltpu.VMEM((G * BL, HD), BF16), pltpu.VMEM((L, HD), F32)],
-        flops=6 * G * BL * L * HD,
-        nbytes=6 * MIB,
-        limit=limit,
-    )
-    query_pieces, key_parts = made[:G], made[G:]
+    query_pieces, value_parts, key_parts = made[:G], made[G : G + R], made[G + R :]
 
     def home(pair_parts):
         moved = [swap(pair_parts[dr], "seq", dr) for dr in range(1, R)]

time: 155 us -> 153 us (0.987)
    pallas_call x16 -> x15, Pallas kernels: 30.8 us -> 30.2 us  [local_call(): pl.pallas_call(kernel, out_shape=[jax.ShapeDtypeStruct(x[0], x[1]) for x...]
where the time goes in v5:
time: 153 us
  starting transfers between devices  59.8 us (39%)
  waiting for transfers between devices  49.3 us (32%)
  Pallas kernels  41.8 us (27%)
    ppermute x47, starting transfers between devices, swap(): return lax.ppermute(block, axis, [(i, i ^ distance) for i in devices])  59.8 us
    ppermute x47, waiting for transfers between devices, swap(): return lax.ppermute(block, axis, [(i, i ^ distance) for i in devices])  49.3 us
    pallas_call x15, Pallas kernels, local_call(): pl.pallas_call(kernel, out_shape=[jax.ShapeDtypeStruct(x[0], x[1]) for x...  30.2 us
    pallas_call x2, Pallas kernels, grid_call(): pl.pallas_call(kernel, out_shape=[jax.ShapeDtypeStruct(shape, dtype) for...  11.6 us
  transfers between devices with their start and end apart: 47, of which 20 were waited for; matrix products, arithmetic and copies ran while one was open for 0% of the time, Pallas kernels for 17%

profile of v5, /device:TPU:0, one launch (start us, length us, event | category | flops | bytes accessed | tf_op | source)
XLA Modules:
  0.0 153.0 jit_solution(12234163593617028184)
XLA Ops:
  0.6 3.4 %shard_map.128 = (bf16[784,128]{1,0:T(8,128)(2,1)}, bf16[784,128]{1,0:T(8,128)(2,1)}, bf16[784,128]{1,0:T(8,128)(2,1)}, bf16[784,128]{1,0:T(8,128)(2,1)}, bf16[3...) custom-call(bf16[256,512]{1,0:T(8,128)(2,1)} %refs_0_.2, bf16[256,512]{1,0:T(8,128)(2,1)} %refs_1_.2, ...), custom_call_target="tpu_custom_call" | custom-call | bytes 1572864 | tf_op jit(solution)/shard_map/pallas_call | solution.py:56
  4.1 3.1 %collective-permute-start = (bf16[784,128]{1,0:T(8,128)(2,1)}, bf16[784,128]{1,0:T(8,128)(2,1)S(1)}, u32[]{:S(2)}, u32[]{:S(2)}) collective-permute-start(bf16[784,128]{1,0:T(8,128)(2,1)} %get-tuple-element.71), channel_id=1, source_target_pairs={{0,8},{4,12},{8,0},{12,4},{16,24},{20,28},{24,16},{28,20},{1,9},{5... | collective-permute-start | bytes 602120 | tf_op jit(solution)/shard_map/ppermute | solution.py:40
  7.2 2.6 %collective-permute-start.1 = (bf16[784,128]{1,0:T(8,128)(2,1)}, bf16[784,128]{1,0:T(8,128)(2,1)S(1)}, u32[]{:S(2)}, u32[]{:S(2)}) collective-permute-start(bf16[784,128]{1,0:T(8,128)(2,1)} %get-tuple-element.72), channel_id=1, source_target_pairs={{0,16},{4,20},{8,24},{12,28},{16,0},{20,4},{24,8},{28,12},{1,17},{... | collective-permute-start | bytes 602120 | tf_op jit(solution)/shard_map/ppermute | solution.py:40
  9.8 1.7 %collective-permute-start.5 = (bf16[320,512]{1,0:T(8,128)(2,1)}, bf16[320,512]{1,0:T(8,128)(2,1)S(1)}, u32[]{:S(2)}, u32[]{:S(2)}) collective-permute-start(bf16[320,512]{1,0:T(8,128)(2,1)} %get-tuple-element.77), channel_id=1, source_target_pairs={{0,4},{4,0},{8,12},{12,8},{16,20},{20,16},{24,28},{28,24},{1,5},{5... | collective-permute-start | bytes 983048 | tf_op jit(solution)/shard_map/ppermute | solution.py:40
  11.5 4.4 %collective-permute-done.refs_2_.refs_1_.refs_0_ = bf16[784,128]{1,0:T(8,128)(2,1)S(1)} collective-permute-done((bf16[784,128]{1,0:T(8,128)(2,1)}, bf16[784,128]{1,0:T(8,128)(2,1)S(1)}, u32[]{:S(2)}, u32[]{:S(2)}) %collective-permute-start) | collective-permute-done | bytes 200736 | tf_op jit(solution)/shard_map/ppermute | solution.py:40
  15.9 8.9 %collective-permute-done.1.refs_3_.refs_2_.refs_1_ = bf16[784,128]{1,0:T(8,128)(2,1)S(1)} collective-permute-done((bf16[784,128]{1,0:T(8,128)(2,1)}, bf16[784,128]{1,0:T(8,128)(2,1)S(1)}, u32[]{:S(2)}, u32[]{:S(2)}) %collective-permute-start.1) | collective-permute-done | bytes 200736 | tf_op jit(solution)/shard_map/ppermute | solution.py:40
  27.5 3.5 %collective-permute-start.6 = (bf16[160,512]{1,0:T(8,128)(2,1)S(1)}, bf16[160,512]{1,0:T(8,128)(2,1)S(1)}, u32[]{:S(2)}, u32[]{:S(2)}) collective-permute-start(bf16[160,512]{1,0:T(8,128)(2,1)S(1)} %get-tuple-element.79), channel_id=1, source_target_pairs={{0,8},{4,12},{8,0},{12,4},{16,24},{20,28},{24,16},{28,20},{1,9},{5... | collective-permute-start | bytes 491528 | tf_op jit(solution)/shard_map/ppermute | solution.py:40
  35.1 3.4 %collective-permute-done.3.refs_5_ = bf16[512,128]{1,0:T(8,128)(2,1)S(1)} collective-permute-done((bf16[512,128]{1,0:T(8,128)(2,1)S(1)}, bf16[512,128]{1,0:T(8,128)(2,1)S(1)}, u32[]{:S(2)}, u32[]{:S(2)}) %collective-permute-start.3) | collective-permute-done | bytes 131104 | tf_op jit(solution)/shard_map/ppermute | solution.py:40
  38.5 4.7 %shard_map.129 = (bf16[256,512]{1,0:T(8,128)(2,1)S(1)}, bf16[256,1024]{1,0:T(8,128)(2,1)S(1)}, bf16[256,1536]{1,0:T(8,128)(2,1)S(1)}, bf16[256,2048]{1,0:T(8,128...) custom-call(f32[4]{0:T(128)S(1)} %copy-done.3, ...), custom_call_target="tpu_custom_call" | custom-call | tf_op jit(solution)/shard_map/pallas_call | solution.py:56
  45.0 1.6 %collective-permute-start.9 = (bf16[640,512]{1,0:T(8,128)(2,1)S(1)}, bf16[640,512]{1,0:T(8,128)(2,1)S(1)}, u32[]{:S(2)}, u32[]{:S(2)}) collective-permute-start(bf16[640,512]{1,0:T(8,128)(2,1)S(1)} %shard_map.133.refs_1_), channel_id=1, source_target_pairs={{0,2},{1,3},{2,0},{3,1},{4,6},{5,7},{6,4},{7,5},{8,10},{9,11},{10,... | collective-permute-start | bytes 1966088 | tf_op jit(solution)/shard_map/ppermute | solution.py:40
  46.6 2.3 %collective-permute-start.10 = (bf16[640,128]{1,0:T(8,128)(2,1)S(1)}, bf16[640,128]{1,0:T(8,128)(2,1)S(1)}, u32[]{:S(2)}, u32[]{:S(2)}) collective-permute-start(bf16[640,128]{1,0:T(8,128)(2,1)S(1)} %get-tuple-element.82), channel_id=1, source_target_pairs={{0,8},{4,12},{8,0},{12,4},{16,24},{20,28},{24,16},{28,20},{1,9},{5... | collective-permute-start | bytes 491528 | tf_op jit(solution)/shard_map/ppermute | solution.py:40
  51.3 2.2 %collective-permute-done.10.refs_2_.refs_0_ = bf16[640,128]{1,0:T(8,128)(2,1)S(1)} collective-permute-done((bf16[640,128]{1,0:T(8,128)(2,1)S(1)}, bf16[640,128]{1,0:T(8,128)(2,1)S(1)}, u32[]{:S(2)}, u32[]{:S(2)}) %collective-permute-start.10) | collective-permute-done | bytes 163872 | tf_op jit(solution)/shard_map/ppermute | solution.py:40
  53.5 8.9 %collective-permute-done.11.refs_3_.refs_1_ = bf16[640,128]{1,0:T(8,128)(2,1)S(1)} collective-permute-done((bf16[640,128]{1,0:T(8,128)(2,1)S(1)}, bf16[640,128]{1,0:T(8,128)(2,1)S(1)}, u32[]{:S(2)}, u32[]{:S(2)}) %collective-permute-start.11) | collective-permute-done | bytes 163872 | tf_op jit(solution)/shard_map/ppermute | solution.py:40
  64.7 6.9 %shard_map.136 = (f32[640,1024]{1,0:T(8,128)S(1)}, bf16[640,2048]{1,0:T(8,128)(2,1)S(1)}) custom-call(bf16[1024,2048]{1,0:T(8,128)(2,1)S(1)} %bitcast.6, bf16[640,512]{1,0:T(8,128)(2,1)S(1)} %shard_map.133.refs_1_, bf16[640,512]{1,0:T(8,128)(2,1)S(1)} %collective-permute-done.13.refs_2_, bf16[640,512]{1,0:T(8,128)(2,1)S(1)} %shard_map.135.refs_3_, ...), custom_call_target="tpu_custom_call" | custom-call | flops 2684354560 | bytes 10485760 | tf_op jit(solution)/shard_map/pallas_call | solution.py:56
  73.4 2.4 %collective-permute-start.19 = (bf16[256,128]{1,0:T(8,128)(2,1)S(1)}, bf16[256,128]{1,0:T(8,128)(2,1)S(1)}, u32[]{:S(2)}, u32[]{:S(2)}) collective-permute-start(bf16[256,128]{1,0:T(8,128)(2,1)S(1)} %get-tuple-element.88), channel_id=1, source_target_pairs={{0,8},{4,12},{8,0},{12,4},{16,24},{20,28},{24,16},{28,20},{1,9},{5... | collective-permute-start | bytes 196616 | tf_op jit(solution)/shard_map/ppermute | solution.py:40
  78.9 4.5 %collective-permute-done.20.refs_1_.refs_11_ = bf16[256,128]{1,0:T(8,128)(2,1)S(1)} collective-permute-done((bf16[256,128]{1,0:T(8,128)(2,1)S(1)}, bf16[256,128]{1,0:T(8,128)(2,1)S(1)}, u32[]{:S(2)}, u32[]{:S(2)}) %collective-permute-start.20) | collective-permute-done | bytes 65568 | tf_op jit(solution)/shard_map/ppermute | solution.py:40
  85.5 8.0 %shard_map.140 = (bf16[640,2048]{1,0:T(8,128)(2,1)S(1)}, bf16[640,1024]{1,0:T(8,128)(2,1)S(1)}, bf16[640,1024]{1,0:T(8,128)(2,1)S(1)}, f32[640,512]{1,0:T(8,128)...) custom-call(bf16[2048,1024]{1,0:T(8,128)(2,1)S(1)} %bitcast.7, ...), custom_call_target="tpu_custom_call" | custom-call | flops 5368709120 | bytes 8388608 | tf_op jit(solution)/shard_map/pallas_call | solution.py:56
  94.1 1.6 %collective-permute-done.25.refs_1_ = bf16[640,512]{1,0:T(8,128)(2,1)S(1)} collective-permute-done((bf16[640,512]{1,0:T(8,128)(2,1)S(1)}, bf16[640,512]{1,0:T(8,128)(2,1)S(1)}, u32[]{:S(2)}, u32[]{:S(2)}) %collective-permute-start.25) | collective-permute-done | bytes 655392 | tf_op jit(solution)/shard_map/ppermute | solution.py:40
  97.9 5.8 %shard_map.142 = (bf16[1024,2048]{1,0:T(8,128)(2,1)}, f32[8,128]{1,0:T(8,128)S(1)}) custom-call(s32[1]{0:T(128)} %get-tuple-element.69.place, bf16[640,1024]{1,0:T(8,128)(2,1)S(1)} %get-tuple-element.94.refs_0_, bf16[640,2048]{1,0:T(8,128)(2,1)S(1)} %get-tuple-element.95.refs_1_), custom_call_target="tpu_custom_call" | custom-call | flops 2684354560 | bytes 10485760 | tf_op jit(solution)/shard_map/pallas_call | solution.py:93
  103.7 2.7 %collective-permute-done.26.refs_1_ = bf16[320,512]{1,0:T(8,128)(2,1)S(1)} collective-permute-done((bf16[320,512]{1,0:T(8,128)(2,1)S(1)}, bf16[320,512]{1,0:T(8,128)(2,1)S(1)}, u32[]{:S(2)}, u32[]{:S(2)}) %collective-permute-start.26) | collective-permute-done | bytes 327712 | tf_op jit(solution)/shard_map/ppermute | solution.py:40
  107.5 2.1 %collective-permute-start.32 = (bf16[320,128]{1,0:T(8,128)(2,1)S(1)}, bf16[320,128]{1,0:T(8,128)(2,1)S(1)}, u32[]{:S(2)}, u32[]{:S(2)}) collective-permute-start(bf16[320,128]{1,0:T(8,128)(2,1)S(1)} %get-tuple-element.107), channel_id=1, source_target_pairs={{0,16},{4,20},{8,24},{12,28},{16,0},{20,4},{24,8},{28,12},{1,17},{... | collective-permute-start | bytes 245768 | tf_op jit(solution)/shard_map/ppermute | solution.py:40
  111.1 1.6 %collective-permute-done.29.refs_1_ = bf16[320,512]{1,0:T(8,128)(2,1)S(1)} collective-permute-done((bf16[320,512]{1,0:T(8,128)(2,1)S(1)}, bf16[320,512]{1,0:T(8,128)(2,1)S(1)}, u32[]{:S(2)}, u32[]{:S(2)}) %collective-permute-start.29) | collective-permute-done | bytes 327712 | tf_op jit(solution)/shard_map/ppermute | solution.py:40
  113.6 1.6 %collective-permute-start.31 = (bf16[320,128]{1,0:T(8,128)(2,1)S(1)}, bf16[320,128]{1,0:T(8,128)(2,1)S(1)}, u32[]{:S(2)}, u32[]{:S(2)}) collective-permute-start(bf16[320,128]{1,0:T(8,128)(2,1)S(1)} %get-tuple-element.106), channel_id=1, source_target_pairs={{0,12},{4,8},{8,4},{12,0},{16,28},{20,24},{24,20},{28,16},{1,13},{... | collective-permute-start | bytes 245768 | tf_op jit(solution)/shard_map/ppermute | solution.py:40
  115.2 2.3 %collective-permute-start.33 = (bf16[320,128]{1,0:T(8,128)(2,1)S(1)}, bf16[320,128]{1,0:T(8,128)(2,1)S(1)}, u32[]{:S(2)}, u32[]{:S(2)}) collective-permute-start(bf16[320,128]{1,0:T(8,128)(2,1)S(1)} %get-tuple-element.108), channel_id=1, source_target_pairs={{0,20},{4,16},{8,28},{12,24},{16,4},{20,0},{24,12},{28,8},{1,21},{... | collective-permute-start | bytes 245768 | tf_op jit(solution)/shard_map/ppermute | solution.py:40
  117.5 2.2 %collective-permute-start.35 = (bf16[320,128]{1,0:T(8,128)(2,1)S(1)}, bf16[320,128]{1,0:T(8,128)(2,1)S(1)}, u32[]{:S(2)}, u32[]{:S(2)}) collective-permute-start(bf16[320,128]{1,0:T(8,128)(2,1)S(1)} %get-tuple-element.110), channel_id=1, source_target_pairs={{0,28},{4,24},{8,20},{12,16},{16,12},{20,8},{24,4},{28,0},{1,29},{... | collective-permute-start | bytes 245768 | tf_op jit(solution)/shard_map/ppermute | solution.py:40
  119.7 5.8 %shard_map.141 = (bf16[2048,1024]{1,0:T(8,128)(2,1)}, f32[8,128]{1,0:T(8,128)S(1)}) custom-call(s32[1]{0:T(128)} %get-tuple-element.69.place, bf16[640,2048]{1,0:T(8,128)(2,1)S(1)} %get-tuple-element.91.refs_0_, bf16[640,1024]{1,0:T(8,128)(2,1)S(1)} %get-tuple-element.92.refs_1_), custom_call_target="tpu_custom_call" | custom-call | flops 2684354560 | bytes 10485760 | tf_op jit(solution)/shard_map/pallas_call | solution.py:93
  125.5 3.8 %shard_map.146 = (bf16[256,128]{1,0:T(8,128)(2,1)S(1)}, bf16[256,128]{1,0:T(8,128)(2,1)S(1)}, bf16[256,128]{1,0:T(8,128)(2,1)S(1)}, bf16[256,128]{1,0:T(8,128)(2...) custom-call(f32[8,128]{1,0:T(8,128)S(1)} %get-tuple-element.93.refs_, ...), custom_call_target="tpu_custom_call" | custom-call | flops 2147483648 | bytes 10485760 | tf_op jit(solution)/shard_map/pallas_call | solution.py:56
  131.8 2.6 %collective-permute-start.37 = (bf16[256,128]{1,0:T(8,128)(2,1)S(1)}, bf16[256,128]{1,0:T(8,128)(2,1)S(1)}, u32[]{:S(2)}, u32[]{:S(2)}) collective-permute-start(bf16[256,128]{1,0:T(8,128)(2,1)S(1)} %get-tuple-element.122), channel_id=1, source_target_pairs={{0,16},{4,20},{8,24},{12,28},{16,0},{20,4},{24,8},{28,12},{1,17},{... | collective-permute-start | bytes 196616 | tf_op jit(solution)/shard_map/ppermute | solution.py:40
  135.8 2.8 %collective-permute-done.39 = bf16[1024,128]{1,0:T(8,128)(2,1)S(1)} collective-permute-done((bf16[1024,128]{1,0:T(8,128)(2,1)S(1)}, bf16[1024,128]{1,0:T(8,128)(2,1)S(1)}, u32[]{:S(2)}, u32[]{:S(2)}) %collective-permute-start.39) | collective-permute-done | bytes 262176 | tf_op jit(solution)/shard_map/ppermute | solution.py:40
  138.7 2.4 %collective-permute-start.42 = (bf16[256,128]{1,0:T(8,128)(2,1)S(1)}, bf16[256,128]{1,0:T(8,128)(2,1)S(1)}, u32[]{:S(2)}, u32[]{:S(2)}) collective-permute-start(bf16[256,128]{1,0:T(8,128)(2,1)S(1)} %get-tuple-element.137), channel_id=1, source_target_pairs={{0,24},{4,28},{8,16},{12,20},{16,8},{20,12},{24,0},{28,4},{1,25},{... | collective-permute-start | bytes 196616 | tf_op jit(solution)/shard_map/ppermute | solution.py:40
  141.4 1.7 %collective-permute-start.41 = (bf16[256,128]{1,0:T(8,128)(2,1)S(1)}, bf16[256,128]{1,0:T(8,128)(2,1)S(1)}, u32[]{:S(2)}, u32[]{:S(2)}) collective-permute-start(bf16[256,128]{1,0:T(8,128)(2,1)S(1)} %get-tuple-element.138), channel_id=1, source_target_pairs={{0,16},{4,20},{8,24},{12,28},{16,0},{20,4},{24,8},{28,12},{1,17},{... | collective-permute-start | bytes 196616 | tf_op jit(solution)/shard_map/ppermute | solution.py:40
  146.8 2.1 %collective-permute-start.44 = (bf16[256,128]{1,0:T(8,128)(2,1)S(1)}, bf16[256,128]{1,0:T(8,128)(2,1)S(1)}, u32[]{:S(2)}, u32[]{:S(2)}) collective-permute-start(bf16[256,128]{1,0:T(8,128)(2,1)S(1)} %get-tuple-element.135), channel_id=1, source_target_pairs={{0,8},{4,12},{8,0},{12,4},{16,24},{20,28},{24,16},{28,20},{1,9},{5... | collective-permute-start | bytes 196616 | tf_op jit(solution)/shard_map/ppermute | solution.py:40
  (101 shorter events, 38.4 us)
Async XLA Ops:
  4.1 11.8 %collective-permute-start = (bf16[784,128]{1,0:T(8,128)(2,1)}, bf16[784,128]{1,0:T(8,128)(2,1)S(1)}, u32[]{:S(2)}, u32[]{:S(2)}) collective-permute-start(bf16[784,128]{1,0:T(8,128)(2,1)} %get-tuple-element.71), channel_id=1, source_target_pairs={{0,8},{4,12},{8,0},{12,4},{16,24},{20,28},{24,16},{28,20},{1,9},{5... | collective-permute-start | bytes 602120 | tf_op jit(solution)/shard_map/ppermute | solution.py:40
  7.2 17.6 %collective-permute-start.1 = (bf16[784,128]{1,0:T(8,128)(2,1)}, bf16[784,128]{1,0:T(8,128)(2,1)S(1)}, u32[]{:S(2)}, u32[]{:S(2)}) collective-permute-start(bf16[784,128]{1,0:T(8,128)(2,1)} %get-tuple-element.72), channel_id=1, source_target_pairs={{0,16},{4,20},{8,24},{12,28},{16,0},{20,4},{24,8},{28,12},{1,17},{... | collective-permute-start | bytes 602120 | tf_op jit(solution)/shard_map/ppermute | solution.py:40
  9.8 15.1 %collective-permute-start.2 = (bf16[784,128]{1,0:T(8,128)(2,1)}, bf16[784,128]{1,0:T(8,128)(2,1)S(1)}, u32[]{:S(2)}, u32[]{:S(2)}) collective-permute-start(bf16[784,128]{1,0:T(8,128)(2,1)} %get-tuple-element.73), channel_id=1, source_target_pairs={{0,24},{4,28},{8,16},{12,20},{16,8},{20,12},{24,0},{28,4},{1,25},{... | collective-permute-start | bytes 602120 | tf_op jit(solution)/shard_map/ppermute | solution.py:40
  9.8 16.7 %collective-permute-start.5 = (bf16[320,512]{1,0:T(8,128)(2,1)}, bf16[320,512]{1,0:T(8,128)(2,1)S(1)}, u32[]{:S(2)}, u32[]{:S(2)}) collective-permute-start(bf16[320,512]{1,0:T(8,128)(2,1)} %get-tuple-element.77), channel_id=1, source_target_pairs={{0,4},{4,0},{8,12},{12,8},{16,20},{20,16},{24,28},{28,24},{1,5},{5... | collective-permute-start | bytes 983048 | tf_op jit(solution)/shard_map/ppermute | solution.py:40
  24.9 13.6 %collective-permute-start.4 = (bf16[1536,128]{1,0:T(8,128)(2,1)S(1)}, bf16[1536,128]{1,0:T(8,128)(2,1)S(1)}, u32[]{:S(2)}, u32[]{:S(2)}) collective-permute-start(bf16[1536,128]{1,0:T(8,128)(2,1)S(1)} %pad_maximum_fusion), channel_id=1, source_target_pairs={{0,4},{4,0},{8,12},{12,8},{16,20},{20,16},{24,28},{28,24},{1,5},{5... | collective-permute-start | bytes 1179656 | tf_op jit(solution)/shard_map/ppermute | solution.py:40
  27.5 16.2 %collective-permute-start.6 = (bf16[160,512]{1,0:T(8,128)(2,1)S(1)}, bf16[160,512]{1,0:T(8,128)(2,1)S(1)}, u32[]{:S(2)}, u32[]{:S(2)}) collective-permute-start(bf16[160,512]{1,0:T(8,128)(2,1)S(1)} %get-tuple-element.79), channel_id=1, source_target_pairs={{0,8},{4,12},{8,0},{12,4},{16,24},{20,28},{24,16},{28,20},{1,9},{5... | collective-permute-start | bytes 491528 | tf_op jit(solution)/shard_map/ppermute | solution.py:40
  30.9 14.0 %collective-permute-start.7 = (bf16[160,512]{1,0:T(8,128)(2,1)S(1)}, bf16[160,512]{1,0:T(8,128)(2,1)S(1)}, u32[]{:S(2)}, u32[]{:S(2)}) collective-permute-start(bf16[160,512]{1,0:T(8,128)(2,1)S(1)} %get-tuple-element.80), channel_id=1, source_target_pairs={{0,16},{4,20},{8,24},{12,28},{16,0},{20,4},{24,8},{28,12},{1,17},{... | collective-permute-start | bytes 491528 | tf_op jit(solution)/shard_map/ppermute | solution.py:40
  32.0 12.9 %collective-permute-start.8 = (bf16[160,512]{1,0:T(8,128)(2,1)S(1)}, bf16[160,512]{1,0:T(8,128)(2,1)S(1)}, u32[]{:S(2)}, u32[]{:S(2)}) collective-permute-start(bf16[160,512]{1,0:T(8,128)(2,1)S(1)} %get-tuple-element.81), channel_id=1, source_target_pairs={{0,24},{4,28},{8,16},{12,20},{16,8},{20,12},{24,0},{28,4},{1,25},{... | collective-permute-start | bytes 491528 | tf_op jit(solution)/shard_map/ppermute | solution.py:40
  45.0 17.5 %collective-permute-start.9 = (bf16[640,512]{1,0:T(8,128)(2,1)S(1)}, bf16[640,512]{1,0:T(8,128)(2,1)S(1)}, u32[]{:S(2)}, u32[]{:S(2)}) collective-permute-start(bf16[640,512]{1,0:T(8,128)(2,1)S(1)} %shard_map.133.refs_1_), channel_id=1, source_target_pairs={{0,2},{1,3},{2,0},{3,1},{4,6},{5,7},{6,4},{7,5},{8,10},{9,11},{10,... | collective-permute-start | bytes 1966088 | tf_op jit(solution)/shard_map/ppermute | solution.py:40
  48.9 13.5 %collective-permute-start.11 = (bf16[640,128]{1,0:T(8,128)(2,1)S(1)}, bf16[640,128]{1,0:T(8,128)(2,1)S(1)}, u32[]{:S(2)}, u32[]{:S(2)}) collective-permute-start(bf16[640,128]{1,0:T(8,128)(2,1)S(1)} %get-tuple-element.83), channel_id=1, source_target_pairs={{0,16},{4,20},{8,24},{12,28},{16,0},{20,4},{24,8},{28,12},{1,17},{... | collective-permute-start | bytes 491528 | tf_op jit(solution)/shard_map/ppermute | solution.py:40
  49.8 12.6 %collective-permute-start.12 = (bf16[640,128]{1,0:T(8,128)(2,1)S(1)}, bf16[640,128]{1,0:T(8,128)(2,1)S(1)}, u32[]{:S(2)}, u32[]{:S(2)}) collective-permute-start(bf16[640,128]{1,0:T(8,128)(2,1)S(1)} %get-tuple-element.84), channel_id=1, source_target_pairs={{0,24},{4,28},{8,16},{12,20},{16,8},{20,12},{24,0},{28,4},{1,25},{... | collective-permute-start | bytes 491528 | tf_op jit(solution)/shard_map/ppermute | solution.py:40
  51.3 12.4 %collective-permute-start.13 = (bf16[640,512]{1,0:T(8,128)(2,1)S(1)}, bf16[640,512]{1,0:T(8,128)(2,1)S(1)}, u32[]{:S(2)}, u32[]{:S(2)}) collective-permute-start(bf16[640,512]{1,0:T(8,128)(2,1)S(1)} %shard_map.133.refs_1_), channel_id=1, source_target_pairs={{0,1},{1,0},{2,3},{3,2},{4,5},{5,4},{6,7},{7,6},{8,9},{9,8},{10,11... | collective-permute-start | bytes 1966088 | tf_op jit(solution)/shard_map/ppermute | solution.py:40
  62.6 10.1 %collective-permute-start.15 = (bf16[320,512]{1,0:T(8,128)(2,1)S(1)}, bf16[320,512]{1,0:T(8,128)(2,1)S(1)}, u32[]{:S(2)}, u32[]{:S(2)}) collective-permute-start(bf16[320,512]{1,0:T(8,128)(2,1)S(1)} %get-tuple-element.87), channel_id=1, source_target_pairs={{0,4},{4,0},{8,12},{12,8},{16,20},{20,16},{24,28},{28,24},{1,5},{5... | collective-permute-start | bytes 983048 | tf_op jit(solution)/shard_map/ppermute | solution.py:40
  63.2 15.2 %collective-permute-start.18 = (bf16[320,512]{1,0:T(8,128)(2,1)S(1)}, bf16[320,512]{1,0:T(8,128)(2,1)S(1)}, u32[]{:S(2)}, u32[]{:S(2)}) collective-permute-start(bf16[320,512]{1,0:T(8,128)(2,1)S(1)} %get-tuple-element.85.refs_1_), channel_id=1, source_target_pairs={{0,2},{1,3},{2,0},{3,1},{4,6},{5,7},{6,4},{7,5},{8,10},{9,11},{10,... | collective-permute-start | bytes 983048 | tf_op jit(solution)/shard_map/ppermute | solution.py:40
  72.8 10.6 %collective-permute-start.22 = (bf16[320,512]{1,0:T(8,128)(2,1)S(1)}, bf16[320,512]{1,0:T(8,128)(2,1)S(1)}, u32[]{:S(2)}, u32[]{:S(2)}) collective-permute-start(bf16[320,512]{1,0:T(8,128)(2,1)S(1)} %shard_map.137.refs_0_.refs_2_), channel_id=1, source_target_pairs={{0,2},{1,3},{2,0},{3,1},{4,6},{5,7},{6,4},{7,5},{8,10},{9,11},{10,... | collective-permute-start | bytes 983048 | tf_op jit(solution)/shard_map/ppermute | solution.py:40
  75.7 7.7 %collective-permute-start.20 = (bf16[256,128]{1,0:T(8,128)(2,1)S(1)}, bf16[256,128]{1,0:T(8,128)(2,1)S(1)}, u32[]{:S(2)}, u32[]{:S(2)}) collective-permute-start(bf16[256,128]{1,0:T(8,128)(2,1)S(1)} %get-tuple-element.89), channel_id=1, source_target_pairs={{0,16},{4,20},{8,24},{12,28},{16,0},{20,4},{24,8},{28,12},{1,17},{... | collective-permute-start | bytes 196616 | tf_op jit(solution)/shard_map/ppermute | solution.py:40
  93.8 10.0 %collective-permute-start.27 = (bf16[640,512]{1,0:T(8,128)(2,1)S(1)}, bf16[640,512]{1,0:T(8,128)(2,1)S(1)}, u32[]{:S(2)}, u32[]{:S(2)}) collective-permute-start(bf16[640,512]{1,0:T(8,128)(2,1)S(1)} %get-tuple-element.101), channel_id=1, source_target_pairs={{0,1},{1,0},{2,3},{3,2},{4,5},{5,4},{6,7},{7,6},{8,9},{9,8},{10,11... | collective-permute-start | bytes 1966088 | tf_op jit(solution)/shard_map/ppermute | solution.py:40
  95.8 10.6 %collective-permute-start.26 = (bf16[320,512]{1,0:T(8,128)(2,1)S(1)}, bf16[320,512]{1,0:T(8,128)(2,1)S(1)}, u32[]{:S(2)}, u32[]{:S(2)}) collective-permute-start(bf16[320,512]{1,0:T(8,128)(2,1)S(1)} %get-tuple-element.99), channel_id=1, source_target_pairs={{0,2},{1,3},{2,0},{3,1},{4,6},{5,7},{6,4},{7,5},{8,10},{9,11},{10,... | collective-permute-start | bytes 983048 | tf_op jit(solution)/shard_map/ppermute | solution.py:40
  97.4 15.3 %collective-permute-start.29 = (bf16[320,512]{1,0:T(8,128)(2,1)S(1)}, bf16[320,512]{1,0:T(8,128)(2,1)S(1)}, u32[]{:S(2)}, u32[]{:S(2)}) collective-permute-start(bf16[320,512]{1,0:T(8,128)(2,1)S(1)} %get-tuple-element.104), channel_id=1, source_target_pairs={{0,2},{1,3},{2,0},{3,1},{4,6},{5,7},{6,4},{7,5},{8,10},{9,11},{10,... | collective-permute-start | bytes 983048 | tf_op jit(solution)/shard_map/ppermute | solution.py:40
  107.5 10.0 %collective-permute-start.32 = (bf16[320,128]{1,0:T(8,128)(2,1)S(1)}, bf16[320,128]{1,0:T(8,128)(2,1)S(1)}, u32[]{:S(2)}, u32[]{:S(2)}) collective-permute-start(bf16[320,128]{1,0:T(8,128)(2,1)S(1)} %get-tuple-element.107), channel_id=1, source_target_pairs={{0,16},{4,20},{8,24},{12,28},{16,0},{20,4},{24,8},{28,12},{1,17},{... | collective-permute-start | bytes 245768 | tf_op jit(solution)/shard_map/ppermute | solution.py:40
  109.6 15.9 %collective-permute-start.34 = (bf16[320,128]{1,0:T(8,128)(2,1)S(1)}, bf16[320,128]{1,0:T(8,128)(2,1)S(1)}, u32[]{:S(2)}, u32[]{:S(2)}) collective-permute-start(bf16[320,128]{1,0:T(8,128)(2,1)S(1)} %get-tuple-element.109), channel_id=1, source_target_pairs={{0,24},{4,28},{8,16},{12,20},{16,8},{20,12},{24,0},{28,4},{1,25},{... | collective-permute-start | bytes 245768 | tf_op jit(solution)/shard_map/ppermute | solution.py:40
  112.8 12.7 %collective-permute-start.30 = (bf16[320,128]{1,0:T(8,128)(2,1)S(1)}, bf16[320,128]{1,0:T(8,128)(2,1)S(1)}, u32[]{:S(2)}, u32[]{:S(2)}) collective-permute-start(bf16[320,128]{1,0:T(8,128)(2,1)S(1)} %get-tuple-element.105), channel_id=1, source_target_pairs={{0,4},{4,0},{8,12},{12,8},{16,20},{20,16},{24,28},{28,24},{1,5},{5... | collective-permute-start | bytes 245768 | tf_op jit(solution)/shard_map/ppermute | solution.py:40
  113.6 11.9 %collective-permute-start.31 = (bf16[320,128]{1,0:T(8,128)(2,1)S(1)}, bf16[320,128]{1,0:T(8,128)(2,1)S(1)}, u32[]{:S(2)}, u32[]{:S(2)}) collective-permute-start(bf16[320,128]{1,0:T(8,128)(2,1)S(1)} %get-tuple-element.106), channel_id=1, source_target_pairs={{0,12},{4,8},{8,4},{12,0},{16,28},{20,24},{24,20},{28,16},{1,13},{... | collective-permute-start | bytes 245768 | tf_op jit(solution)/shard_map/ppermute | solution.py:40
  115.2 10.3 %collective-permute-start.33 = (bf16[320,128]{1,0:T(8,128)(2,1)S(1)}, bf16[320,128]{1,0:T(8,128)(2,1)S(1)}, u32[]{:S(2)}, u32[]{:S(2)}) collective-permute-start(bf16[320,128]{1,0:T(8,128)(2,1)S(1)} %get-tuple-element.108), channel_id=1, source_target_pairs={{0,20},{4,16},{8,28},{12,24},{16,4},{20,0},{24,12},{28,8},{1,21},{... | collective-permute-start | bytes 245768 | tf_op jit(solution)/shard_map/ppermute | solution.py:40
  117.5 8.1 %collective-permute-start.35 = (bf16[320,128]{1,0:T(8,128)(2,1)S(1)}, bf16[320,128]{1,0:T(8,128)(2,1)S(1)}, u32[]{:S(2)}, u32[]{:S(2)}) collective-permute-start(bf16[320,128]{1,0:T(8,128)(2,1)S(1)} %get-tuple-element.110), channel_id=1, source_target_pairs={{0,28},{4,24},{8,20},{12,16},{16,12},{20,8},{24,4},{28,0},{1,29},{... | collective-permute-start | bytes 245768 | tf_op jit(solution)/shard_map/ppermute | solution.py:40
  129.3 9.3 %collective-permute-start.39 = (bf16[1024,128]{1,0:T(8,128)(2,1)S(1)}, bf16[1024,128]{1,0:T(8,128)(2,1)S(1)}, u32[]{:S(2)}, u32[]{:S(2)}) collective-permute-start(bf16[1024,128]{1,0:T(8,128)(2,1)S(1)} %get-tuple-element.125), channel_id=1, source_target_pairs={{0,4},{4,0},{8,12},{12,8},{16,20},{20,16},{24,28},{28,24},{1,5},{5... | collective-permute-start | bytes 786440 | tf_op jit(solution)/shard_map/ppermute | solution.py:40
  130.1 11.3 %collective-permute-start.43 = (bf16[1024,128]{1,0:T(8,128)(2,1)S(1)}, bf16[1024,128]{1,0:T(8,128)(2,1)S(1)}, u32[]{:S(2)}, u32[]{:S(2)}) collective-permute-start(bf16[1024,128]{1,0:T(8,128)(2,1)S(1)} %get-tuple-element.127), channel_id=1, source_target_pairs={{0,4},{4,0},{8,12},{12,8},{16,20},{20,16},{24,28},{28,24},{1,5},{5... | collective-permute-start | bytes 786440 | tf_op jit(solution)/shard_map/ppermute | solution.py:40
  131.4 11.8 %collective-permute-start.36 = (bf16[256,128]{1,0:T(8,128)(2,1)S(1)}, bf16[256,128]{1,0:T(8,128)(2,1)S(1)}, u32[]{:S(2)}, u32[]{:S(2)}) collective-permute-start(bf16[256,128]{1,0:T(8,128)(2,1)S(1)} %get-tuple-element.121), channel_id=1, source_target_pairs={{0,8},{4,12},{8,0},{12,4},{16,24},{20,28},{24,16},{28,20},{1,9},{5... | collective-permute-start | bytes 196616 | tf_op jit(solution)/shard_map/ppermute | solution.py:40
  131.8 12.7 %collective-permute-start.37 = (bf16[256,128]{1,0:T(8,128)(2,1)S(1)}, bf16[256,128]{1,0:T(8,128)(2,1)S(1)}, u32[]{:S(2)}, u32[]{:S(2)}) collective-permute-start(bf16[256,128]{1,0:T(8,128)(2,1)S(1)} %get-tuple-element.122), channel_id=1, source_target_pairs={{0,16},{4,20},{8,24},{12,28},{16,0},{20,4},{24,8},{28,12},{1,17},{... | collective-permute-start | bytes 196616 | tf_op jit(solution)/shard_map/ppermute | solution.py:40
  134.4 11.6 %collective-permute-start.38 = (bf16[256,128]{1,0:T(8,128)(2,1)S(1)}, bf16[256,128]{1,0:T(8,128)(2,1)S(1)}, u32[]{:S(2)}, u32[]{:S(2)}) collective-permute-start(bf16[256,128]{1,0:T(8,128)(2,1)S(1)} %get-tuple-element.123), channel_id=1, source_target_pairs={{0,24},{4,28},{8,16},{12,20},{16,8},{20,12},{24,0},{28,4},{1,25},{... | collective-permute-start | bytes 196616 | tf_op jit(solution)/shard_map/ppermute | solution.py:40
  138.7 8.1 %collective-permute-start.42 = (bf16[256,128]{1,0:T(8,128)(2,1)S(1)}, bf16[256,128]{1,0:T(8,128)(2,1)S(1)}, u32[]{:S(2)}, u32[]{:S(2)}) collective-permute-start(bf16[256,128]{1,0:T(8,128)(2,1)S(1)} %get-tuple-element.137), channel_id=1, source_target_pairs={{0,24},{4,28},{8,16},{12,20},{16,8},{20,12},{24,0},{28,4},{1,25},{... | collective-permute-start | bytes 196616 | tf_op jit(solution)/shard_map/ppermute | solution.py:40
  141.4 7.6 %collective-permute-start.41 = (bf16[256,128]{1,0:T(8,128)(2,1)S(1)}, bf16[256,128]{1,0:T(8,128)(2,1)S(1)}, u32[]{:S(2)}, u32[]{:S(2)}) collective-permute-start(bf16[256,128]{1,0:T(8,128)(2,1)S(1)} %get-tuple-element.138), channel_id=1, source_target_pairs={{0,16},{4,20},{8,24},{12,28},{16,0},{20,4},{24,8},{28,12},{1,17},{... | collective-permute-start | bytes 196616 | tf_op jit(solution)/shard_map/ppermute | solution.py:40
  (21 other events, 173.2 us)

commit v6 on v5

--- a/solution.py
+++ b/solution.py
@@ -423,30 +423,34 @@
     wide = weight.shape[1] // steps
     kept = keep_moves(parts, 0, shards, full, own_sems)
 
-    def fetch(c):
-        return pltpu.make_async_copy(weight.at[:, pl.ds(c * wide, wide)], held.at[c], sems.at[c])
+    def fetch(c, k):
+        at = pl.ds(pl.multiple_of((place ^ k) * width, 128), width)
+        return pltpu.make_async_copy(weight.at[at, pl.ds(c * wide, wide)], held.at[c, at], sems.at[c, k])
 
     for c in range(min(2, steps)):
-        fetch(c).start()
+        for k in range(count):
+            fetch(c, k).start()
     for c in range(steps):
         cols = slice(c * wide, (c + 1) * wide)
-        fetch(c).wait()
-        if c == 0:
-            for move in kept:
-                move.start()
         if c + 2 < steps:
-            fetch(c + 2).start()
+            for k in range(count):
+                fetch(c + 2, k).start()
         for h in range(parts):
             mine = slice(h * rows, (h + 1) * rows)
             total = None
             for k in range(len(shards) // parts):
                 at = pl.ds(pl.multiple_of((place ^ k) * width, 128), width)
+                if h == 0:
+                    fetch(c, k).wait()
                 part = plain(shards[k * parts + h][...], held[c, at, :])
                 total = part if total is None else total + part
             logistic = 1.0 / (1.0 + jnp.exp(-total))
             hidden[mine, cols] = (total * logistic).astype(BF16)
             grad = through[mine, cols] * logistic * (1.0 + total * (1.0 - logistic))
             hidden_grad[mine, cols] = grad.astype(BF16)
+        if c == 0:
+            for move in kept:
+                move.start()
     for k, out in enumerate(back):
         at = pl.ds(pl.multiple_of((place ^ k) * width, 128), width)
         total = None
@@ -634,7 +638,7 @@
         far=[weight_in],
         scratch=[
             pltpu.VMEM((steps, E * features, width), BF16),
-            pltpu.SemaphoreType.DMA((steps,)),
+            pltpu.SemaphoreType.DMA((steps, E)),
             pltpu.SemaphoreType.DMA((E * parts,)),
         ],
         flops=2 * work * E,

time: 153 us -> 155 us (1.013)
  Pallas kernels: 41.8 us -> 43.6 us
    pallas_call x15, Pallas kernels: 30.2 us -> 32 us  [local_call(): pl.pallas_call(kernel, out_shape=[jax.ShapeDtypeStruct(x[0], x[1]) for x...]
  transfers between devices with their start and end apart: 47 -> 47, of which waited for: 20 -> 20; matrix products, arithmetic and copies ran while one was open for 0% -> 0% of each run, Pallas kernels for 17% -> 16%
where the time goes in v6:
time: 155 us
  starting transfers between devices  59.8 us (39%)
  waiting for transfers between devices  49.3 us (32%)
  Pallas kernels  43.6 us (28%)
    ppermute x47, starting transfers between devices, swap(): return lax.ppermute(block, axis, [(i, i ^ distance) for i in devices])  59.8 us
    ppermute x47, waiting for transfers between devices, swap(): return lax.ppermute(block, axis, [(i, i ^ distance) for i in devices])  49.3 us
    pallas_call x15, Pallas kernels, local_call(): pl.pallas_call(kernel, out_shape=[jax.ShapeDtypeStruct(x[0], x[1]) for x...  32 us
    pallas_call x2, Pallas kernels, grid_call(): pl.pallas_call(kernel, out_shape=[jax.ShapeDtypeStruct(shape, dtype) for...  11.6 us
  transfers between devices with their start and end apart: 47, of which 20 were waited for; matrix products, arithmetic and copies ran while one was open for 0% of the time, Pallas kernels for 16%

profile of v6, /device:TPU:0, one launch (start us, length us, event | category | flops | bytes accessed | tf_op | source)
XLA Modules:
  0.0 154.9 jit_solution(642978232544249939)
XLA Ops:
  0.6 3.4 %shard_map.128 = (bf16[784,128]{1,0:T(8,128)(2,1)}, bf16[784,128]{1,0:T(8,128)(2,1)}, bf16[784,128]{1,0:T(8,128)(2,1)}, bf16[784,128]{1,0:T(8,128)(2,1)}, bf16[3...) custom-call(bf16[256,512]{1,0:T(8,128)(2,1)} %refs_0_.2, bf16[256,512]{1,0:T(8,128)(2,1)} %refs_1_.2, ...), custom_call_target="tpu_custom_call" | custom-call | bytes 1572864 | tf_op jit(solution)/shard_map/pallas_call | solution.py:56
  4.1 3.1 %collective-permute-start = (bf16[784,128]{1,0:T(8,128)(2,1)}, bf16[784,128]{1,0:T(8,128)(2,1)S(1)}, u32[]{:S(2)}, u32[]{:S(2)}) collective-permute-start(bf16[784,128]{1,0:T(8,128)(2,1)} %get-tuple-element.71), channel_id=1, source_target_pairs={{0,8},{4,12},{8,0},{12,4},{16,24},{20,28},{24,16},{28,20},{1,9},{5... | collective-permute-start | bytes 602120 | tf_op jit(solution)/shard_map/ppermute | solution.py:40
  7.2 2.6 %collective-permute-start.1 = (bf16[784,128]{1,0:T(8,128)(2,1)}, bf16[784,128]{1,0:T(8,128)(2,1)S(1)}, u32[]{:S(2)}, u32[]{:S(2)}) collective-permute-start(bf16[784,128]{1,0:T(8,128)(2,1)} %get-tuple-element.72), channel_id=1, source_target_pairs={{0,16},{4,20},{8,24},{12,28},{16,0},{20,4},{24,8},{28,12},{1,17},{... | collective-permute-start | bytes 602120 | tf_op jit(solution)/shard_map/ppermute | solution.py:40
  9.8 1.7 %collective-permute-start.5 = (bf16[320,512]{1,0:T(8,128)(2,1)}, bf16[320,512]{1,0:T(8,128)(2,1)S(1)}, u32[]{:S(2)}, u32[]{:S(2)}) collective-permute-start(bf16[320,512]{1,0:T(8,128)(2,1)} %get-tuple-element.77), channel_id=1, source_target_pairs={{0,4},{4,0},{8,12},{12,8},{16,20},{20,16},{24,28},{28,24},{1,5},{5... | collective-permute-start | bytes 983048 | tf_op jit(solution)/shard_map/ppermute | solution.py:40
  11.5 4.4 %collective-permute-done.refs_2_.refs_1_.refs_0_ = bf16[784,128]{1,0:T(8,128)(2,1)S(1)} collective-permute-done((bf16[784,128]{1,0:T(8,128)(2,1)}, bf16[784,128]{1,0:T(8,128)(2,1)S(1)}, u32[]{:S(2)}, u32[]{:S(2)}) %collective-permute-start) | collective-permute-done | bytes 200736 | tf_op jit(solution)/shard_map/ppermute | solution.py:40
  15.9 8.9 %collective-permute-done.1.refs_3_.refs_2_.refs_1_ = bf16[784,128]{1,0:T(8,128)(2,1)S(1)} collective-permute-done((bf16[784,128]{1,0:T(8,128)(2,1)}, bf16[784,128]{1,0:T(8,128)(2,1)S(1)}, u32[]{:S(2)}, u32[]{:S(2)}) %collective-permute-start.1) | collective-permute-done | bytes 200736 | tf_op jit(solution)/shard_map/ppermute | solution.py:40
  27.5 3.5 %collective-permute-start.6 = (bf16[160,512]{1,0:T(8,128)(2,1)S(1)}, bf16[160,512]{1,0:T(8,128)(2,1)S(1)}, u32[]{:S(2)}, u32[]{:S(2)}) collective-permute-start(bf16[160,512]{1,0:T(8,128)(2,1)S(1)} %get-tuple-element.79), channel_id=1, source_target_pairs={{0,8},{4,12},{8,0},{12,4},{16,24},{20,28},{24,16},{28,20},{1,9},{5... | collective-permute-start | bytes 491528 | tf_op jit(solution)/shard_map/ppermute | solution.py:40
  35.1 3.4 %collective-permute-done.3.refs_5_ = bf16[512,128]{1,0:T(8,128)(2,1)S(1)} collective-permute-done((bf16[512,128]{1,0:T(8,128)(2,1)S(1)}, bf16[512,128]{1,0:T(8,128)(2,1)S(1)}, u32[]{:S(2)}, u32[]{:S(2)}) %collective-permute-start.3) | collective-permute-done | bytes 131104 | tf_op jit(solution)/shard_map/ppermute | solution.py:40
  38.5 4.7 %shard_map.129 = (bf16[256,512]{1,0:T(8,128)(2,1)S(1)}, bf16[256,1024]{1,0:T(8,128)(2,1)S(1)}, bf16[256,1536]{1,0:T(8,128)(2,1)S(1)}, bf16[256,2048]{1,0:T(8,128...) custom-call(f32[4]{0:T(128)S(1)} %copy-done.3, ...), custom_call_target="tpu_custom_call" | custom-call | tf_op jit(solution)/shard_map/pallas_call | solution.py:56
  45.0 1.6 %collective-permute-start.9 = (bf16[640,512]{1,0:T(8,128)(2,1)S(1)}, bf16[640,512]{1,0:T(8,128)(2,1)S(1)}, u32[]{:S(2)}, u32[]{:S(2)}) collective-permute-start(bf16[640,512]{1,0:T(8,128)(2,1)S(1)} %shard_map.133.refs_1_), channel_id=1, source_target_pairs={{0,2},{1,3},{2,0},{3,1},{4,6},{5,7},{6,4},{7,5},{8,10},{9,11},{10,... | collective-permute-start | bytes 1966088 | tf_op jit(solution)/shard_map/ppermute | solution.py:40
  46.6 2.3 %collective-permute-start.10 = (bf16[640,128]{1,0:T(8,128)(2,1)S(1)}, bf16[640,128]{1,0:T(8,128)(2,1)S(1)}, u32[]{:S(2)}, u32[]{:S(2)}) collective-permute-start(bf16[640,128]{1,0:T(8,128)(2,1)S(1)} %get-tuple-element.82), channel_id=1, source_target_pairs={{0,8},{4,12},{8,0},{12,4},{16,24},{20,28},{24,16},{28,20},{1,9},{5... | collective-permute-start | bytes 491528 | tf_op jit(solution)/shard_map/ppermute | solution.py:40
  51.3 2.2 %collective-permute-done.10.refs_2_.refs_0_ = bf16[640,128]{1,0:T(8,128)(2,1)S(1)} collective-permute-done((bf16[640,128]{1,0:T(8,128)(2,1)S(1)}, bf16[640,128]{1,0:T(8,128)(2,1)S(1)}, u32[]{:S(2)}, u32[]{:S(2)}) %collective-permute-start.10) | collective-permute-done | bytes 163872 | tf_op jit(solution)/shard_map/ppermute | solution.py:40
  53.5 8.9 %collective-permute-done.11.refs_3_.refs_1_ = bf16[640,128]{1,0:T(8,128)(2,1)S(1)} collective-permute-done((bf16[640,128]{1,0:T(8,128)(2,1)S(1)}, bf16[640,128]{1,0:T(8,128)(2,1)S(1)}, u32[]{:S(2)}, u32[]{:S(2)}) %collective-permute-start.11) | collective-permute-done | bytes 163872 | tf_op jit(solution)/shard_map/ppermute | solution.py:40
  64.7 6.9 %shard_map.136 = (f32[640,1024]{1,0:T(8,128)S(1)}, bf16[640,2048]{1,0:T(8,128)(2,1)S(1)}) custom-call(bf16[1024,2048]{1,0:T(8,128)(2,1)S(1)} %bitcast.6, bf16[640,512]{1,0:T(8,128)(2,1)S(1)} %shard_map.133.refs_1_, bf16[640,512]{1,0:T(8,128)(2,1)S(1)} %collective-permute-done.13.refs_2_, bf16[640,512]{1,0:T(8,128)(2,1)S(1)} %shard_map.135.refs_3_, ...), custom_call_target="tpu_custom_call" | custom-call | flops 2684354560 | bytes 10485760 | tf_op jit(solution)/shard_map/pallas_call | solution.py:56
  73.4 2.4 %collective-permute-start.19 = (bf16[256,128]{1,0:T(8,128)(2,1)S(1)}, bf16[256,128]{1,0:T(8,128)(2,1)S(1)}, u32[]{:S(2)}, u32[]{:S(2)}) collective-permute-start(bf16[256,128]{1,0:T(8,128)(2,1)S(1)} %get-tuple-element.88), channel_id=1, source_target_pairs={{0,8},{4,12},{8,0},{12,4},{16,24},{20,28},{24,16},{28,20},{1,9},{5... | collective-permute-start | bytes 196616 | tf_op jit(solution)/shard_map/ppermute | solution.py:40
  78.9 4.5 %collective-permute-done.20.refs_1_.refs_11_ = bf16[256,128]{1,0:T(8,128)(2,1)S(1)} collective-permute-done((bf16[256,128]{1,0:T(8,128)(2,1)S(1)}, bf16[256,128]{1,0:T(8,128)(2,1)S(1)}, u32[]{:S(2)}, u32[]{:S(2)}) %collective-permute-start.20) | collective-permute-done | bytes 65568 | tf_op jit(solution)/shard_map/ppermute | solution.py:40
  85.5 9.9 %shard_map.140 = (bf16[640,2048]{1,0:T(8,128)(2,1)S(1)}, bf16[640,1024]{1,0:T(8,128)(2,1)S(1)}, bf16[640,1024]{1,0:T(8,128)(2,1)S(1)}, f32[640,512]{1,0:T(8,128)...) custom-call(bf16[2048,1024]{1,0:T(8,128)(2,1)S(1)} %bitcast.7, ...), custom_call_target="tpu_custom_call" | custom-call | flops 5368709120 | bytes 8388608 | tf_op jit(solution)/shard_map/pallas_call | solution.py:56
  96.0 1.6 %collective-permute-done.25.refs_1_ = bf16[640,512]{1,0:T(8,128)(2,1)S(1)} collective-permute-done((bf16[640,512]{1,0:T(8,128)(2,1)S(1)}, bf16[640,512]{1,0:T(8,128)(2,1)S(1)}, u32[]{:S(2)}, u32[]{:S(2)}) %collective-permute-start.25) | collective-permute-done | bytes 655392 | tf_op jit(solution)/shard_map/ppermute | solution.py:40
  99.8 5.8 %shard_map.142 = (bf16[1024,2048]{1,0:T(8,128)(2,1)}, f32[8,128]{1,0:T(8,128)S(1)}) custom-call(s32[1]{0:T(128)} %get-tuple-element.69.place, bf16[640,1024]{1,0:T(8,128)(2,1)S(1)} %get-tuple-element.94.refs_0_, bf16[640,2048]{1,0:T(8,128)(2,1)S(1)} %get-tuple-element.95.refs_1_), custom_call_target="tpu_custom_call" | custom-call | flops 2684354560 | bytes 10485760 | tf_op jit(solution)/shard_map/pallas_call | solution.py:93
  105.6 2.7 %collective-permute-done.26.refs_1_ = bf16[320,512]{1,0:T(8,128)(2,1)S(1)} collective-permute-done((bf16[320,512]{1,0:T(8,128)(2,1)S(1)}, bf16[320,512]{1,0:T(8,128)(2,1)S(1)}, u32[]{:S(2)}, u32[]{:S(2)}) %collective-permute-start.26) | collective-permute-done | bytes 327712 | tf_op jit(solution)/shard_map/ppermute | solution.py:40
  109.3 2.1 %collective-permute-start.32 = (bf16[320,128]{1,0:T(8,128)(2,1)S(1)}, bf16[320,128]{1,0:T(8,128)(2,1)S(1)}, u32[]{:S(2)}, u32[]{:S(2)}) collective-permute-start(bf16[320,128]{1,0:T(8,128)(2,1)S(1)} %get-tuple-element.107), channel_id=1, source_target_pairs={{0,16},{4,20},{8,24},{12,28},{16,0},{20,4},{24,8},{28,12},{1,17},{... | collective-permute-start | bytes 245768 | tf_op jit(solution)/shard_map/ppermute | solution.py:40
  112.9 1.6 %collective-permute-done.29.refs_1_ = bf16[320,512]{1,0:T(8,128)(2,1)S(1)} collective-permute-done((bf16[320,512]{1,0:T(8,128)(2,1)S(1)}, bf16[320,512]{1,0:T(8,128)(2,1)S(1)}, u32[]{:S(2)}, u32[]{:S(2)}) %collective-permute-start.29) | collective-permute-done | bytes 327712 | tf_op jit(solution)/shard_map/ppermute | solution.py:40
  115.4 1.6 %collective-permute-start.31 = (bf16[320,128]{1,0:T(8,128)(2,1)S(1)}, bf16[320,128]{1,0:T(8,128)(2,1)S(1)}, u32[]{:S(2)}, u32[]{:S(2)}) collective-permute-start(bf16[320,128]{1,0:T(8,128)(2,1)S(1)} %get-tuple-element.106), channel_id=1, source_target_pairs={{0,12},{4,8},{8,4},{12,0},{16,28},{20,24},{24,20},{28,16},{1,13},{... | collective-permute-start | bytes 245768 | tf_op jit(solution)/shard_map/ppermute | solution.py:40
  117.0 2.3 %collective-permute-start.33 = (bf16[320,128]{1,0:T(8,128)(2,1)S(1)}, bf16[320,128]{1,0:T(8,128)(2,1)S(1)}, u32[]{:S(2)}, u32[]{:S(2)}) collective-permute-start(bf16[320,128]{1,0:T(8,128)(2,1)S(1)} %get-tuple-element.108), channel_id=1, source_target_pairs={{0,20},{4,16},{8,28},{12,24},{16,4},{20,0},{24,12},{28,8},{1,21},{... | collective-permute-start | bytes 245768 | tf_op jit(solution)/shard_map/ppermute | solution.py:40
  119.3 2.2 %collective-permute-start.35 = (bf16[320,128]{1,0:T(8,128)(2,1)S(1)}, bf16[320,128]{1,0:T(8,128)(2,1)S(1)}, u32[]{:S(2)}, u32[]{:S(2)}) collective-permute-start(bf16[320,128]{1,0:T(8,128)(2,1)S(1)} %get-tuple-element.110), channel_id=1, source_target_pairs={{0,28},{4,24},{8,20},{12,16},{16,12},{20,8},{24,4},{28,0},{1,29},{... | collective-permute-start | bytes 245768 | tf_op jit(solution)/shard_map/ppermute | solution.py:40
  121.5 5.8 %shard_map.141 = (bf16[2048,1024]{1,0:T(8,128)(2,1)}, f32[8,128]{1,0:T(8,128)S(1)}) custom-call(s32[1]{0:T(128)} %get-tuple-element.69.place, bf16[640,2048]{1,0:T(8,128)(2,1)S(1)} %get-tuple-element.91.refs_0_, bf16[640,1024]{1,0:T(8,128)(2,1)S(1)} %get-tuple-element.92.refs_1_), custom_call_target="tpu_custom_call" | custom-call | flops 2684354560 | bytes 10485760 | tf_op jit(solution)/shard_map/pallas_call | solution.py:93
  127.4 3.8 %shard_map.146 = (bf16[256,128]{1,0:T(8,128)(2,1)S(1)}, bf16[256,128]{1,0:T(8,128)(2,1)S(1)}, bf16[256,128]{1,0:T(8,128)(2,1)S(1)}, bf16[256,128]{1,0:T(8,128)(2...) custom-call(f32[8,128]{1,0:T(8,128)S(1)} %get-tuple-element.93.refs_, ...), custom_call_target="tpu_custom_call" | custom-call | flops 2147483648 | bytes 10485760 | tf_op jit(solution)/shard_map/pallas_call | solution.py:56
  133.6 2.6 %collective-permute-start.37 = (bf16[256,128]{1,0:T(8,128)(2,1)S(1)}, bf16[256,128]{1,0:T(8,128)(2,1)S(1)}, u32[]{:S(2)}, u32[]{:S(2)}) collective-permute-start(bf16[256,128]{1,0:T(8,128)(2,1)S(1)} %get-tuple-element.122), channel_id=1, source_target_pairs={{0,16},{4,20},{8,24},{12,28},{16,0},{20,4},{24,8},{28,12},{1,17},{... | collective-permute-start | bytes 196616 | tf_op jit(solution)/shard_map/ppermute | solution.py:40
  137.6 2.8 %collective-permute-done.39 = bf16[1024,128]{1,0:T(8,128)(2,1)S(1)} collective-permute-done((bf16[1024,128]{1,0:T(8,128)(2,1)S(1)}, bf16[1024,128]{1,0:T(8,128)(2,1)S(1)}, u32[]{:S(2)}, u32[]{:S(2)}) %collective-permute-start.39) | collective-permute-done | bytes 262176 | tf_op jit(solution)/shard_map/ppermute | solution.py:40
  140.5 2.4 %collective-permute-start.42 = (bf16[256,128]{1,0:T(8,128)(2,1)S(1)}, bf16[256,128]{1,0:T(8,128)(2,1)S(1)}, u32[]{:S(2)}, u32[]{:S(2)}) collective-permute-start(bf16[256,128]{1,0:T(8,128)(2,1)S(1)} %get-tuple-element.137), channel_id=1, source_target_pairs={{0,24},{4,28},{8,16},{12,20},{16,8},{20,12},{24,0},{28,4},{1,25},{... | collective-permute-start | bytes 196616 | tf_op jit(solution)/shard_map/ppermute | solution.py:40
  143.3 1.8 %collective-permute-start.41 = (bf16[256,128]{1,0:T(8,128)(2,1)S(1)}, bf16[256,128]{1,0:T(8,128)(2,1)S(1)}, u32[]{:S(2)}, u32[]{:S(2)}) collective-permute-start(bf16[256,128]{1,0:T(8,128)(2,1)S(1)} %get-tuple-element.138), channel_id=1, source_target_pairs={{0,16},{4,20},{8,24},{12,28},{16,0},{20,4},{24,8},{28,12},{1,17},{... | collective-permute-start | bytes 196616 | tf_op jit(solution)/shard_map/ppermute | solution.py:40
  148.7 2.1 %collective-permute-start.44 = (bf16[256,128]{1,0:T(8,128)(2,1)S(1)}, bf16[256,128]{1,0:T(8,128)(2,1)S(1)}, u32[]{:S(2)}, u32[]{:S(2)}) collective-permute-start(bf16[256,128]{1,0:T(8,128)(2,1)S(1)} %get-tuple-element.135), channel_id=1, source_target_pairs={{0,8},{4,12},{8,0},{12,4},{16,24},{20,28},{24,16},{28,20},{1,9},{5... | collective-permute-start | bytes 196616 | tf_op jit(solution)/shard_map/ppermute | solution.py:40
  (101 shorter events, 38.4 us)
Async XLA Ops:
  4.1 11.8 %collective-permute-start = (bf16[784,128]{1,0:T(8,128)(2,1)}, bf16[784,128]{1,0:T(8,128)(2,1)S(1)}, u32[]{:S(2)}, u32[]{:S(2)}) collective-permute-start(bf16[784,128]{1,0:T(8,128)(2,1)} %get-tuple-element.71), channel_id=1, source_target_pairs={{0,8},{4,12},{8,0},{12,4},{16,24},{20,28},{24,16},{28,20},{1,9},{5... | collective-permute-start | bytes 602120 | tf_op jit(solution)/shard_map/ppermute | solution.py:40
  7.2 17.6 %collective-permute-start.1 = (bf16[784,128]{1,0:T(8,128)(2,1)}, bf16[784,128]{1,0:T(8,128)(2,1)S(1)}, u32[]{:S(2)}, u32[]{:S(2)}) collective-permute-start(bf16[784,128]{1,0:T(8,128)(2,1)} %get-tuple-element.72), channel_id=1, source_target_pairs={{0,16},{4,20},{8,24},{12,28},{16,0},{20,4},{24,8},{28,12},{1,17},{... | collective-permute-start | bytes 602120 | tf_op jit(solution)/shard_map/ppermute | solution.py:40
  9.8 15.1 %collective-permute-start.2 = (bf16[784,128]{1,0:T(8,128)(2,1)}, bf16[784,128]{1,0:T(8,128)(2,1)S(1)}, u32[]{:S(2)}, u32[]{:S(2)}) collective-permute-start(bf16[784,128]{1,0:T(8,128)(2,1)} %get-tuple-element.73), channel_id=1, source_target_pairs={{0,24},{4,28},{8,16},{12,20},{16,8},{20,12},{24,0},{28,4},{1,25},{... | collective-permute-start | bytes 602120 | tf_op jit(solution)/shard_map/ppermute | solution.py:40
  9.8 16.7 %collective-permute-start.5 = (bf16[320,512]{1,0:T(8,128)(2,1)}, bf16[320,512]{1,0:T(8,128)(2,1)S(1)}, u32[]{:S(2)}, u32[]{:S(2)}) collective-permute-start(bf16[320,512]{1,0:T(8,128)(2,1)} %get-tuple-element.77), channel_id=1, source_target_pairs={{0,4},{4,0},{8,12},{12,8},{16,20},{20,16},{24,28},{28,24},{1,5},{5... | collective-permute-start | bytes 983048 | tf_op jit(solution)/shard_map/ppermute | solution.py:40
  24.9 13.6 %collective-permute-start.4 = (bf16[1536,128]{1,0:T(8,128)(2,1)S(1)}, bf16[1536,128]{1,0:T(8,128)(2,1)S(1)}, u32[]{:S(2)}, u32[]{:S(2)}) collective-permute-start(bf16[1536,128]{1,0:T(8,128)(2,1)S(1)} %pad_maximum_fusion), channel_id=1, source_target_pairs={{0,4},{4,0},{8,12},{12,8},{16,20},{20,16},{24,28},{28,24},{1,5},{5... | collective-permute-start | bytes 1179656 | tf_op jit(solution)/shard_map/ppermute | solution.py:40
  27.5 16.2 %collective-permute-start.6 = (bf16[160,512]{1,0:T(8,128)(2,1)S(1)}, bf16[160,512]{1,0:T(8,128)(2,1)S(1)}, u32[]{:S(2)}, u32[]{:S(2)}) collective-permute-start(bf16[160,512]{1,0:T(8,128)(2,1)S(1)} %get-tuple-element.79), channel_id=1, source_target_pairs={{0,8},{4,12},{8,0},{12,4},{16,24},{20,28},{24,16},{28,20},{1,9},{5... | collective-permute-start | bytes 491528 | tf_op jit(solution)/shard_map/ppermute | solution.py:40
  30.9 14.0 %collective-permute-start.7 = (bf16[160,512]{1,0:T(8,128)(2,1)S(1)}, bf16[160,512]{1,0:T(8,128)(2,1)S(1)}, u32[]{:S(2)}, u32[]{:S(2)}) collective-permute-start(bf16[160,512]{1,0:T(8,128)(2,1)S(1)} %get-tuple-element.80), channel_id=1, source_target_pairs={{0,16},{4,20},{8,24},{12,28},{16,0},{20,4},{24,8},{28,12},{1,17},{... | collective-permute-start | bytes 491528 | tf_op jit(solution)/shard_map/ppermute | solution.py:40
  32.0 12.9 %collective-permute-start.8 = (bf16[160,512]{1,0:T(8,128)(2,1)S(1)}, bf16[160,512]{1,0:T(8,128)(2,1)S(1)}, u32[]{:S(2)}, u32[]{:S(2)}) collective-permute-start(bf16[160,512]{1,0:T(8,128)(2,1)S(1)} %get-tuple-element.81), channel_id=1, source_target_pairs={{0,24},{4,28},{8,16},{12,20},{16,8},{20,12},{24,0},{28,4},{1,25},{... | collective-permute-start | bytes 491528 | tf_op jit(solution)/shard_map/ppermute | solution.py:40
  45.0 17.5 %collective-permute-start.9 = (bf16[640,512]{1,0:T(8,128)(2,1)S(1)}, bf16[640,512]{1,0:T(8,128)(2,1)S(1)}, u32[]{:S(2)}, u32[]{:S(2)}) collective-permute-start(bf16[640,512]{1,0:T(8,128)(2,1)S(1)} %shard_map.133.refs_1_), channel_id=1, source_target_pairs={{0,2},{1,3},{2,0},{3,1},{4,6},{5,7},{6,4},{7,5},{8,10},{9,11},{10,... | collective-permute-start | bytes 1966088 | tf_op jit(solution)/shard_map/ppermute | solution.py:40
  48.9 13.5 %collective-permute-start.11 = (bf16[640,128]{1,0:T(8,128)(2,1)S(1)}, bf16[640,128]{1,0:T(8,128)(2,1)S(1)}, u32[]{:S(2)}, u32[]{:S(2)}) collective-permute-start(bf16[640,128]{1,0:T(8,128)(2,1)S(1)} %get-tuple-element.83), channel_id=1, source_target_pairs={{0,16},{4,20},{8,24},{12,28},{16,0},{20,4},{24,8},{28,12},{1,17},{... | collective-permute-start | bytes 491528 | tf_op jit(solution)/shard_map/ppermute | solution.py:40
  49.8 12.6 %collective-permute-start.12 = (bf16[640,128]{1,0:T(8,128)(2,1)S(1)}, bf16[640,128]{1,0:T(8,128)(2,1)S(1)}, u32[]{:S(2)}, u32[]{:S(2)}) collective-permute-start(bf16[640,128]{1,0:T(8,128)(2,1)S(1)} %get-tuple-element.84), channel_id=1, source_target_pairs={{0,24},{4,28},{8,16},{12,20},{16,8},{20,12},{24,0},{28,4},{1,25},{... | collective-permute-start | bytes 491528 | tf_op jit(solution)/shard_map/ppermute | solution.py:40
  51.3 12.4 %collective-permute-start.13 = (bf16[640,512]{1,0:T(8,128)(2,1)S(1)}, bf16[640,512]{1,0:T(8,128)(2,1)S(1)}, u32[]{:S(2)}, u32[]{:S(2)}) collective-permute-start(bf16[640,512]{1,0:T(8,128)(2,1)S(1)} %shard_map.133.refs_1_), channel_id=1, source_target_pairs={{0,1},{1,0},{2,3},{3,2},{4,5},{5,4},{6,7},{7,6},{8,9},{9,8},{10,11... | collective-permute-start | bytes 1966088 | tf_op jit(solution)/shard_map/ppermute | solution.py:40
  62.6 10.1 %collective-permute-start.15 = (bf16[320,512]{1,0:T(8,128)(2,1)S(1)}, bf16[320,512]{1,0:T(8,128)(2,1)S(1)}, u32[]{:S(2)}, u32[]{:S(2)}) collective-permute-start(bf16[320,512]{1,0:T(8,128)(2,1)S(1)} %get-tuple-element.87), channel_id=1, source_target_pairs={{0,4},{4,0},{8,12},{12,8},{16,20},{20,16},{24,28},{28,24},{1,5},{5... | collective-permute-start | bytes 983048 | tf_op jit(solution)/shard_map/ppermute | solution.py:40
  63.2 15.2 %collective-permute-start.18 = (bf16[320,512]{1,0:T(8,128)(2,1)S(1)}, bf16[320,512]{1,0:T(8,128)(2,1)S(1)}, u32[]{:S(2)}, u32[]{:S(2)}) collective-permute-start(bf16[320,512]{1,0:T(8,128)(2,1)S(1)} %get-tuple-element.85.refs_1_), channel_id=1, source_target_pairs={{0,2},{1,3},{2,0},{3,1},{4,6},{5,7},{6,4},{7,5},{8,10},{9,11},{10,... | collective-permute-start | bytes 983048 | tf_op jit(solution)/shard_map/ppermute | solution.py:40
  72.8 10.6 %collective-permute-start.22 = (bf16[320,512]{1,0:T(8,128)(2,1)S(1)}, bf16[320,512]{1,0:T(8,128)(2,1)S(1)}, u32[]{:S(2)}, u32[]{:S(2)}) collective-permute-start(bf16[320,512]{1,0:T(8,128)(2,1)S(1)} %shard_map.137.refs_0_.refs_2_), channel_id=1, source_target_pairs={{0,2},{1,3},{2,0},{3,1},{4,6},{5,7},{6,4},{7,5},{8,10},{9,11},{10,... | collective-permute-start | bytes 983048 | tf_op jit(solution)/shard_map/ppermute | solution.py:40
  75.7 7.7 %collective-permute-start.20 = (bf16[256,128]{1,0:T(8,128)(2,1)S(1)}, bf16[256,128]{1,0:T(8,128)(2,1)S(1)}, u32[]{:S(2)}, u32[]{:S(2)}) collective-permute-start(bf16[256,128]{1,0:T(8,128)(2,1)S(1)} %get-tuple-element.89), channel_id=1, source_target_pairs={{0,16},{4,20},{8,24},{12,28},{16,0},{20,4},{24,8},{28,12},{1,17},{... | collective-permute-start | bytes 196616 | tf_op jit(solution)/shard_map/ppermute | solution.py:40
  95.6 10.0 %collective-permute-start.27 = (bf16[640,512]{1,0:T(8,128)(2,1)S(1)}, bf16[640,512]{1,0:T(8,128)(2,1)S(1)}, u32[]{:S(2)}, u32[]{:S(2)}) collective-permute-start(bf16[640,512]{1,0:T(8,128)(2,1)S(1)} %get-tuple-element.101), channel_id=1, source_target_pairs={{0,1},{1,0},{2,3},{3,2},{4,5},{5,4},{6,7},{7,6},{8,9},{9,8},{10,11... | collective-permute-start | bytes 1966088 | tf_op jit(solution)/shard_map/ppermute | solution.py:40
  97.7 10.6 %collective-permute-start.26 = (bf16[320,512]{1,0:T(8,128)(2,1)S(1)}, bf16[320,512]{1,0:T(8,128)(2,1)S(1)}, u32[]{:S(2)}, u32[]{:S(2)}) collective-permute-start(bf16[320,512]{1,0:T(8,128)(2,1)S(1)} %get-tuple-element.99), channel_id=1, source_target_pairs={{0,2},{1,3},{2,0},{3,1},{4,6},{5,7},{6,4},{7,5},{8,10},{9,11},{10,... | collective-permute-start | bytes 983048 | tf_op jit(solution)/shard_map/ppermute | solution.py:40
  99.2 15.3 %collective-permute-start.29 = (bf16[320,512]{1,0:T(8,128)(2,1)S(1)}, bf16[320,512]{1,0:T(8,128)(2,1)S(1)}, u32[]{:S(2)}, u32[]{:S(2)}) collective-permute-start(bf16[320,512]{1,0:T(8,128)(2,1)S(1)} %get-tuple-element.104), channel_id=1, source_target_pairs={{0,2},{1,3},{2,0},{3,1},{4,6},{5,7},{6,4},{7,5},{8,10},{9,11},{10,... | collective-permute-start | bytes 983048 | tf_op jit(solution)/shard_map/ppermute | solution.py:40
  109.3 10.0 %collective-permute-start.32 = (bf16[320,128]{1,0:T(8,128)(2,1)S(1)}, bf16[320,128]{1,0:T(8,128)(2,1)S(1)}, u32[]{:S(2)}, u32[]{:S(2)}) collective-permute-start(bf16[320,128]{1,0:T(8,128)(2,1)S(1)} %get-tuple-element.107), channel_id=1, source_target_pairs={{0,16},{4,20},{8,24},{12,28},{16,0},{20,4},{24,8},{28,12},{1,17},{... | collective-permute-start | bytes 245768 | tf_op jit(solution)/shard_map/ppermute | solution.py:40
  111.5 15.9 %collective-permute-start.34 = (bf16[320,128]{1,0:T(8,128)(2,1)S(1)}, bf16[320,128]{1,0:T(8,128)(2,1)S(1)}, u32[]{:S(2)}, u32[]{:S(2)}) collective-permute-start(bf16[320,128]{1,0:T(8,128)(2,1)S(1)} %get-tuple-element.109), channel_id=1, source_target_pairs={{0,24},{4,28},{8,16},{12,20},{16,8},{20,12},{24,0},{28,4},{1,25},{... | collective-permute-start | bytes 245768 | tf_op jit(solution)/shard_map/ppermute | solution.py:40
  114.7 12.7 %collective-permute-start.30 = (bf16[320,128]{1,0:T(8,128)(2,1)S(1)}, bf16[320,128]{1,0:T(8,128)(2,1)S(1)}, u32[]{:S(2)}, u32[]{:S(2)}) collective-permute-start(bf16[320,128]{1,0:T(8,128)(2,1)S(1)} %get-tuple-element.105), channel_id=1, source_target_pairs={{0,4},{4,0},{8,12},{12,8},{16,20},{20,16},{24,28},{28,24},{1,5},{5... | collective-permute-start | bytes 245768 | tf_op jit(solution)/shard_map/ppermute | solution.py:40
  115.4 11.9 %collective-permute-start.31 = (bf16[320,128]{1,0:T(8,128)(2,1)S(1)}, bf16[320,128]{1,0:T(8,128)(2,1)S(1)}, u32[]{:S(2)}, u32[]{:S(2)}) collective-permute-start(bf16[320,128]{1,0:T(8,128)(2,1)S(1)} %get-tuple-element.106), channel_id=1, source_target_pairs={{0,12},{4,8},{8,4},{12,0},{16,28},{20,24},{24,20},{28,16},{1,13},{... | collective-permute-start | bytes 245768 | tf_op jit(solution)/shard_map/ppermute | solution.py:40
  117.0 10.3 %collective-permute-start.33 = (bf16[320,128]{1,0:T(8,128)(2,1)S(1)}, bf16[320,128]{1,0:T(8,128)(2,1)S(1)}, u32[]{:S(2)}, u32[]{:S(2)}) collective-permute-start(bf16[320,128]{1,0:T(8,128)(2,1)S(1)} %get-tuple-element.108), channel_id=1, source_target_pairs={{0,20},{4,16},{8,28},{12,24},{16,4},{20,0},{24,12},{28,8},{1,21},{... | collective-permute-start | bytes 245768 | tf_op jit(solution)/shard_map/ppermute | solution.py:40
  119.3 8.0 %collective-permute-start.35 = (bf16[320,128]{1,0:T(8,128)(2,1)S(1)}, bf16[320,128]{1,0:T(8,128)(2,1)S(1)}, u32[]{:S(2)}, u32[]{:S(2)}) collective-permute-start(bf16[320,128]{1,0:T(8,128)(2,1)S(1)} %get-tuple-element.110), channel_id=1, source_target_pairs={{0,28},{4,24},{8,20},{12,16},{16,12},{20,8},{24,4},{28,0},{1,29},{... | collective-permute-start | bytes 245768 | tf_op jit(solution)/shard_map/ppermute | solution.py:40
  131.2 9.3 %collective-permute-start.39 = (bf16[1024,128]{1,0:T(8,128)(2,1)S(1)}, bf16[1024,128]{1,0:T(8,128)(2,1)S(1)}, u32[]{:S(2)}, u32[]{:S(2)}) collective-permute-start(bf16[1024,128]{1,0:T(8,128)(2,1)S(1)} %get-tuple-element.125), channel_id=1, source_target_pairs={{0,4},{4,0},{8,12},{12,8},{16,20},{20,16},{24,28},{28,24},{1,5},{5... | collective-permute-start | bytes 786440 | tf_op jit(solution)/shard_map/ppermute | solution.py:40
  131.9 11.3 %collective-permute-start.43 = (bf16[1024,128]{1,0:T(8,128)(2,1)S(1)}, bf16[1024,128]{1,0:T(8,128)(2,1)S(1)}, u32[]{:S(2)}, u32[]{:S(2)}) collective-permute-start(bf16[1024,128]{1,0:T(8,128)(2,1)S(1)} %get-tuple-element.127), channel_id=1, source_target_pairs={{0,4},{4,0},{8,12},{12,8},{16,20},{20,16},{24,28},{28,24},{1,5},{5... | collective-permute-start | bytes 786440 | tf_op jit(solution)/shard_map/ppermute | solution.py:40
  133.3 11.8 %collective-permute-start.36 = (bf16[256,128]{1,0:T(8,128)(2,1)S(1)}, bf16[256,128]{1,0:T(8,128)(2,1)S(1)}, u32[]{:S(2)}, u32[]{:S(2)}) collective-permute-start(bf16[256,128]{1,0:T(8,128)(2,1)S(1)} %get-tuple-element.121), channel_id=1, source_target_pairs={{0,8},{4,12},{8,0},{12,4},{16,24},{20,28},{24,16},{28,20},{1,9},{5... | collective-permute-start | bytes 196616 | tf_op jit(solution)/shard_map/ppermute | solution.py:40
  133.6 12.7 %collective-permute-start.37 = (bf16[256,128]{1,0:T(8,128)(2,1)S(1)}, bf16[256,128]{1,0:T(8,128)(2,1)S(1)}, u32[]{:S(2)}, u32[]{:S(2)}) collective-permute-start(bf16[256,128]{1,0:T(8,128)(2,1)S(1)} %get-tuple-element.122), channel_id=1, source_target_pairs={{0,16},{4,20},{8,24},{12,28},{16,0},{20,4},{24,8},{28,12},{1,17},{... | collective-permute-start | bytes 196616 | tf_op jit(solution)/shard_map/ppermute | solution.py:40
  136.2 11.6 %collective-permute-start.38 = (bf16[256,128]{1,0:T(8,128)(2,1)S(1)}, bf16[256,128]{1,0:T(8,128)(2,1)S(1)}, u32[]{:S(2)}, u32[]{:S(2)}) collective-permute-start(bf16[256,128]{1,0:T(8,128)(2,1)S(1)} %get-tuple-element.123), channel_id=1, source_target_pairs={{0,24},{4,28},{8,16},{12,20},{16,8},{20,12},{24,0},{28,4},{1,25},{... | collective-permute-start | bytes 196616 | tf_op jit(solution)/shard_map/ppermute | solution.py:40
  140.5 8.1 %collective-permute-start.42 = (bf16[256,128]{1,0:T(8,128)(2,1)S(1)}, bf16[256,128]{1,0:T(8,128)(2,1)S(1)}, u32[]{:S(2)}, u32[]{:S(2)}) collective-permute-start(bf16[256,128]{1,0:T(8,128)(2,1)S(1)} %get-tuple-element.137), channel_id=1, source_target_pairs={{0,24},{4,28},{8,16},{12,20},{16,8},{20,12},{24,0},{28,4},{1,25},{... | collective-permute-start | bytes 196616 | tf_op jit(solution)/shard_map/ppermute | solution.py:40
  143.3 7.6 %collective-permute-start.41 = (bf16[256,128]{1,0:T(8,128)(2,1)S(1)}, bf16[256,128]{1,0:T(8,128)(2,1)S(1)}, u32[]{:S(2)}, u32[]{:S(2)}) collective-permute-start(bf16[256,128]{1,0:T(8,128)(2,1)S(1)} %get-tuple-element.138), channel_id=1, source_target_pairs={{0,16},{4,20},{8,24},{12,28},{16,0},{20,4},{24,8},{28,12},{1,17},{... | collective-permute-start | bytes 196616 | tf_op jit(solution)/shard_map/ppermute | solution.py:40
  (21 other events, 173.2 us)
